TPU v7x, 512 devices: a whole 4x4x16 slice. The times are simulated.
512 devices in a mesh: gx: 16 (over x, y), gy: 4 (over z_lo), gz: 8 (over z_hi, core).
Axes of the slice: x: 4, y: 4, z: 16 (z_hi: 4, z_lo: 4; z = z_hi * 4 + z_lo), core: 2. Of those that a mesh axis runs over, the one named last changes fastest.
Arguments:
- conc: float32 [1, 128, 256, 1024], P(None, 'gz', 'gx', 'gy'), may hold values from 0.1 to 10
- wind_x: float32 [128, 256, 1024], P('gz', 'gx', 'gy'), may hold values from -0.35 to 0.35
- wind_y: float32 [128, 256, 1024], P('gz', 'gx', 'gy'), may hold values from -0.35 to 0.35
- profiles: float32 [8, 128], replicated, may hold values from 1 to 500
- classes: int32 [256, 1024], P('gx', 'gy'), may hold values from 0 to 7
- heights: int32 [256, 1024], P('gx', 'gy'), may hold values from 0 to 32
- emission: float32 [1, 256, 1024], P(None, 'gx', 'gy'), may hold values from 0.5 to 5
Outputs:
- conc_out: float32 [1, 128, 256, 1024], P(None, 'gz', 'gx', 'gy')
All inputs are finite; a program needn't handle non-finite values.
Results may differ from a plain program's by a relative error of at most 0.0003.
Values sent between devices are 32-bit elements; how exact they have to be, the bound alone decides.
No kernel may reach another device: no remote copies, remote signals or barrier semaphores. Data moves between devices by JAX's collectives and lax.ppermute only.
A program may use at most 64 MiB of HBM per device.

v0:
```python
import jax
import jax.numpy as jnp
from jax import lax
from jax.sharding import PartitionSpec as P

HSTEPS = 8


diffusion_number = 0.05
canopy_scale = 0.2


def shifted(x, axis, by):
    length = lax.axis_size(axis)
    pairs = [(i, i + by) for i in range(length) if 0 <= i + by < length]
    return lax.ppermute(x, axis, pairs)


def padded_2(block, sides, width):
    for axis, dim in sides:
        count = lax.axis_size(axis)
        forward = [(i, i + 1) for i in range(count - 1)]
        backward = [(target, source) for source, target in forward]
        low = lax.ppermute(
            lax.slice_in_dim(block, block.shape[dim] - width, None, axis=dim), axis, forward
        )
        high = lax.ppermute(lax.slice_in_dim(block, 0, width, axis=dim), axis, backward)
        block = jnp.concatenate([low, block, high], axis=dim)
    return block


def update(padded, centre, wind_x, wind_y, west_x, south_y):
    east = padded[:, :, 2:, 1:-1]
    west = padded[:, :, :-2, 1:-1]
    north = padded[:, :, 1:-1, 2:]
    south = padded[:, :, 1:-1, :-2]
    flux_east = jnp.maximum(wind_x, 0.0) * centre + jnp.minimum(wind_x, 0.0) * east
    flux_west = jnp.maximum(west_x, 0.0) * west + jnp.minimum(west_x, 0.0) * centre
    flux_north = jnp.maximum(wind_y, 0.0) * centre + jnp.minimum(wind_y, 0.0) * north
    flux_south = jnp.maximum(south_y, 0.0) * south + jnp.minimum(south_y, 0.0) * centre
    spread = east + west + north + south - 4.0 * centre
    return centre - (flux_east - flux_west) - (flux_north - flux_south) + diffusion_number * spread


def class_table(table, classes):
    count = table.shape[0]
    onehot = (classes[None] == jnp.arange(count, dtype=jnp.int32)[:, None, None]).astype(
        jnp.float32
    )
    return jnp.einsum("cz,cxy->zxy", table, onehot, precision=lax.Precision.HIGHEST)


def local(conc, wind_x, wind_y, profiles, classes, heights, emission):
    species, depth, rows, width = conc.shape
    edge_x = shifted(wind_x[:, -1:, :], "gx", 1)
    west_x = jnp.concatenate([edge_x, wind_x[:, :-1, :]], axis=1)
    edge_y = shifted(wind_y[:, :, -1:], "gy", 1)
    south_y = jnp.concatenate([edge_y, wind_y[:, :, :-1]], axis=2)
    for step in range(HSTEPS):
        padded = padded_2(conc, (("gx", 2), ("gy", 3)), 1)
        conc = update(padded, conc, wind_x, wind_y, west_x, south_y)
    groups = lax.axis_size("gz")
    layer = lax.axis_index("gz")
    total = depth * groups
    share = rows // groups
    columns = lax.all_to_all(conc, "gz", split_axis=2, concat_axis=1, tiled=True)
    offset = layer * share
    my_classes = lax.dynamic_slice_in_dim(classes, offset, share, 0)
    my_heights = lax.dynamic_slice_in_dim(heights, offset, share, 0)
    my_emission = lax.dynamic_slice_in_dim(emission, offset, share, 1)
    above = class_table(profiles, my_classes)
    levels = jnp.arange(total, dtype=jnp.int32)[:, None, None]
    above = jnp.where(levels < my_heights[None], canopy_scale * above, above)
    above = jnp.transpose(above, (1, 2, 0))
    zero_plane = jnp.zeros_like(above[:, :, :1])
    below = jnp.concatenate([zero_plane, above[:, :, :-1]], axis=2)
    upper = -jnp.concatenate([above[:, :, :-1], zero_plane], axis=2)
    rhs = jnp.transpose(columns, (2, 3, 1, 0))
    rhs = rhs.at[:, :, 0, :].add(jnp.transpose(my_emission, (1, 2, 0)))
    solved = lax.linalg.tridiagonal_solve(-below, 1.0 + below + above, upper, rhs)
    result = lax.all_to_all(
        jnp.transpose(solved, (3, 2, 0, 1)), "gz", split_axis=1, concat_axis=2, tiled=True
    )
    return result


def solution(mesh):
    return jax.shard_map(
        local,
        mesh=mesh,
        in_specs=(
            P(None, "gz", "gx", "gy"),
            P("gz", "gx", "gy"),
            P("gz", "gx", "gy"),
            P(),
            P("gx", "gy"),
            P("gx", "gy"),
            P(None, "gx", "gy"),
        ),
        out_specs=P(None, "gz", "gx", "gy"),
        check_vma=False,
    )
```

profile of v0, /device:TPU:4, one launch (start us, length us, event | category | flops | bytes accessed | tf_op | source)
XLA Modules:
  0.0 254.0 jit_solution(16860839394332790579)
XLA Ops:
  1.2 3.6 %collective-permute-start.2 = (f32[1,16,1,256]{3,1,0,2:T(8,128)S(1)}, f32[1,16,1,256]{3,1,0,2:T(8,128)S(1)}, u32[]{:S(2)}, u32[]{:S(2)}) collective-permute-start(f32[1,16,1,256]{3,1,0,2:T(8,128)S(1)} %get-tuple-element.1142), channel_id=1, source_target_pairs={{0,32},{32,64},{64,96},{96,128},{128,160},{160,192},{192,224},{224... | collective-permute-start | bytes 49160 | tf_op jit(solution)/shard_map/ppermute | solution.py:24
  4.8 4.5 %collective-permute-start = (f32[1,16,1,256]{3,1,0,2:T(8,128)S(1)}, f32[1,16,1,256]{3,1,0,2:T(8,128)S(1)}, u32[]{:S(2)}, u32[]{:S(2)}) collective-permute-start(f32[1,16,1,256]{3,1,0,2:T(8,128)S(1)} %get-tuple-element.1141), channel_id=1, source_target_pairs={{32,0},{64,32},{96,64},{128,96},{160,128},{192,160},{224,192},{256... | collective-permute-start | bytes 49160 | tf_op jit(solution)/shard_map/ppermute | solution.py:27
  9.3 1.9 collective-permute-start.1
  11.5 3.8 %collective-permute-start.4 = (f32[16,16,1]{1,0,2:T(8,128)S(1)}, f32[16,16,1]{1,0,2:T(8,128)S(1)}, u32[]{:S(2)}, u32[]{:S(2)}) collective-permute-start(f32[16,16,1]{1,0,2:T(8,128)S(1)} %copy.2908), channel_id=1, source_target_pairs={{0,8},{8,16},{16,24},{1,9},{9,17},{17,25},{2,10},{10,18},{18,26},{... | collective-permute-start | bytes 3080 | tf_op jit(solution)/shard_map/ppermute | solution.py:16
  17.0 4.6 %collective-permute-start.5 = (f32[1,16,18,1]{3,1,0,2:T(8,128)S(1)}, f32[1,16,18,1]{3,1,0,2:T(8,128)S(1)}, u32[]{:S(2)}, u32[]{:S(2)}) collective-permute-start(f32[1,16,18,1]{3,1,0,2:T(8,128)S(1)} %get-tuple-element.1119), channel_id=1, source_target_pairs={{0,8},{8,16},{16,24},{1,9},{9,17},{17,25},{2,10},{10,18},{18,26},{... | collective-permute-start | bytes 3464 | tf_op jit(solution)/shard_map/ppermute | solution.py:24
  25.1 6.0 %collective-permute-start.6 = (f32[1,16,1,256]{3,1,0,2:T(8,128)S(1)}, f32[1,16,1,256]{3,1,0,2:T(8,128)S(1)}, u32[]{:S(2)}, u32[]{:S(2)}) collective-permute-start(f32[1,16,1,256]{3,1,0,2:T(8,128)S(1)} %get-tuple-element.1136), channel_id=1, source_target_pairs={{32,0},{64,32},{96,64},{128,96},{160,128},{192,160},{224,192},{256... | collective-permute-start | bytes 49160 | tf_op jit(solution)/shard_map/ppermute | solution.py:27
  31.2 1.9 collective-permute-start.7
  33.1 5.8 %collective-permute-done.7 = f32[1,16,1,256]{3,1,0,2:T(8,128)S(1)} collective-permute-done((f32[1,16,1,256]{3,1,0,2:T(8,128)S(1)}, f32[1,16,1,256]{3,1,0,2:T(8,128)S(1)}, u32[]{:S(2)}, u32[]{:S(2)}) %collective-permute-start.7) | collective-permute-done | bytes 16416 | tf_op jit(solution)/shard_map/ppermute | solution.py:24
  40.3 5.0 %collective-permute-start.9 = (f32[1,16,18,1]{3,1,0,2:T(8,128)S(1)}, f32[1,16,18,1]{3,1,0,2:T(8,128)S(1)}, u32[]{:S(2)}, u32[]{:S(2)}) collective-permute-start(f32[1,16,18,1]{3,1,0,2:T(8,128)S(1)} %get-tuple-element.1117), channel_id=1, source_target_pairs={{0,8},{8,16},{16,24},{1,9},{9,17},{17,25},{2,10},{10,18},{18,26},{... | collective-permute-start | bytes 3464 | tf_op jit(solution)/shard_map/ppermute | solution.py:24
  48.9 1.9 collective-permute-start.10
  50.8 3.9 %collective-permute-start.11 = (f32[1,16,1,256]{3,1,0,2:T(8,128)S(1)}, f32[1,16,1,256]{3,1,0,2:T(8,128)S(1)}, u32[]{:S(2)}, u32[]{:S(2)}) collective-permute-start(f32[1,16,1,256]{3,1,0,2:T(8,128)S(1)} %get-tuple-element.1133), channel_id=1, source_target_pairs={{0,32},{32,64},{64,96},{96,128},{128,160},{160,192},{192,224},{224... | collective-permute-start | bytes 49160 | tf_op jit(solution)/shard_map/ppermute | solution.py:24
  54.8 3.8 %collective-permute-done.11 = f32[1,16,1,256]{3,1,0,2:T(8,128)S(1)} collective-permute-done((f32[1,16,1,256]{3,1,0,2:T(8,128)S(1)}, f32[1,16,1,256]{3,1,0,2:T(8,128)S(1)}, u32[]{:S(2)}, u32[]{:S(2)}) %collective-permute-start.11) | collective-permute-done | bytes 16416 | tf_op jit(solution)/shard_map/ppermute | solution.py:24
  60.0 5.0 %collective-permute-start.13 = (f32[1,16,18,1]{3,1,0,2:T(8,128)S(1)}, f32[1,16,18,1]{3,1,0,2:T(8,128)S(1)}, u32[]{:S(2)}, u32[]{:S(2)}) collective-permute-start(f32[1,16,18,1]{3,1,0,2:T(8,128)S(1)} %get-tuple-element.1115), channel_id=1, source_target_pairs={{0,8},{8,16},{16,24},{1,9},{9,17},{17,25},{2,10},{10,18},{18,26},{... | collective-permute-start | bytes 3464 | tf_op jit(solution)/shard_map/ppermute | solution.py:24
  68.6 1.9 collective-permute-start.14
  70.5 3.9 %collective-permute-start.15 = (f32[1,16,1,256]{3,1,0,2:T(8,128)S(1)}, f32[1,16,1,256]{3,1,0,2:T(8,128)S(1)}, u32[]{:S(2)}, u32[]{:S(2)}) collective-permute-start(f32[1,16,1,256]{3,1,0,2:T(8,128)S(1)} %get-tuple-element.1131), channel_id=1, source_target_pairs={{0,32},{32,64},{64,96},{96,128},{128,160},{160,192},{192,224},{224... | collective-permute-start | bytes 49160 | tf_op jit(solution)/shard_map/ppermute | solution.py:24
  74.4 3.8 %collective-permute-done.15 = f32[1,16,1,256]{3,1,0,2:T(8,128)S(1)} collective-permute-done((f32[1,16,1,256]{3,1,0,2:T(8,128)S(1)}, f32[1,16,1,256]{3,1,0,2:T(8,128)S(1)}, u32[]{:S(2)}, u32[]{:S(2)}) %collective-permute-start.15) | collective-permute-done | bytes 16416 | tf_op jit(solution)/shard_map/ppermute | solution.py:24
  79.7 5.0 %collective-permute-start.17 = (f32[1,16,18,1]{3,1,0,2:T(8,128)S(1)}, f32[1,16,18,1]{3,1,0,2:T(8,128)S(1)}, u32[]{:S(2)}, u32[]{:S(2)}) collective-permute-start(f32[1,16,18,1]{3,1,0,2:T(8,128)S(1)} %get-tuple-element.1113), channel_id=1, source_target_pairs={{0,8},{8,16},{16,24},{1,9},{9,17},{17,25},{2,10},{10,18},{18,26},{... | collective-permute-start | bytes 3464 | tf_op jit(solution)/shard_map/ppermute | solution.py:24
  85.9 1.5 collective-permute-done.17
  88.2 1.9 collective-permute-start.18
  90.2 3.9 %collective-permute-start.19 = (f32[1,16,1,256]{3,1,0,2:T(8,128)S(1)}, f32[1,16,1,256]{3,1,0,2:T(8,128)S(1)}, u32[]{:S(2)}, u32[]{:S(2)}) collective-permute-start(f32[1,16,1,256]{3,1,0,2:T(8,128)S(1)} %get-tuple-element.1129), channel_id=1, source_target_pairs={{0,32},{32,64},{64,96},{96,128},{128,160},{160,192},{192,224},{224... | collective-permute-start | bytes 49160 | tf_op jit(solution)/shard_map/ppermute | solution.py:24
  94.1 3.8 %collective-permute-done.19 = f32[1,16,1,256]{3,1,0,2:T(8,128)S(1)} collective-permute-done((f32[1,16,1,256]{3,1,0,2:T(8,128)S(1)}, f32[1,16,1,256]{3,1,0,2:T(8,128)S(1)}, u32[]{:S(2)}, u32[]{:S(2)}) %collective-permute-start.19) | collective-permute-done | bytes 16416 | tf_op jit(solution)/shard_map/ppermute | solution.py:24
  99.3 5.0 %collective-permute-start.21 = (f32[1,16,18,1]{3,1,0,2:T(8,128)S(1)}, f32[1,16,18,1]{3,1,0,2:T(8,128)S(1)}, u32[]{:S(2)}, u32[]{:S(2)}) collective-permute-start(f32[1,16,18,1]{3,1,0,2:T(8,128)S(1)} %get-tuple-element.1111), channel_id=1, source_target_pairs={{0,8},{8,16},{16,24},{1,9},{9,17},{17,25},{2,10},{10,18},{18,26},{... | collective-permute-start | bytes 3464 | tf_op jit(solution)/shard_map/ppermute | solution.py:24
  105.5 1.5 collective-permute-done.21
  107.9 1.9 collective-permute-start.22
  109.8 3.9 %collective-permute-start.23 = (f32[1,16,1,256]{3,1,0,2:T(8,128)S(1)}, f32[1,16,1,256]{3,1,0,2:T(8,128)S(1)}, u32[]{:S(2)}, u32[]{:S(2)}) collective-permute-start(f32[1,16,1,256]{3,1,0,2:T(8,128)S(1)} %get-tuple-element.1127), channel_id=1, source_target_pairs={{0,32},{32,64},{64,96},{96,128},{128,160},{160,192},{192,224},{224... | collective-permute-start | bytes 49160 | tf_op jit(solution)/shard_map/ppermute | solution.py:24
  114.2 3.4 %collective-permute-done.23 = f32[1,16,1,256]{3,1,0,2:T(8,128)S(1)} collective-permute-done((f32[1,16,1,256]{3,1,0,2:T(8,128)S(1)}, f32[1,16,1,256]{3,1,0,2:T(8,128)S(1)}, u32[]{:S(2)}, u32[]{:S(2)}) %collective-permute-start.23) | collective-permute-done | bytes 16416 | tf_op jit(solution)/shard_map/ppermute | solution.py:24
  119.0 5.0 %collective-permute-start.25 = (f32[1,16,18,1]{3,1,0,2:T(8,128)S(1)}, f32[1,16,18,1]{3,1,0,2:T(8,128)S(1)}, u32[]{:S(2)}, u32[]{:S(2)}) collective-permute-start(f32[1,16,18,1]{3,1,0,2:T(8,128)S(1)} %get-tuple-element.1109), channel_id=1, source_target_pairs={{0,8},{8,16},{16,24},{1,9},{9,17},{17,25},{2,10},{10,18},{18,26},{... | collective-permute-start | bytes 3464 | tf_op jit(solution)/shard_map/ppermute | solution.py:24
  125.2 1.5 collective-permute-done.25
  127.6 1.9 collective-permute-start.26
  129.5 3.9 %collective-permute-start.27 = (f32[1,16,1,256]{3,1,0,2:T(8,128)S(1)}, f32[1,16,1,256]{3,1,0,2:T(8,128)S(1)}, u32[]{:S(2)}, u32[]{:S(2)}) collective-permute-start(f32[1,16,1,256]{3,1,0,2:T(8,128)S(1)} %get-tuple-element.1125), channel_id=1, source_target_pairs={{0,32},{32,64},{64,96},{96,128},{128,160},{160,192},{192,224},{224... | collective-permute-start | bytes 49160 | tf_op jit(solution)/shard_map/ppermute | solution.py:24
  133.6 3.7 %collective-permute-done.27 = f32[1,16,1,256]{3,1,0,2:T(8,128)S(1)} collective-permute-done((f32[1,16,1,256]{3,1,0,2:T(8,128)S(1)}, f32[1,16,1,256]{3,1,0,2:T(8,128)S(1)}, u32[]{:S(2)}, u32[]{:S(2)}) %collective-permute-start.27) | collective-permute-done | bytes 16416 | tf_op jit(solution)/shard_map/ppermute | solution.py:24
  138.7 5.0 %collective-permute-start.29 = (f32[1,16,18,1]{3,1,0,2:T(8,128)S(1)}, f32[1,16,18,1]{3,1,0,2:T(8,128)S(1)}, u32[]{:S(2)}, u32[]{:S(2)}) collective-permute-start(f32[1,16,18,1]{3,1,0,2:T(8,128)S(1)} %get-tuple-element.1107), channel_id=1, source_target_pairs={{0,8},{8,16},{16,24},{1,9},{9,17},{17,25},{2,10},{10,18},{18,26},{... | collective-permute-start | bytes 3464 | tf_op jit(solution)/shard_map/ppermute | solution.py:24
  144.9 1.5 collective-permute-done.29
  147.2 1.9 collective-permute-start.30
  149.2 4.1 %collective-permute-start.31 = (f32[1,16,1,256]{3,1,0,2:T(8,128)S(1)}, f32[1,16,1,256]{3,1,0,2:T(8,128)S(1)}, u32[]{:S(2)}, u32[]{:S(2)}) collective-permute-start(f32[1,16,1,256]{3,1,0,2:T(8,128)S(1)} %get-tuple-element.1123), channel_id=1, source_target_pairs={{0,32},{32,64},{64,96},{96,128},{128,160},{160,192},{192,224},{224... | collective-permute-start | bytes 49160 | tf_op jit(solution)/shard_map/ppermute | solution.py:24
  153.3 2.2 slice_reduce_fusion.38
  159.6 5.7 %collective-permute-start.33 = (f32[1,16,18,1]{3,1,0,2:T(8,128)}, f32[1,16,18,1]{3,1,0,2:T(8,128)}, u32[]{:S(2)}, u32[]{:S(2)}) collective-permute-start(f32[1,16,18,1]{3,1,0,2:T(8,128)} %get-tuple-element.1105), channel_id=1, source_target_pairs={{0,8},{8,16},{16,24},{1,9},{9,17},{17,25},{2,10},{10,18},{18,26},{... | collective-permute-start | bytes 3464 | tf_op jit(solution)/shard_map/ppermute | solution.py:24
  167.6 2.5 fusion.288
  170.1 14.2 %all-to-all-start = ((f32[1,16,16,256]{3,1,0,2:T(8,128)}), f32[1,16,16,256]{3,1,0,2:T(8,128)S(1)}, u32[]{:S(2)}, u32[]{:S(2)}) async-start(f32[1,16,16,256]{3,1,0,2:T(8,128)} %fusion.288), calls=%async_computation | async-start | bytes 524288 | tf_op jit(solution)/shard_map/all_to_all | solution.py:66
  184.4 1.8 slice_reduce_fusion.39
  186.2 1.8 slice_reduce_fusion.90
  188.0 2.7 %slice_reduce_fusion.91 = (f32[2,256]{1,0:T(2,128)S(1)}, f32[2,256]{1,0:T(2,128)S(1)}, f32[2,256]{1,0:T(2,128)S(1)}, f32[2,256]{1,0:T(2,128)S(1)}, f32[2,256]{1,...) fusion(f32[127,2,256]{0,2,1:T(8,128)S(1)} %fusion.256), kind=kLoop, calls=%fused_computation.806 | loop fusion | bytes 77824 | tf_op jit(solution)/shard_map/vmap(vmap())/slice | solution.py:80
  190.7 2.7 %slice_reduce_fusion = (f32[2,256]{1,0:T(2,128)S(1)}, f32[2,256]{1,0:T(2,128)S(1)}, f32[2,256]{1,0:T(2,128)S(1)}, f32[2,256]{1,0:T(2,128)S(1)}, f32[2,256]{1,0:T...) fusion(f32[127,2,256]{0,2,1:T(8,128)S(1)} %slice_bitcast_fusion.1), kind=kLoop, calls=%fused_computation.715 | loop fusion | bytes 77824 | tf_op jit(solution)/shard_map/vmap(vmap())/slice | solution.py:80
  193.4 2.7 %slice_reduce_fusion.1 = (f32[2,256]{1,0:T(2,128)S(1)}, f32[2,256]{1,0:T(2,128)S(1)}, f32[2,256]{1,0:T(2,128)S(1)}, f32[2,256]{1,0:T(2,128)S(1)}, f32[2,256]{1,0...) fusion(f32[127,2,256]{0,2,1:T(8,128)S(1)} %slice_bitcast_fusion), kind=kLoop, calls=%fused_computation.716 | loop fusion | bytes 77824 | tf_op jit(solution)/shard_map/vmap(vmap())/slice | solution.py:80
  196.1 11.3 %all-to-all-done = f32[1,16,16,256]{3,1,0,2:T(8,128)S(1)} async-done(((f32[1,16,16,256]{3,1,0,2:T(8,128)}), f32[1,16,16,256]{3,1,0,2:T(8,128)S(1)}, u32[]{:S(2)}, u32[]{:S(2)}) %all-to-all-start) | async-done | bytes 262176 | tf_op jit(solution)/shard_map/all_to_all | solution.py:66
  209.9 5.3 %while.33 = (s32[]{:T(128)}, f32[2,256]{1,0:T(2,128)S(1)}, f32[2,256,1]{1,0,2:T(2,128)S(1)}, f32[3,32,2,256]{3,2,1,0:T(2,128)S(1)}, f32[3,32,2,256,1]{3,2,1,4,0:...) while((s32[]{:T(128)}, f32[2,256]{1,0:T(2,128)S(1)}, ...), condition=%wide.region_1.2_spmd, body=%wide.region_0.1_spmd.sunk | while | flops 131105 | bytes 1250533 | solution.py:80
  223.9 3.3 %while.34 = (s32[]{:T(128)}, f32[2,256,1]{1,2,0:T(1,128)S(1)}, f32[3,32,2,256,1]{3,2,4,1,0:T(2,128)S(1)}, f32[3,32,2,256,1]{3,2,1,0,4:T(2,128)S(1)}, f32[3,32,2,...) while((s32[]{:T(128)}, f32[2,256,1]{1,2,0:T(1,128)S(1)}, ...), condition=%wide.region_3.4_spmd, body=%wide.region_2.3_spmd.sunk | while | flops 32801 | bytes 723929 | solution.py:80
  227.8 25.2 %all_to_all.36 = f32[1,128,2,256]{3,2,0,1:T(2,128)S(1)} all-to-all(f32[1,128,2,256]{3,2,0,1:T(2,128)S(1)} %maximum_bitcast_fusion), channel_id=1, replica_groups=mesh['gx'=16,'gy'=4,'gz'=8] {'gz'}, dimensions={1} | all-to-all | bytes 524288 | tf_op jit(solution)/shard_map/all_to_all | solution.py:81
  (568 shorter events, 56.9 us)
Async XLA Ops:
  0.0 165.3 %copy-start = (f32[1,16,256]{2,1,0:T(8,128)S(1)}, f32[1,16,256]{2,1,0:T(8,128)}, u32[]{:S(2)}) copy-start(f32[1,16,256]{2,1,0:T(8,128)} %param.19) | copy-start | bytes 49156
  0.0 9.3 %copy-start.2 = (f32[16,16,256]{2,1,0:T(8,128)S(1)}, f32[16,16,256]{2,1,0:T(8,128)}, u32[]{:S(2)}) copy-start(f32[16,16,256]{2,1,0:T(8,128)} %param.14) | copy-start | bytes 786436
  0.0 11.3 %copy-start.1 = (f32[16,16,256]{2,1,0:T(8,128)S(1)}, f32[16,16,256]{2,1,0:T(8,128)}, u32[]{:S(2)}) copy-start(f32[16,16,256]{2,1,0:T(8,128)} %param.15) | copy-start | bytes 786436
  1.2 14.2 %copy-start.4 = (f32[1,16,16,256]{3,2,1,0:T(8,128)S(1)}, f32[1,16,16,256]{3,2,1,0:T(8,128)}, u32[]{:S(2)}) copy-start(f32[1,16,16,256]{3,2,1,0:T(8,128)} %param.13) | copy-start | bytes 786436
  1.2 14.2 %collective-permute-start.2 = (f32[1,16,1,256]{3,1,0,2:T(8,128)S(1)}, f32[1,16,1,256]{3,1,0,2:T(8,128)S(1)}, u32[]{:S(2)}, u32[]{:S(2)}) collective-permute-start(f32[1,16,1,256]{3,1,0,2:T(8,128)S(1)} %get-tuple-element.1142), channel_id=1, source_target_pairs={{0,32},{32,64},{64,96},{96,128},{128,160},{160,192},{192,224},{224... | collective-permute-start | bytes 49160 | tf_op jit(solution)/shard_map/ppermute | solution.py:24
  4.8 10.7 %collective-permute-start = (f32[1,16,1,256]{3,1,0,2:T(8,128)S(1)}, f32[1,16,1,256]{3,1,0,2:T(8,128)S(1)}, u32[]{:S(2)}, u32[]{:S(2)}) collective-permute-start(f32[1,16,1,256]{3,1,0,2:T(8,128)S(1)} %get-tuple-element.1141), channel_id=1, source_target_pairs={{32,0},{64,32},{96,64},{128,96},{160,128},{192,160},{224,192},{256... | collective-permute-start | bytes 49160 | tf_op jit(solution)/shard_map/ppermute | solution.py:27
  9.3 12.9 %collective-permute-start.1 = (f32[16,1,256]{2,1,0:T(1,128)S(1)}, f32[16,1,256]{2,1,0:T(1,128)S(1)}, u32[]{:S(2)}, u32[]{:S(2)}) collective-permute-start(f32[16,1,256]{2,1,0:T(1,128)S(1)} %slice.2209), channel_id=1, source_target_pairs={{0,32},{32,64},{64,96},{96,128},{128,160},{160,192},{192,224},{224... | collective-permute-start | bytes 49160 | tf_op jit(solution)/shard_map/ppermute | solution.py:16
  11.5 10.5 %collective-permute-start.4 = (f32[16,16,1]{1,0,2:T(8,128)S(1)}, f32[16,16,1]{1,0,2:T(8,128)S(1)}, u32[]{:S(2)}, u32[]{:S(2)}) collective-permute-start(f32[16,16,1]{1,0,2:T(8,128)S(1)} %copy.2908), channel_id=1, source_target_pairs={{0,8},{8,16},{16,24},{1,9},{9,17},{17,25},{2,10},{10,18},{18,26},{... | collective-permute-start | bytes 3080 | tf_op jit(solution)/shard_map/ppermute | solution.py:16
  15.7 7.0 %collective-permute-start.3 = (f32[1,16,18,1]{3,1,0,2:T(8,128)S(1)}, f32[1,16,18,1]{3,1,0,2:T(8,128)S(1)}, u32[]{:S(2)}, u32[]{:S(2)}) collective-permute-start(f32[1,16,18,1]{3,1,0,2:T(8,128)S(1)} %get-tuple-element.1120), channel_id=1, source_target_pairs={{8,0},{16,8},{24,16},{9,1},{17,9},{25,17},{10,2},{18,10},{26,18},{... | collective-permute-start | bytes 3464 | tf_op jit(solution)/shard_map/ppermute | solution.py:27
  17.0 7.2 %collective-permute-start.5 = (f32[1,16,18,1]{3,1,0,2:T(8,128)S(1)}, f32[1,16,18,1]{3,1,0,2:T(8,128)S(1)}, u32[]{:S(2)}, u32[]{:S(2)}) collective-permute-start(f32[1,16,18,1]{3,1,0,2:T(8,128)S(1)} %get-tuple-element.1119), channel_id=1, source_target_pairs={{0,8},{8,16},{16,24},{1,9},{9,17},{17,25},{2,10},{10,18},{18,26},{... | collective-permute-start | bytes 3464 | tf_op jit(solution)/shard_map/ppermute | solution.py:24
  25.1 8.0 %collective-permute-start.6 = (f32[1,16,1,256]{3,1,0,2:T(8,128)S(1)}, f32[1,16,1,256]{3,1,0,2:T(8,128)S(1)}, u32[]{:S(2)}, u32[]{:S(2)}) collective-permute-start(f32[1,16,1,256]{3,1,0,2:T(8,128)S(1)} %get-tuple-element.1136), channel_id=1, source_target_pairs={{32,0},{64,32},{96,64},{128,96},{160,128},{192,160},{224,192},{256... | collective-permute-start | bytes 49160 | tf_op jit(solution)/shard_map/ppermute | solution.py:27
  31.2 7.7 %collective-permute-start.7 = (f32[1,16,1,256]{3,1,0,2:T(8,128)S(1)}, f32[1,16,1,256]{3,1,0,2:T(8,128)S(1)}, u32[]{:S(2)}, u32[]{:S(2)}) collective-permute-start(f32[1,16,1,256]{3,1,0,2:T(8,128)S(1)} %get-tuple-element.1135), channel_id=1, source_target_pairs={{0,32},{32,64},{64,96},{96,128},{128,160},{160,192},{192,224},{224... | collective-permute-start | bytes 49160 | tf_op jit(solution)/shard_map/ppermute | solution.py:24
  39.0 7.5 %collective-permute-start.8 = (f32[1,16,18,1]{3,1,0,2:T(8,128)S(1)}, f32[1,16,18,1]{3,1,0,2:T(8,128)S(1)}, u32[]{:S(2)}, u32[]{:S(2)}) collective-permute-start(f32[1,16,18,1]{3,1,0,2:T(8,128)S(1)} %get-tuple-element.1118), channel_id=1, source_target_pairs={{8,0},{16,8},{24,16},{9,1},{17,9},{25,17},{10,2},{18,10},{26,18},{... | collective-permute-start | bytes 3464 | tf_op jit(solution)/shard_map/ppermute | solution.py:27
  40.3 7.7 %collective-permute-start.9 = (f32[1,16,18,1]{3,1,0,2:T(8,128)S(1)}, f32[1,16,18,1]{3,1,0,2:T(8,128)S(1)}, u32[]{:S(2)}, u32[]{:S(2)}) collective-permute-start(f32[1,16,18,1]{3,1,0,2:T(8,128)S(1)} %get-tuple-element.1117), channel_id=1, source_target_pairs={{0,8},{8,16},{16,24},{1,9},{9,17},{17,25},{2,10},{10,18},{18,26},{... | collective-permute-start | bytes 3464 | tf_op jit(solution)/shard_map/ppermute | solution.py:24
  48.9 5.9 %collective-permute-start.10 = (f32[1,16,1,256]{3,1,0,2:T(8,128)S(1)}, f32[1,16,1,256]{3,1,0,2:T(8,128)S(1)}, u32[]{:S(2)}, u32[]{:S(2)}) collective-permute-start(f32[1,16,1,256]{3,1,0,2:T(8,128)S(1)} %get-tuple-element.1134), channel_id=1, source_target_pairs={{32,0},{64,32},{96,64},{128,96},{160,128},{192,160},{224,192},{256... | collective-permute-start | bytes 49160 | tf_op jit(solution)/shard_map/ppermute | solution.py:27
  50.8 7.7 %collective-permute-start.11 = (f32[1,16,1,256]{3,1,0,2:T(8,128)S(1)}, f32[1,16,1,256]{3,1,0,2:T(8,128)S(1)}, u32[]{:S(2)}, u32[]{:S(2)}) collective-permute-start(f32[1,16,1,256]{3,1,0,2:T(8,128)S(1)} %get-tuple-element.1133), channel_id=1, source_target_pairs={{0,32},{32,64},{64,96},{96,128},{128,160},{160,192},{192,224},{224... | collective-permute-start | bytes 49160 | tf_op jit(solution)/shard_map/ppermute | solution.py:24
  58.7 7.5 %collective-permute-start.12 = (f32[1,16,18,1]{3,1,0,2:T(8,128)S(1)}, f32[1,16,18,1]{3,1,0,2:T(8,128)S(1)}, u32[]{:S(2)}, u32[]{:S(2)}) collective-permute-start(f32[1,16,18,1]{3,1,0,2:T(8,128)S(1)} %get-tuple-element.1116), channel_id=1, source_target_pairs={{8,0},{16,8},{24,16},{9,1},{17,9},{25,17},{10,2},{18,10},{26,18},{... | collective-permute-start | bytes 3464 | tf_op jit(solution)/shard_map/ppermute | solution.py:27
  60.0 7.7 %collective-permute-start.13 = (f32[1,16,18,1]{3,1,0,2:T(8,128)S(1)}, f32[1,16,18,1]{3,1,0,2:T(8,128)S(1)}, u32[]{:S(2)}, u32[]{:S(2)}) collective-permute-start(f32[1,16,18,1]{3,1,0,2:T(8,128)S(1)} %get-tuple-element.1115), channel_id=1, source_target_pairs={{0,8},{8,16},{16,24},{1,9},{9,17},{17,25},{2,10},{10,18},{18,26},{... | collective-permute-start | bytes 3464 | tf_op jit(solution)/shard_map/ppermute | solution.py:24
  68.6 5.9 %collective-permute-start.14 = (f32[1,16,1,256]{3,1,0,2:T(8,128)S(1)}, f32[1,16,1,256]{3,1,0,2:T(8,128)S(1)}, u32[]{:S(2)}, u32[]{:S(2)}) collective-permute-start(f32[1,16,1,256]{3,1,0,2:T(8,128)S(1)} %get-tuple-element.1132), channel_id=1, source_target_pairs={{32,0},{64,32},{96,64},{128,96},{160,128},{192,160},{224,192},{256... | collective-permute-start | bytes 49160 | tf_op jit(solution)/shard_map/ppermute | solution.py:27
  70.5 7.7 %collective-permute-start.15 = (f32[1,16,1,256]{3,1,0,2:T(8,128)S(1)}, f32[1,16,1,256]{3,1,0,2:T(8,128)S(1)}, u32[]{:S(2)}, u32[]{:S(2)}) collective-permute-start(f32[1,16,1,256]{3,1,0,2:T(8,128)S(1)} %get-tuple-element.1131), channel_id=1, source_target_pairs={{0,32},{32,64},{64,96},{96,128},{128,160},{160,192},{192,224},{224... | collective-permute-start | bytes 49160 | tf_op jit(solution)/shard_map/ppermute | solution.py:24
  78.4 7.5 %collective-permute-start.16 = (f32[1,16,18,1]{3,1,0,2:T(8,128)S(1)}, f32[1,16,18,1]{3,1,0,2:T(8,128)S(1)}, u32[]{:S(2)}, u32[]{:S(2)}) collective-permute-start(f32[1,16,18,1]{3,1,0,2:T(8,128)S(1)} %get-tuple-element.1114), channel_id=1, source_target_pairs={{8,0},{16,8},{24,16},{9,1},{17,9},{25,17},{10,2},{18,10},{26,18},{... | collective-permute-start | bytes 3464 | tf_op jit(solution)/shard_map/ppermute | solution.py:27
  79.7 7.7 %collective-permute-start.17 = (f32[1,16,18,1]{3,1,0,2:T(8,128)S(1)}, f32[1,16,18,1]{3,1,0,2:T(8,128)S(1)}, u32[]{:S(2)}, u32[]{:S(2)}) collective-permute-start(f32[1,16,18,1]{3,1,0,2:T(8,128)S(1)} %get-tuple-element.1113), channel_id=1, source_target_pairs={{0,8},{8,16},{16,24},{1,9},{9,17},{17,25},{2,10},{10,18},{18,26},{... | collective-permute-start | bytes 3464 | tf_op jit(solution)/shard_map/ppermute | solution.py:24
  88.2 5.9 %collective-permute-start.18 = (f32[1,16,1,256]{3,1,0,2:T(8,128)S(1)}, f32[1,16,1,256]{3,1,0,2:T(8,128)S(1)}, u32[]{:S(2)}, u32[]{:S(2)}) collective-permute-start(f32[1,16,1,256]{3,1,0,2:T(8,128)S(1)} %get-tuple-element.1130), channel_id=1, source_target_pairs={{32,0},{64,32},{96,64},{128,96},{160,128},{192,160},{224,192},{256... | collective-permute-start | bytes 49160 | tf_op jit(solution)/shard_map/ppermute | solution.py:27
  90.2 7.7 %collective-permute-start.19 = (f32[1,16,1,256]{3,1,0,2:T(8,128)S(1)}, f32[1,16,1,256]{3,1,0,2:T(8,128)S(1)}, u32[]{:S(2)}, u32[]{:S(2)}) collective-permute-start(f32[1,16,1,256]{3,1,0,2:T(8,128)S(1)} %get-tuple-element.1129), channel_id=1, source_target_pairs={{0,32},{32,64},{64,96},{96,128},{128,160},{160,192},{192,224},{224... | collective-permute-start | bytes 49160 | tf_op jit(solution)/shard_map/ppermute | solution.py:24
  98.0 7.5 %collective-permute-start.20 = (f32[1,16,18,1]{3,1,0,2:T(8,128)S(1)}, f32[1,16,18,1]{3,1,0,2:T(8,128)S(1)}, u32[]{:S(2)}, u32[]{:S(2)}) collective-permute-start(f32[1,16,18,1]{3,1,0,2:T(8,128)S(1)} %get-tuple-element.1112), channel_id=1, source_target_pairs={{8,0},{16,8},{24,16},{9,1},{17,9},{25,17},{10,2},{18,10},{26,18},{... | collective-permute-start | bytes 3464 | tf_op jit(solution)/shard_map/ppermute | solution.py:27
  99.3 7.7 %collective-permute-start.21 = (f32[1,16,18,1]{3,1,0,2:T(8,128)S(1)}, f32[1,16,18,1]{3,1,0,2:T(8,128)S(1)}, u32[]{:S(2)}, u32[]{:S(2)}) collective-permute-start(f32[1,16,18,1]{3,1,0,2:T(8,128)S(1)} %get-tuple-element.1111), channel_id=1, source_target_pairs={{0,8},{8,16},{16,24},{1,9},{9,17},{17,25},{2,10},{10,18},{18,26},{... | collective-permute-start | bytes 3464 | tf_op jit(solution)/shard_map/ppermute | solution.py:24
  107.9 5.9 %copy-start.21 = (f32[8,128]{1,0:T(8,128)S(1)}, f32[8,128]{1,0:T(8,128)}, u32[]{:S(2)}) copy-start(f32[8,128]{1,0:T(8,128)} %param.16) | copy-start | bytes 12292
  107.9 6.3 %collective-permute-start.22 = (f32[1,16,1,256]{3,1,0,2:T(8,128)S(1)}, f32[1,16,1,256]{3,1,0,2:T(8,128)S(1)}, u32[]{:S(2)}, u32[]{:S(2)}) collective-permute-start(f32[1,16,1,256]{3,1,0,2:T(8,128)S(1)} %get-tuple-element.1128), channel_id=1, source_target_pairs={{32,0},{64,32},{96,64},{128,96},{160,128},{192,160},{224,192},{256... | collective-permute-start | bytes 49160 | tf_op jit(solution)/shard_map/ppermute | solution.py:27
  109.8 7.7 %collective-permute-start.23 = (f32[1,16,1,256]{3,1,0,2:T(8,128)S(1)}, f32[1,16,1,256]{3,1,0,2:T(8,128)S(1)}, u32[]{:S(2)}, u32[]{:S(2)}) collective-permute-start(f32[1,16,1,256]{3,1,0,2:T(8,128)S(1)} %get-tuple-element.1127), channel_id=1, source_target_pairs={{0,32},{32,64},{64,96},{96,128},{128,160},{160,192},{192,224},{224... | collective-permute-start | bytes 49160 | tf_op jit(solution)/shard_map/ppermute | solution.py:24
  117.7 7.5 %collective-permute-start.24 = (f32[1,16,18,1]{3,1,0,2:T(8,128)S(1)}, f32[1,16,18,1]{3,1,0,2:T(8,128)S(1)}, u32[]{:S(2)}, u32[]{:S(2)}) collective-permute-start(f32[1,16,18,1]{3,1,0,2:T(8,128)S(1)} %get-tuple-element.1110), channel_id=1, source_target_pairs={{8,0},{16,8},{24,16},{9,1},{17,9},{25,17},{10,2},{18,10},{26,18},{... | collective-permute-start | bytes 3464 | tf_op jit(solution)/shard_map/ppermute | solution.py:27
  119.0 5.0 %copy-start.20 = (pred[128]{0:T(512)(128)(4,1)S(1)}, pred[128]{0:T(512)(128)(4,1)}, u32[]{:S(2)}) copy-start(pred[128]{0:T(512)(128)(4,1)} %constant.93.clone.1) | copy-start | bytes 388
  119.0 7.7 %collective-permute-start.25 = (f32[1,16,18,1]{3,1,0,2:T(8,128)S(1)}, f32[1,16,18,1]{3,1,0,2:T(8,128)S(1)}, u32[]{:S(2)}, u32[]{:S(2)}) collective-permute-start(f32[1,16,18,1]{3,1,0,2:T(8,128)S(1)} %get-tuple-element.1109), channel_id=1, source_target_pairs={{0,8},{8,16},{16,24},{1,9},{9,17},{17,25},{2,10},{10,18},{18,26},{... | collective-permute-start | bytes 3464 | tf_op jit(solution)/shard_map/ppermute | solution.py:24
  127.6 6.0 %collective-permute-start.26 = (f32[1,16,1,256]{3,1,0,2:T(8,128)S(1)}, f32[1,16,1,256]{3,1,0,2:T(8,128)S(1)}, u32[]{:S(2)}, u32[]{:S(2)}) collective-permute-start(f32[1,16,1,256]{3,1,0,2:T(8,128)S(1)} %get-tuple-element.1126), channel_id=1, source_target_pairs={{32,0},{64,32},{96,64},{128,96},{160,128},{192,160},{224,192},{256... | collective-permute-start | bytes 49160 | tf_op jit(solution)/shard_map/ppermute | solution.py:27
  129.5 7.7 %collective-permute-start.27 = (f32[1,16,1,256]{3,1,0,2:T(8,128)S(1)}, f32[1,16,1,256]{3,1,0,2:T(8,128)S(1)}, u32[]{:S(2)}, u32[]{:S(2)}) collective-permute-start(f32[1,16,1,256]{3,1,0,2:T(8,128)S(1)} %get-tuple-element.1125), channel_id=1, source_target_pairs={{0,32},{32,64},{64,96},{96,128},{128,160},{160,192},{192,224},{224... | collective-permute-start | bytes 49160 | tf_op jit(solution)/shard_map/ppermute | solution.py:24
  137.4 7.5 %collective-permute-start.28 = (f32[1,16,18,1]{3,1,0,2:T(8,128)S(1)}, f32[1,16,18,1]{3,1,0,2:T(8,128)S(1)}, u32[]{:S(2)}, u32[]{:S(2)}) collective-permute-start(f32[1,16,18,1]{3,1,0,2:T(8,128)S(1)} %get-tuple-element.1108), channel_id=1, source_target_pairs={{8,0},{16,8},{24,16},{9,1},{17,9},{25,17},{10,2},{18,10},{26,18},{... | collective-permute-start | bytes 3464 | tf_op jit(solution)/shard_map/ppermute | solution.py:27
  138.7 7.7 %collective-permute-start.29 = (f32[1,16,18,1]{3,1,0,2:T(8,128)S(1)}, f32[1,16,18,1]{3,1,0,2:T(8,128)S(1)}, u32[]{:S(2)}, u32[]{:S(2)}) collective-permute-start(f32[1,16,18,1]{3,1,0,2:T(8,128)S(1)} %get-tuple-element.1107), channel_id=1, source_target_pairs={{0,8},{8,16},{16,24},{1,9},{9,17},{17,25},{2,10},{10,18},{18,26},{... | collective-permute-start | bytes 3464 | tf_op jit(solution)/shard_map/ppermute | solution.py:24
  147.2 8.3 %collective-permute-start.30 = (f32[1,16,1,256]{3,1,0,2:T(8,128)S(1)}, f32[1,16,1,256]{3,1,0,2:T(8,128)S(1)}, u32[]{:S(2)}, u32[]{:S(2)}) collective-permute-start(f32[1,16,1,256]{3,1,0,2:T(8,128)S(1)} %get-tuple-element.1124), channel_id=1, source_target_pairs={{32,0},{64,32},{96,64},{128,96},{160,128},{192,160},{224,192},{256... | collective-permute-start | bytes 49160 | tf_op jit(solution)/shard_map/ppermute | solution.py:27
  149.2 7.7 %collective-permute-start.31 = (f32[1,16,1,256]{3,1,0,2:T(8,128)S(1)}, f32[1,16,1,256]{3,1,0,2:T(8,128)S(1)}, u32[]{:S(2)}, u32[]{:S(2)}) collective-permute-start(f32[1,16,1,256]{3,1,0,2:T(8,128)S(1)} %get-tuple-element.1123), channel_id=1, source_target_pairs={{0,32},{32,64},{64,96},{96,128},{128,160},{160,192},{192,224},{224... | collective-permute-start | bytes 49160 | tf_op jit(solution)/shard_map/ppermute | solution.py:24
  155.5 1.4 copy-start.7
  158.3 8.1 %collective-permute-start.32 = (f32[1,16,18,1]{3,1,0,2:T(8,128)}, f32[1,16,18,1]{3,1,0,2:T(8,128)}, u32[]{:S(2)}, u32[]{:S(2)}) collective-permute-start(f32[1,16,18,1]{3,1,0,2:T(8,128)} %get-tuple-element.1106), channel_id=1, source_target_pairs={{8,0},{16,8},{24,16},{9,1},{17,9},{25,17},{10,2},{18,10},{26,18},{... | collective-permute-start | bytes 3464 | tf_op jit(solution)/shard_map/ppermute | solution.py:27
  159.6 8.0 %collective-permute-start.33 = (f32[1,16,18,1]{3,1,0,2:T(8,128)}, f32[1,16,18,1]{3,1,0,2:T(8,128)}, u32[]{:S(2)}, u32[]{:S(2)}) collective-permute-start(f32[1,16,18,1]{3,1,0,2:T(8,128)} %get-tuple-element.1105), channel_id=1, source_target_pairs={{0,8},{8,16},{16,24},{1,9},{9,17},{17,25},{2,10},{10,18},{18,26},{... | collective-permute-start | bytes 3464 | tf_op jit(solution)/shard_map/ppermute | solution.py:24
  170.1 37.4 %all-to-all-start = ((f32[1,16,16,256]{3,1,0,2:T(8,128)}), f32[1,16,16,256]{3,1,0,2:T(8,128)S(1)}, u32[]{:S(2)}, u32[]{:S(2)}) async-start(f32[1,16,16,256]{3,1,0,2:T(8,128)} %fusion.288), calls=%async_computation | async-start | bytes 524288 | tf_op jit(solution)/shard_map/all_to_all | solution.py:66
  207.7 1.0 copy-start.3
  208.9 0.9 copy-start.5
  208.9 1.0 copy-start.6
  215.2 0.7 copy-start.19
  217.3 0.7 copy-start.16
  222.1 0.7 copy-start.9
  (9 other events, 6.0 us)
where the time goes:
time: 256 us; the launch traced here: 254 us
  starting transfers between devices  122 us (48%)
  waiting for transfers between devices  55.1 us (22%)
  local copies, waits for them, and re-layouts  34.6 us (14%)
  blocking collectives  25.2 us (10%)
  other arithmetic  14.4 us (6%)
    ppermute x16, starting transfers between devices, padded_2(): lax.ppermute(lax.slice_in_dim(block, block.shape[dim] - width, None, axis...  69.5 us
    ppermute x16, waiting for transfers between devices, padded_2(): lax.ppermute(lax.slice_in_dim(block, block.shape[dim] - width, None, axis...  37.2 us
    ppermute x16, starting transfers between devices, padded_2(): lax.ppermute(lax.slice_in_dim(block, 0, width, axis=dim), axis, backward)  32.3 us
    all_to_all x1, blocking collectives, local(): lax.all_to_all(jnp.transpose(solved, (3, 2, 0, 1)), 'gz', split_axis=1, c...  25.2 us
    slice x30, local copies, waits for them, and re-layouts, local(): lax.linalg.tridiagonal_solve(-below, 1.0 + below + above, upper, rhs)  16 us
    all_to_all x1, starting transfers between devices, local(): lax.all_to_all(conc, 'gz', split_axis=2, concat_axis=1, tiled=True)  14.2 us
    unnamed x69, local copies, waits for them, and re-layouts  11.4 us
    all_to_all x1, waiting for transfers between devices, local(): lax.all_to_all(conc, 'gz', split_axis=2, concat_axis=1, tiled=True)  11.3 us
  transfers between devices with their start and end apart: 35, of which 23 were waited for; matrix products, arithmetic and copies ran while one was open for 7% of the time, Pallas kernels for 0%

commit v1 on v0

v1 whole, which is shorter than its diff:
```python
import jax
import jax.numpy as jnp
from jax import lax
from jax.experimental import pallas as pl
from jax.experimental.pallas import tpu as pltpu
from jax.sharding import PartitionSpec as P

HSTEPS = 8
NCLASS = 8
TILE = 128
DIFFUSION = 0.05
CANOPY = 0.2
LIMIT = 24 * 1024 * 1024

VMEM = pl.BlockSpec(memory_space=pltpu.VMEM)
SMEM = pl.BlockSpec(memory_space=pltpu.SMEM)


def call(kernel, outs, n_smem, scratch, flops):
    return lambda *args: pl.pallas_call(
        kernel,
        out_shape=[jax.ShapeDtypeStruct(s, jnp.float32) for s in outs],
        in_specs=[SMEM] * n_smem + [VMEM] * (len(args) - n_smem),
        out_specs=[VMEM] * len(outs),
        scratch_shapes=[pltpu.VMEM(s, jnp.float32) for s in scratch],
        compiler_params=pltpu.CompilerParams(vmem_limit_bytes=LIMIT),
        cost_estimate=pl.CostEstimate(flops=flops, bytes_accessed=1 << 20, transcendentals=0),
    )(*args)


def pack_kernel(c_ref, wx_ref, wy_ref, lo_ref, hi_ref, yl_ref, yr_ref):
    depth, rows, width = c_ref.shape
    half, strip = rows // 2, HSTEPS
    lane = lax.broadcasted_iota(jnp.int32, (depth, TILE), 1) // strip
    for a, ref in enumerate((c_ref, wx_ref, wy_ref)):
        left = jnp.zeros((depth, TILE), jnp.float32)
        right = left
        for x in range(rows):
            row = ref[:, x, :]
            if x < half:
                lo_ref[a * half + x] = row
            else:
                hi_ref[a * half + x - half] = row
            at = strip * x
            first, last = row[:, :TILE], row[:, width - TILE :]
            if at:
                first = pltpu.roll(first, at, 1)
            if (at + strip) % TILE:
                last = pltpu.roll(last, (at + strip) % TILE, 1)
            left = jnp.where(lane == x, first, left)
            right = jnp.where(lane == x, last, right)
        yl_ref[a] = left
        yr_ref[a] = right


def mixing_kernel(idx_ref, profiles_ref, classes_ref, heights_ref,
                  f_ref, h_ref, g_ref, a_ref, b_ref, w_ref,
                  k_ref, e_ref, d_ref, up_ref, down_ref):
    me = idx_ref[2]
    depth = g_ref.shape[0]
    groups = w_ref.shape[0]
    shape = classes_ref.shape
    total = depth * groups
    classes, heights = classes_ref[...], heights_ref[...]
    bits = [(classes & (1 << b)) != 0 for b in range(3)]

    k_ref[0] = jnp.zeros(shape, jnp.float32)

    def mixing(z, _):
        table = [profiles_ref[c, z] for c in range(NCLASS)]
        for bit in bits:
            table = [jnp.where(bit, table[i + 1], table[i]) for i in range(0, len(table), 2)]
        k = table[0]
        k_ref[z + 1] = jnp.where(z < heights, CANOPY * k, k)
        return 0

    lax.fori_loop(0, total, mixing, 0, unroll=2)

    one = jnp.ones(shape, jnp.float32)

    def chunk(n, carry):
        e, d = carry
        m = groups - 1 - n
        aside_e = jnp.where(n == me, 0, depth)
        aside_d = jnp.where(m == me, 0, depth)

        def level(i, carry):
            e, d, up, down = carry
            k = k_ref[n * depth + i + 1]
            f = k / (e + k)
            f_ref[aside_e + i] = f
            e_ref[aside_e + i] = e
            j = depth - 1 - i
            kb = k_ref[m * depth + j]
            h = kb / (d + kb)
            h_ref[aside_d + j] = h
            d_ref[aside_d + j] = d
            return 1.0 + f * e, 1.0 + h * d, up * f, down * h

        e, d, up, down = lax.fori_loop(0, depth, level, (e, d, one, one))
        up_ref[n] = up
        down_ref[m] = down
        return e, d

    lax.fori_loop(0, groups, chunk, (one, 1.0 + k_ref[total]))

    run = one
    for i in range(depth):
        g = 1.0 / (e_ref[i] + d_ref[i] - 1.0)
        g_ref[i] = g
        a_ref[i] = g * run
        run = run * f_ref[i]
    run = one
    for i in reversed(range(depth)):
        b_ref[i] = g_ref[i] * run
        run = run * h_ref[i]
    zero = jnp.zeros(shape, jnp.float32)
    run = one
    for s in reversed(range(groups)):
        below = s < me
        w_ref[s] = jnp.where(below, run, zero)
        run = jnp.where(below, run * up_ref[s], one)
    run = one
    for s in range(groups):
        above = s > me
        w_ref[s] = w_ref[s] + jnp.where(above, run, zero)
        run = jnp.where(above, run * down_ref[s], one)


def transport_kernel(idx_ref, lo_ref, hi_ref, west_ref, east_ref, f_ref, h_ref, g_ref, emission_ref,
                     u_ref, send_ref, c_ref, k_ref, t_ref):
    gx, gy, me = idx_ref[0], idx_ref[1], idx_ref[2]
    depth, rows, width = u_ref.shape
    groups = send_ref.shape[0]
    half, strip = rows // 2, HSTEPS
    ext = rows + 2 * strip
    wide = width + TILE
    lane = lax.broadcasted_iota(jnp.int32, (depth, TILE), 1)
    n_gx, n_gy = idx_ref[3], idx_ref[4]

    def plane(a, r):
        if r < strip:
            ref, at, group = west_ref, r, half + r
        elif r < strip + half:
            ref, at, group = lo_ref, r - strip, r - strip
        elif r < strip + rows:
            ref, at, group = hi_ref, r - strip - half, r - strip
        else:
            ref, at, group = east_ref, r - strip - rows, r - strip - rows
        side = ref[3 * half + a]
        low, high = side[:, :TILE], side[:, TILE:]
        shift_high = (-strip * group) % TILE
        shift_low = (-strip * (group + 1)) % TILE
        if shift_high:
            high = pltpu.roll(high, shift_high, 1)
        if shift_low:
            low = pltpu.roll(low, shift_low, 1)
        last = jnp.where(lane < strip, high, jnp.where(lane >= TILE - strip, low, 0.0))
        return jnp.concatenate([ref[a * half + at], last], axis=1)

    one = jnp.ones((depth, width), jnp.float32)
    sides = jnp.where((lane < strip) & (gy < n_gy - 1) | (lane >= TILE - strip) & (gy > 0), 1.0, 0.0)
    inside = jnp.concatenate([one, sides], axis=1)
    west_in = inside * jnp.where(gx > 0, 1.0, 0.0)
    east_in = inside * jnp.where(gx < n_gx - 1, 1.0, 0.0)

    c_ref[0] = plane(0, 0)
    c_ref[ext - 1] = plane(0, ext - 1)
    aw = plane(1, 0)
    for r in range(1, ext - 1):
        c_ref[r] = plane(0, r)
        ax, ay = plane(1, r), plane(2, r)
        south = pltpu.roll(ay, 1, 1)
        ax_up, aw_up = jnp.maximum(ax, 0.0), jnp.maximum(aw, 0.0)
        ay_up, as_up = jnp.maximum(ay, 0.0), jnp.maximum(south, 0.0)
        ax_down, aw_down = jnp.minimum(ax, 0.0), jnp.minimum(aw, 0.0)
        ay_down, as_down = jnp.minimum(ay, 0.0), jnp.minimum(south, 0.0)
        own = (1.0 - 4.0 * DIFFUSION) - (ax_up - aw_down) - (ay_up - as_down)
        mask = west_in if r < strip else east_in if r >= strip + rows else inside
        k_ref[0, r] = own * mask
        k_ref[1, r] = (DIFFUSION - ax_down) * mask
        k_ref[2, r] = (DIFFUSION + aw_up) * mask
        k_ref[3, r] = (DIFFUSION - ay_down) * mask
        k_ref[4, r] = (DIFFUSION + as_up) * mask
        aw = ax

    for step in range(1, HSTEPS + 1):

        def row(r, carry):
            west, own = carry
            east = c_ref[r + 1]
            north = pltpu.roll(own, wide - 1, 1)
            south = pltpu.roll(own, 1, 1)
            c_ref[r] = (
                (k_ref[0, r] * own + k_ref[1, r] * east)
                + (k_ref[2, r] * west + k_ref[3, r] * north)
                + k_ref[4, r] * south
            )
            return own, east

        lax.fori_loop(step, ext - step, row, (c_ref[step - 1], c_ref[step]), unroll=2)

    def level(z):
        d = c_ref[strip : strip + rows, z, :width]
        if z == 0:
            d = d + emission_ref[...] * jnp.where(me == 0, 1.0, 0.0)
        return d

    run = None
    for z in range(depth):
        d = level(z)
        run = d if z == 0 else d + f_ref[z - 1] * run
        t_ref[z] = run - d
    beta = f_ref[depth - 1] * run
    run = None
    for z in reversed(range(depth)):
        d = level(z)
        run = d if z == depth - 1 else d + h_ref[z + 1] * run
        u_ref[z] = g_ref[z] * (t_ref[z] + run)
    gamma = h_ref[0] * run
    for s in range(groups):
        send_ref[s] = jnp.where(s > me, beta, gamma)


def finish_kernel(idx_ref, u_ref, a_ref, b_ref, w_ref, got_ref, out_ref):
    me = idx_ref[2]
    depth, rows, width = u_ref.shape
    groups = w_ref.shape[0]
    zero = jnp.zeros((rows, width), jnp.float32)
    below, above = zero, zero
    for s in range(groups):
        term = w_ref[s] * got_ref[s]
        below = below + jnp.where(s < me, term, zero)
        above = above + jnp.where(s > me, term, zero)
    for z in range(depth):
        out_ref[z] = u_ref[z] + (a_ref[z] * below + b_ref[z] * above)


def shifted(x, axis, by):
    length = lax.axis_size(axis)
    return lax.ppermute(x, axis, [(i, i + by) for i in range(length) if 0 <= i + by < length])


def local(conc, wind_x, wind_y, profiles, classes, heights, emission):
    species, depth, rows, width = conc.shape
    groups = lax.axis_size("gz")
    half, ext, wide = rows // 2, rows + 2 * HSTEPS, width + TILE
    idx = jnp.stack(
        [lax.axis_index("gx"), lax.axis_index("gy"), lax.axis_index("gz"),
         jnp.int32(lax.axis_size("gx")), jnp.int32(lax.axis_size("gy"))]
    ).astype(jnp.int32)
    block, pane = (depth, rows, width), (rows, width)
    planes = 3 * half + 3

    lo, hi, left, right = call(
        pack_kernel, [(planes, depth, width)] * 2 + [(3, depth, TILE)] * 2, 0, [], 1 << 20
    )(conc[0], wind_x, wind_y)
    from_south = shifted(right, "gy", 1)
    from_north = shifted(left, "gy", -1)
    side = jnp.concatenate([from_south, from_north], axis=2)
    lo = lax.dynamic_update_slice(lo, side, (3 * half, 0, 0))
    hi = lax.dynamic_update_slice(hi, side, (3 * half, 0, 0))
    west = shifted(hi, "gx", 1)
    east = shifted(lo, "gx", -1)

    twice = (2 * depth, rows, width)
    f, h, g, a, b, w = call(
        mixing_kernel, [twice, twice, block, block, block, (groups, *pane)], 2,
        [(depth * groups + 1, *pane), twice, twice, (groups, *pane), (groups, *pane)], 1 << 26,
    )(idx, profiles, classes, heights)

    u, send = call(
        transport_kernel, [block, (groups, *pane)], 1,
        [(ext, depth, wide), (5, ext, depth, wide), block], 1 << 24,
    )(idx, lo, hi, west, east, f, h, g, emission[0])
    got = lax.all_to_all(send, "gz", split_axis=0, concat_axis=0, tiled=True)
    (out,) = call(finish_kernel, [block], 1, [], 1 << 20)(idx, u, a, b, w, got)
    return out[None]


def solution(mesh):
    return jax.shard_map(
        local,
        mesh=mesh,
        in_specs=(
            P(None, "gz", "gx", "gy"),
            P("gz", "gx", "gy"),
            P("gz", "gx", "gy"),
            P(),
            P("gx", "gy"),
            P("gx", "gy"),
            P(None, "gx", "gy"),
        ),
        out_specs=P(None, "gz", "gx", "gy"),
        check_vma=False,
    )
```

time: 256 us -> 73.7 us (0.29)
  the two profiles are of different devices: /device:TPU:4 before, /device:TPU:58 now
where the time goes in v1:
time: 73.7 us; the launch traced here: 73.4 us
  blocking collectives  30.1 us (41%)
  Pallas kernels  17.7 us (24%)
  starting transfers between devices  11.7 us (16%)
  waiting for transfers between devices  10.2 us (14%)
  local copies, waits for them, and re-layouts  3.55 us (5%)
    all_to_all x1, blocking collectives, local(): got = lax.all_to_all(send, 'gz', split_axis=0, concat_axis=0, tiled=True)  30.1 us
    pallas_call x4, Pallas kernels, call(): pl.pallas_call(kernel, out_shape=[jax.ShapeDtypeStruct(s, jnp.float32) fo...  17.7 us
    ppermute x4, starting transfers between devices, shifted(): lax.ppermute(x, axis, [(i, i + by) for i in range(length) if 0 <= i + by...  11.7 us
    ppermute x4, waiting for transfers between devices, shifted(): lax.ppermute(x, axis, [(i, i + by) for i in range(length) if 0 <= i + by...  10.2 us
    unnamed x15, local copies, waits for them, and re-layouts  3.46 us
  transfers between devices with their start and end apart: 4, of which 3 were waited for; matrix products, arithmetic and copies ran while one was open for 0% of the time, Pallas kernels for 6%

profile of v1, /device:TPU:58, one launch (start us, length us, event | category | flops | bytes accessed | tf_op | source)
XLA Modules:
  0.0 73.4 jit_solution(4155049941994288061)
XLA Ops:
  0.0 0.0 copy-start
  0.0 0.9 %copy-done = f32[1,16,16,256]{3,2,1,0:T(8,128)S(1)} copy-done((f32[1,16,16,256]{3,2,1,0:T(8,128)S(1)}, f32[1,16,16,256]{3,2,1,0:T(8,128)}, u32[]{:S(2)}) %copy-start) | copy-done | bytes 262168
  1.0 0.0 copy-start.1
  1.0 0.9 %copy-done.1 = f32[16,16,256]{2,1,0:T(8,128)S(1)} copy-done((f32[16,16,256]{2,1,0:T(8,128)S(1)}, f32[16,16,256]{2,1,0:T(8,128)}, u32[]{:S(2)}) %copy-start.1) | copy-done | bytes 262168
  1.9 0.0 copy-start.2
  1.9 0.9 %copy-done.2 = f32[16,16,256]{2,1,0:T(8,128)S(1)} copy-done((f32[16,16,256]{2,1,0:T(8,128)S(1)}, f32[16,16,256]{2,1,0:T(8,128)}, u32[]{:S(2)}) %copy-start.2) | copy-done | bytes 262168
  2.9 0.3 shard_map.73
  3.2 3.8 %collective-permute-start = (f32[3,16,128]{2,1,0:T(8,128)S(1)}, f32[3,16,128]{2,1,0:T(8,128)S(1)}, u32[]{:S(2)}, u32[]{:S(2)}) collective-permute-start(f32[3,16,128]{2,1,0:T(8,128)S(1)} %get-tuple-element.18), channel_id=1, source_target_pairs={{0,8},{8,16},{16,24},{1,9},{9,17},{17,25},{2,10},{10,18},{18,26},{... | collective-permute-start | bytes 73736 | tf_op jit(solution)/shard_map/ppermute | solution.py:241
  7.0 2.0 %collective-permute-start.1 = (f32[3,16,128]{2,1,0:T(8,128)S(1)}, f32[3,16,128]{2,1,0:T(8,128)S(1)}, u32[]{:S(2)}, u32[]{:S(2)}) collective-permute-start(f32[3,16,128]{2,1,0:T(8,128)S(1)} %get-tuple-element.19), channel_id=1, source_target_pairs={{8,0},{16,8},{24,16},{9,1},{17,9},{25,17},{10,2},{18,10},{26,18},{... | collective-permute-start | bytes 73736 | tf_op jit(solution)/shard_map/ppermute | solution.py:241
  9.1 0.0 collective-permute-done
  9.1 3.7 %collective-permute-done.1 = f32[3,16,128]{2,1,0:T(8,128)S(1)} collective-permute-done((f32[3,16,128]{2,1,0:T(8,128)S(1)}, f32[3,16,128]{2,1,0:T(8,128)S(1)}, u32[]{:S(2)}, u32[]{:S(2)}) %collective-permute-start.1) | collective-permute-done | bytes 24608 | tf_op jit(solution)/shard_map/ppermute | solution.py:241
  12.8 0.0 copy-start.5
  12.8 0.0 copy-start.4
  12.8 3.1 %collective-permute-start.2 = (f32[27,16,256]{2,1,0:T(8,128)S(1)}, f32[27,16,256]{2,1,0:T(8,128)S(1)}, u32[]{:S(2)}, u32[]{:S(2)}) collective-permute-start(f32[27,16,256]{2,1,0:T(8,128)S(1)} %get-tuple-element.29.hi_ref), channel_id=1, source_target_pairs={{0,32},{32,64},{64,96},{96,128},{128,160},{160,192},{192,224},{224... | collective-permute-start | bytes 1327112 | tf_op jit(solution)/shard_map/ppermute | solution.py:241
  15.8 2.8 %collective-permute-start.3 = (f32[27,16,256]{2,1,0:T(8,128)S(1)}, f32[27,16,256]{2,1,0:T(8,128)S(1)}, u32[]{:S(2)}, u32[]{:S(2)}) collective-permute-start(f32[27,16,256]{2,1,0:T(8,128)S(1)} %get-tuple-element.30.lo_ref), channel_id=1, source_target_pairs={{32,0},{64,32},{96,64},{128,96},{160,128},{192,160},{224,192},{256... | collective-permute-start | bytes 1327112 | tf_op jit(solution)/shard_map/ppermute | solution.py:241
  18.6 0.0 copy-start.6
  18.7 0.1 stack.15.idx_ref
  18.7 0.0 copy-done.5
  18.7 0.0 copy-done.4
  18.7 0.6 copy-done.6
  19.3 0.0 copy-start.3
  19.3 4.4 %shard_map.74 = (f32[32,16,256]{2,1,0:T(8,128)S(1)}, f32[32,16,256]{2,1,0:T(8,128)S(1)}, f32[16,16,256]{2,1,0:T(8,128)S(1)}, f32[16,16,256]{2,1,0:T(8,128)S(1)},...) custom-call(s32[5]{0:T(128)S(1)} %stack.15.idx_ref, f32[8,128]{1,0:T(8,128)S(1)} %copy-done.6, ...), custom_call_target="tpu_custom_call" | custom-call | flops 67108864 | bytes 1048576 | tf_op jit(solution)/shard_map/pallas_call | solution.py:20
  23.7 1.6 %collective-permute-done.2.west_ref = f32[27,16,256]{2,1,0:T(8,128)S(1)} collective-permute-done((f32[27,16,256]{2,1,0:T(8,128)S(1)}, f32[27,16,256]{2,1,0:T(8,128)S(1)}, u32[]{:S(2)}, u32[]{:S(2)}) %collective-permute-start.2) | collective-permute-done | bytes 442400 | tf_op jit(solution)/shard_map/ppermute | solution.py:241
  25.3 4.9 %collective-permute-done.3.east_ref = f32[27,16,256]{2,1,0:T(8,128)S(1)} collective-permute-done((f32[27,16,256]{2,1,0:T(8,128)S(1)}, f32[27,16,256]{2,1,0:T(8,128)S(1)}, u32[]{:S(2)}, u32[]{:S(2)}) %collective-permute-start.3) | collective-permute-done | bytes 442400 | tf_op jit(solution)/shard_map/ppermute | solution.py:241
  30.2 0.0 copy-done.3
  30.2 11.7 %shard_map.75 = (f32[16,16,256]{2,1,0:T(8,128)S(1)}, f32[8,16,256]{2,1,0:T(8,128)S(1)}) custom-call(s32[5]{0:T(128)S(1)} %stack.15.idx_ref, f32[27,16,256]{2,1,0:T(8,128)S(1)} %get-tuple-element.30.lo_ref, f32[27,16,256]{2,1,0:T(8,128)S(1)} %get-tuple-element.29.hi_ref, f32[27,16,256]{2,1,0:T(8,128)S(1)} %collective-permute-done.2.west_ref, ...), custom_call_target="tpu_custom_call" | custom-call | flops 16777216 | bytes 1048576 | tf_op jit(solution)/shard_map/pallas_call | solution.py:20
  41.9 30.1 %all_to_all.5.got_ref = f32[8,16,256]{2,1,0:T(8,128)S(1)} all-to-all(f32[8,16,256]{2,1,0:T(8,128)S(1)} %get-tuple-element.28), channel_id=1, replica_groups=mesh['gx'=16,'gy'=4,'gz'=8] {'gz'}, dimensions={0} | all-to-all | bytes 262144 | tf_op jit(solution)/shard_map/all_to_all | solution.py:276
  72.0 1.3 %shard_map.76 = f32[16,16,256]{2,1,0:T(8,128)} custom-call(s32[5]{0:T(128)S(1)} %stack.15.idx_ref, f32[16,16,256]{2,1,0:T(8,128)S(1)} %get-tuple-element.24.u_ref, f32[16,16,256]{2,1,0:T(8,128)S(1)} %get-tuple-element.25.a_ref, f32[16,16,256]{2,1,0:T(8,128)S(1)} %get-tuple-element.26.b_ref, f32[8,16,256]{2,1,0:T(8,128)S(1)} %get-tuple-element.27.w_ref, ...), custom_call_target="tpu_custom_call" | custom-call | flops 1048576 | bytes 1048576 | tf_op jit(solution)/shard_map/pallas_call | solution.py:20
  (3 shorter events, 0.0 us)
Async XLA Ops:
  0.0 0.9 %copy-start = (f32[1,16,16,256]{3,2,1,0:T(8,128)S(1)}, f32[1,16,16,256]{3,2,1,0:T(8,128)}, u32[]{:S(2)}) copy-start(f32[1,16,16,256]{3,2,1,0:T(8,128)} %param.7) | copy-start | bytes 786436
  1.0 0.9 %copy-start.1 = (f32[16,16,256]{2,1,0:T(8,128)S(1)}, f32[16,16,256]{2,1,0:T(8,128)}, u32[]{:S(2)}) copy-start(f32[16,16,256]{2,1,0:T(8,128)} %wx_ref.1) | copy-start | bytes 786436
  1.9 0.9 %copy-start.2 = (f32[16,16,256]{2,1,0:T(8,128)S(1)}, f32[16,16,256]{2,1,0:T(8,128)}, u32[]{:S(2)}) copy-start(f32[16,16,256]{2,1,0:T(8,128)} %wy_ref.1) | copy-start | bytes 786436
  3.2 5.9 %collective-permute-start = (f32[3,16,128]{2,1,0:T(8,128)S(1)}, f32[3,16,128]{2,1,0:T(8,128)S(1)}, u32[]{:S(2)}, u32[]{:S(2)}) collective-permute-start(f32[3,16,128]{2,1,0:T(8,128)S(1)} %get-tuple-element.18), channel_id=1, source_target_pairs={{0,8},{8,16},{16,24},{1,9},{9,17},{17,25},{2,10},{10,18},{18,26},{... | collective-permute-start | bytes 73736 | tf_op jit(solution)/shard_map/ppermute | solution.py:241
  7.0 5.7 %collective-permute-start.1 = (f32[3,16,128]{2,1,0:T(8,128)S(1)}, f32[3,16,128]{2,1,0:T(8,128)S(1)}, u32[]{:S(2)}, u32[]{:S(2)}) collective-permute-start(f32[3,16,128]{2,1,0:T(8,128)S(1)} %get-tuple-element.19), channel_id=1, source_target_pairs={{8,0},{16,8},{24,16},{9,1},{17,9},{25,17},{10,2},{18,10},{26,18},{... | collective-permute-start | bytes 73736 | tf_op jit(solution)/shard_map/ppermute | solution.py:241
  12.8 6.0 %copy-start.5 = (s32[16,256]{1,0:T(8,128)S(1)}, s32[16,256]{1,0:T(8,128)}, u32[]{:S(2)}) copy-start(s32[16,256]{1,0:T(8,128)} %heights_ref.1) | copy-start | bytes 49156
  12.8 6.0 %copy-start.4 = (s32[16,256]{1,0:T(8,128)S(1)}, s32[16,256]{1,0:T(8,128)}, u32[]{:S(2)}) copy-start(s32[16,256]{1,0:T(8,128)} %classes_ref.1) | copy-start | bytes 49156
  12.8 12.6 %collective-permute-start.2 = (f32[27,16,256]{2,1,0:T(8,128)S(1)}, f32[27,16,256]{2,1,0:T(8,128)S(1)}, u32[]{:S(2)}, u32[]{:S(2)}) collective-permute-start(f32[27,16,256]{2,1,0:T(8,128)S(1)} %get-tuple-element.29.hi_ref), channel_id=1, source_target_pairs={{0,32},{32,64},{64,96},{96,128},{128,160},{160,192},{192,224},{224... | collective-permute-start | bytes 1327112 | tf_op jit(solution)/shard_map/ppermute | solution.py:241
  15.8 14.4 %collective-permute-start.3 = (f32[27,16,256]{2,1,0:T(8,128)S(1)}, f32[27,16,256]{2,1,0:T(8,128)S(1)}, u32[]{:S(2)}, u32[]{:S(2)}) collective-permute-start(f32[27,16,256]{2,1,0:T(8,128)S(1)} %get-tuple-element.30.lo_ref), channel_id=1, source_target_pairs={{32,0},{64,32},{96,64},{128,96},{160,128},{192,160},{224,192},{256... | collective-permute-start | bytes 1327112 | tf_op jit(solution)/shard_map/ppermute | solution.py:241
  18.6 0.7 copy-start.6
  19.3 10.9 %copy-start.3 = (f32[1,16,256]{2,1,0:T(8,128)S(1)}, f32[1,16,256]{2,1,0:T(8,128)}, u32[]{:S(2)}) copy-start(f32[1,16,256]{2,1,0:T(8,128)} %param.13) | copy-start | bytes 49156

commit v2 on v1

v2 whole, which is shorter than its diff:
```python
import jax
import jax.numpy as jnp
from jax import lax
from jax.experimental import pallas as pl
from jax.experimental.pallas import tpu as pltpu
from jax.sharding import PartitionSpec as P

HSTEPS = 8
NCLASS = 8
TILE = 128
DIFFUSION = 0.05
CANOPY = 0.2
LIMIT = 10 * 1024 * 1024
PARTS = 4

VMEM = pl.BlockSpec(memory_space=pltpu.VMEM)
SMEM = pl.BlockSpec(memory_space=pltpu.SMEM)
HBM = pl.BlockSpec(memory_space=pltpu.HBM)


def call(kernel, ins, outs, scratch, flops, out_spec=VMEM):
    return pl.pallas_call(
        kernel,
        out_shape=[jax.ShapeDtypeStruct(s, jnp.float32) for s in outs],
        in_specs=ins,
        out_specs=[out_spec] * len(outs),
        scratch_shapes=[pltpu.VMEM(s, jnp.float32) if isinstance(s, tuple) else s for s in scratch],
        compiler_params=pltpu.CompilerParams(vmem_limit_bytes=LIMIT),
        cost_estimate=pl.CostEstimate(flops=flops, bytes_accessed=1 << 20, transcendentals=0),
    )


def pack_kernel(c_hbm, wx_hbm, wy_hbm, own_ref, yl_ref, yr_ref, in_ref, sems):
    depth, rows, width = c_hbm.shape
    half, strip, part = rows // 2, HSTEPS, depth // PARTS
    copies = []
    for a, ref in enumerate((c_hbm, wx_hbm, wy_hbm)):
        for q in range(PARTS):
            at = pl.ds(q * part, part)
            copies.append(pltpu.make_async_copy(ref.at[at], in_ref.at[a, at], sems.at[a * PARTS + q]))
            copies[-1].start()
    lane = lax.broadcasted_iota(jnp.int32, (depth, TILE), 1) // strip
    for a in range(3):
        for q in range(PARTS):
            copies[a * PARTS + q].wait()
        left = jnp.zeros((depth, TILE), jnp.float32)
        right = left
        for x in range(rows):
            row = in_ref[a, :, x, :]
            own_ref[a, x] = row
            first, last = row[:, :TILE], row[:, width - TILE :]
            group = 2 * (x % half)
            to_left, to_right = group + 1 - x // half, group + x // half
            if to_left:
                first = pltpu.roll(first, strip * to_left, 1)
            if (to_right + 1) * strip % TILE:
                last = pltpu.roll(last, (to_right + 1) * strip % TILE, 1)
            left = jnp.where(lane == to_left, first, left)
            right = jnp.where(lane == to_right, last, right)
        yl_ref[a] = left
        yr_ref[a] = right


def send_kernel(own_ref, south_ref, north_ref, lo_ref, hi_ref, side_lo_ref, side_hi_ref):
    _, rows, depth, width = own_ref.shape
    half = rows // 2
    to_lo, to_hi = 0, 0
    for a in range(3):
        for x in range(rows):
            first, last = own_ref[a, x, :, :TILE], own_ref[a, x, :, TILE:]
            if x < half and not (a > 0 and x == half - 1):
                lo_ref[to_lo], lo_ref[to_lo + 1] = first, last
                to_lo += 2
            if x >= half and not (a == 2 and x == half):
                hi_ref[to_hi], hi_ref[to_hi + 1] = first, last
                to_hi += 2
    even = lax.broadcasted_iota(jnp.int32, (depth, TILE), 1) // HSTEPS % 2 == 0
    for a in range(3):
        south, north = south_ref[a], north_ref[a]
        low = jnp.where(even, south, north)
        high = jnp.where(even, pltpu.roll(south, TILE - HSTEPS, 1), pltpu.roll(north, HSTEPS, 1))
        side_lo_ref[a] = low
        side_hi_ref[a] = high
        lo_ref[to_lo + a] = low
        hi_ref[to_hi + a] = high


def table_kernel(profiles_ref, classes_ref, heights_ref, k_ref):
    total = k_ref.shape[0] - 1
    classes, heights = classes_ref[...], heights_ref[...]
    bits = [(classes & (1 << b)) != 0 for b in range(3)]
    k_ref[0] = jnp.zeros(classes.shape, jnp.float32)

    def mixing(z, _):
        table = [profiles_ref[c, z] for c in range(NCLASS)]
        for bit in bits:
            table = [jnp.where(bit, table[i + 1], table[i]) for i in range(0, len(table), 2)]
        k = table[0]
        k_ref[z + 1] = jnp.where(z < heights, CANOPY * k, k)
        return 0

    lax.fori_loop(0, total, mixing, 0, unroll=4)


def factor_kernel(idx_ref, k_ref, f_ref, h_ref, g_ref, a_ref, b_ref, w_ref,
                  e_ref, d_ref, up_ref, down_ref):
    me = idx_ref[2]
    depth = g_ref.shape[0]
    groups = w_ref.shape[0]
    shape = w_ref.shape[1:]
    total = depth * groups
    one = jnp.ones(shape, jnp.float32)

    def chunk(n, carry):
        e, d = carry
        m = groups - 1 - n
        aside_e = jnp.where(n == me, 0, depth)
        aside_d = jnp.where(m == me, 0, depth)

        def level(i, carry):
            e, d, up, down = carry
            k = k_ref[n * depth + i + 1]
            f = k / (e + k)
            f_ref[aside_e + i] = f
            e_ref[aside_e + i] = e
            j = depth - 1 - i
            kb = k_ref[m * depth + j]
            h = kb / (d + kb)
            h_ref[aside_d + j] = h
            d_ref[aside_d + j] = d
            return 1.0 + f * e, 1.0 + h * d, up * f, down * h

        e, d, up, down = lax.fori_loop(0, depth, level, (e, d, one, one))
        up_ref[n] = up
        down_ref[m] = down
        return e, d

    lax.fori_loop(0, groups, chunk, (one, 1.0 + k_ref[total]))

    run = one
    for i in range(depth):
        g = 1.0 / (e_ref[i] + d_ref[i] - 1.0)
        g_ref[i] = g
        a_ref[i] = g * run
        run = run * f_ref[i]
    run = one
    for i in reversed(range(depth)):
        b_ref[i] = g_ref[i] * run
        run = run * h_ref[i]
    zero = jnp.zeros(shape, jnp.float32)
    run = one
    for s in reversed(range(groups)):
        below = s < me
        w_ref[s] = jnp.where(below, run, zero)
        run = jnp.where(below, run * up_ref[s], one)
    run = one
    for s in range(groups):
        above = s > me
        w_ref[s] = w_ref[s] + jnp.where(above, run, zero)
        run = jnp.where(above, run * down_ref[s], one)


def coefficients(ax, aw, ay, mask):
    south = pltpu.roll(ay, 1, 1)
    ax_up, ay_up, as_up = jnp.maximum(ax, 0.0), jnp.maximum(ay, 0.0), jnp.maximum(south, 0.0)
    ax_down, ay_down, as_down = jnp.minimum(ax, 0.0), jnp.minimum(ay, 0.0), jnp.minimum(south, 0.0)
    own = (1.0 - 4.0 * DIFFUSION) - ax_up - (ay_up - as_down)
    west = DIFFUSION
    if aw is not None:
        own = own + jnp.minimum(aw, 0.0)
        west = west + jnp.maximum(aw, 0.0)
    return own * mask, (DIFFUSION - ax_down) * mask, west * mask, (DIFFUSION - ay_down) * mask, (DIFFUSION + as_up) * mask


def substep(k_ref, r, own, east, west):
    north = pltpu.roll(own, own.shape[1] - 1, 1)
    south = pltpu.roll(own, 1, 1)
    return (k_ref[0, r] * own + k_ref[1, r] * east) + (k_ref[2, r] * west + k_ref[3, r] * north) + k_ref[4, r] * south


def with_strips(first, last, side, row):
    by = (TILE - HSTEPS - 2 * HSTEPS * row) % TILE
    return jnp.concatenate([first, last, pltpu.roll(side, by, 1) if by else side], axis=1)


def inside_mask(depth, width, gy, n_gy):
    lane = lax.broadcasted_iota(jnp.int32, (depth, TILE), 1)
    sides = jnp.where((lane < HSTEPS) & (gy < n_gy - 1) | (lane >= TILE - HSTEPS) & (gy > 0), 1.0, 0.0)
    return jnp.concatenate([jnp.ones((depth, width), jnp.float32), sides], axis=1)


def inner_kernel(idx_ref, own_ref, side_lo_ref, side_hi_ref, k_ref, edge_ref, wind_ref, c_ref):
    gy, n_gy = idx_ref[1], idx_ref[4]
    _, rows, depth, width = own_ref.shape
    half = rows // 2
    mask = inside_mask(depth, width, gy, n_gy)

    def plane(a, x):
        side = side_lo_ref[a] if x < half else side_hi_ref[a]
        return with_strips(own_ref[a, x, :, :TILE], own_ref[a, x, :, TILE:], side, x % half)

    aw = None
    for x in range(rows):
        c_ref[0, x] = plane(0, x)
        ax = plane(1, x)
        for i, k in enumerate(coefficients(ax, aw, plane(2, x), mask)):
            k_ref[i, x] = k
        aw = ax
    wind_ref[...] = aw
    for step in range(HSTEPS):
        src = step % 2
        for i, x in enumerate((step, step + 1, rows - 2 - step, rows - 1 - step)):
            edge_ref[step, i] = c_ref[src, x]
        for x in range(step + 1, rows - 1 - step):
            c_ref[1 - src, x] = substep(k_ref, x, c_ref[src, x], c_ref[src, x + 1], c_ref[src, x - 1])


def outer_kernel(idx_ref, west_ref, east_ref, inner_ref, edge_ref, wind_ref, f_ref, h_ref, g_ref, emission_ref,
                 u_ref, send_ref, c_ref, k_ref, t_ref):
    gx, gy, me = idx_ref[0], idx_ref[1], idx_ref[2]
    n_gx, n_gy = idx_ref[3], idx_ref[4]
    depth, rows, width = u_ref.shape
    groups = send_ref.shape[0]
    half, strip = rows // 2, HSTEPS
    ext = rows + 2 * strip
    inside = inside_mask(depth, width, gy, n_gy)
    west_in = inside * jnp.where(gx > 0, 1.0, 0.0)
    east_in = inside * jnp.where(gx < n_gx - 1, 1.0, 0.0)

    def west_plane(a, r):
        at = 2 * (half * a + r - (a == 2))
        return with_strips(west_ref[at], west_ref[at + 1], west_ref[6 * half - 2 + a], r)

    def east_plane(a, r):
        at = 2 * (half * a + r - (a == 2))
        return with_strips(east_ref[at], east_ref[at + 1], east_ref[6 * half - 4 + a], r)

    aw = west_plane(1, 0)
    c_ref[0, 0] = west_plane(0, 0)
    for r in range(1, strip):
        c_ref[0, r] = west_plane(0, r)
        ax = west_plane(1, r)
        for i, k in enumerate(coefficients(ax, aw, west_plane(2, r), west_in)):
            k_ref[i, r] = k
        aw = ax
    for i in range(5):
        k = inner_ref[i, 0]
        if i == 0:
            k = k + jnp.minimum(aw, 0.0) * inside
        if i == 2:
            k = k + jnp.maximum(aw, 0.0) * inside
        k_ref[i, strip] = k
    aw = wind_ref[...]
    for r in range(strip - 1):
        c_ref[0, strip + rows + r] = east_plane(0, r)
        ax = east_plane(1, r)
        for i, k in enumerate(coefficients(ax, aw, east_plane(2, r), east_in)):
            k_ref[i, strip + rows + r] = k
        aw = ax
    c_ref[0, ext - 1] = east_plane(0, strip - 1)

    for step in range(1, strip + 1):
        src = (step - 1) % 2
        for i in range(strip):
            for r, side in ((step + i, 0), (ext - 1 - step - i, 1)):
                low_side = side == 0
                def at(q):
                    if low_side and q >= strip - 1 + step:
                        return edge_ref[step - 1, q - (strip - 1 + step)]
                    if not low_side and q <= strip + rows - step:
                        return edge_ref[step - 1, q - (strip + rows - step) + 3]
                    return c_ref[src, q]
                weights = k_ref if r <= strip or r >= strip + rows else inner_ref
                row = r if weights is k_ref else r - strip
                new = substep(weights, row, at(r), at(r + 1), at(r - 1))
                if step < strip:
                    c_ref[1 - src, r] = new
                else:
                    c_ref[1 - src, r, :, :width] = new[:, :width]
    last = strip % 2

    def level(z):
        d = c_ref[last, strip : strip + rows, z, :width]
        if z == 0:
            d = d + emission_ref[...] * jnp.where(me == 0, 1.0, 0.0)
        return d

    run = None
    for z in range(depth):
        d = level(z)
        run = d if z == 0 else d + f_ref[z - 1] * run
        t_ref[z] = run - d
    beta = f_ref[depth - 1] * run
    run = None
    for z in reversed(range(depth)):
        d = level(z)
        run = d if z == depth - 1 else d + h_ref[z + 1] * run
        u_ref[z] = g_ref[z] * (t_ref[z] + run)
    gamma = h_ref[0] * run
    for s in range(groups):
        send_ref[s] = jnp.where(s > me, beta, gamma)


def finish_kernel(idx_ref, u_ref, a_ref, b_ref, w_ref, got_ref, out_hbm, out_ref, sems):
    me = idx_ref[2]
    depth, rows, width = u_ref.shape
    groups = w_ref.shape[0]
    part = depth // PARTS
    zero = jnp.zeros((rows, width), jnp.float32)
    below, above = zero, zero
    for s in range(groups):
        term = w_ref[s] * got_ref[s]
        below = below + jnp.where(s < me, term, zero)
        above = above + jnp.where(s > me, term, zero)
    copies = []
    for q in range(PARTS):
        for z in range(q * part, (q + 1) * part):
            out_ref[z] = u_ref[z] + (a_ref[z] * below + b_ref[z] * above)
        at = pl.ds(q * part, part)
        copies.append(pltpu.make_async_copy(out_ref.at[at], out_hbm.at[at], sems.at[q]))
        copies[-1].start()
    for copy in copies:
        copy.wait()


def shifted(x, axis, by):
    length = lax.axis_size(axis)
    return lax.ppermute(x, axis, [(i, i + by) for i in range(length) if 0 <= i + by < length])


def local(conc, wind_x, wind_y, profiles, classes, heights, emission):
    species, depth, rows, width = conc.shape
    groups = lax.axis_size("gz")
    half, ext, wide = rows // 2, rows + 2 * HSTEPS, width + TILE
    idx = jnp.stack(
        [lax.axis_index("gx"), lax.axis_index("gy"), lax.axis_index("gz"),
         jnp.int32(lax.axis_size("gx")), jnp.int32(lax.axis_size("gy"))]
    ).astype(jnp.int32)
    block, pane, tile, row = (depth, rows, width), (rows, width), (depth, TILE), (depth, wide)
    n_lo, n_hi = 6 * half - 4, 6 * half - 2

    own, left, right = call(
        pack_kernel, [HBM] * 3, [(3, rows, depth, width), (3, *tile), (3, *tile)],
        [(3, *block), pltpu.SemaphoreType.DMA((3 * PARTS,))], 1 << 20,
    )(*(pltpu.with_memory_space_constraint(x, pltpu.HBM) for x in (conc[0], wind_x, wind_y)))
    south = shifted(right, "gy", 1)
    north = shifted(left, "gy", -1)
    (k,) = call(table_kernel, [SMEM, VMEM, VMEM], [(depth * groups + 1, *pane)], [], 1 << 24)(
        profiles, classes, heights
    )
    own, south, north, k = lax.optimization_barrier((own, south, north, k))
    lo, hi, side_lo, side_hi = call(
        send_kernel, [VMEM] * 3, [(n_lo + 3, *tile), (n_hi + 3, *tile), (3, *tile), (3, *tile)], [], 1 << 20
    )(own, south, north)
    west = shifted(hi, "gx", 1)
    east = shifted(lo, "gx", -1)
    weights, edge, wind = call(
        inner_kernel, [SMEM] + [VMEM] * 3,
        [(5, rows, *row), (HSTEPS, 4, *row), row], [(2, rows, *row)], 1 << 24,
    )(idx, own, side_lo, side_hi)
    twice = (2 * depth, rows, width)
    f, h, g, a, b, w = call(
        factor_kernel, [SMEM, VMEM], [twice, twice, block, block, block, (groups, *pane)],
        [twice, twice, (groups, *pane), (groups, *pane)], 1 << 24,
    )(idx, k)
    u, send = call(
        outer_kernel, [SMEM] + [VMEM] * 9, [block, (groups, *pane)],
        [(2, ext, *row), (5, ext, *row), block], 1 << 24,
    )(idx, west, east, weights, edge, wind, f, h, g, emission[0])
    got = lax.all_to_all(send, "gz", split_axis=0, concat_axis=0, tiled=True)
    (out,) = call(
        finish_kernel, [SMEM] + [VMEM] * 5, [block], [block, pltpu.SemaphoreType.DMA((PARTS,))], 1 << 20, HBM
    )(idx, u, a, b, w, got)
    return out[None]


def solution(mesh):
    return jax.shard_map(
        local,
        mesh=mesh,
        in_specs=(
            P(None, "gz", "gx", "gy"),
            P("gz", "gx", "gy"),
            P("gz", "gx", "gy"),
            P(),
            P("gx", "gy"),
            P("gx", "gy"),
            P(None, "gx", "gy"),
        ),
        out_specs=P(None, "gz", "gx", "gy"),
        check_vma=False,
    )
```

time: 73.7 us -> 66.2 us (0.90)
  the two profiles are of different devices: /device:TPU:58 before, /device:TPU:24 now
where the time goes in v2:
time: 66.2 us; the launch traced here: 65.8 us
  blocking collectives  31.5 us (48%)
  Pallas kernels  14.7 us (22%)
  starting transfers between devices  10.9 us (16%)
  waiting for transfers between devices  6.26 us (9%)
  local copies, waits for them, and re-layouts  2.21 us (3%)
    all_to_all x1, blocking collectives, local(): got = lax.all_to_all(send, 'gz', split_axis=0, concat_axis=0, tiled=True)  31.5 us
    ppermute x4, starting transfers between devices, shifted(): lax.ppermute(x, axis, [(i, i + by) for i in range(length) if 0 <= i + by...  10.9 us
    ppermute x4, waiting for transfers between devices, shifted(): lax.ppermute(x, axis, [(i, i + by) for i in range(length) if 0 <= i + by...  6.26 us
    pallas_call x1, Pallas kernels, local(): call(outer_kernel, [SMEM] + [VMEM] * 9, [block, (groups, *pane)], [(2, ex...  3.88 us
    pallas_call x1, Pallas kernels, local(): call(factor_kernel, [SMEM, VMEM], [twice, twice, block, block, block, (gr...  2.85 us
    pallas_call x1, Pallas kernels, local(): call(inner_kernel, [SMEM] + [VMEM] * 3, [(5, rows, *row), (HSTEPS, 4, *ro...  2.45 us
    unnamed x8, local copies, waits for them, and re-layouts  2.12 us
    pallas_call x1, Pallas kernels, local(): call(table_kernel, [SMEM, VMEM, VMEM], [(depth * groups + 1, *pane)], [],...  1.77 us
  transfers between devices with their start and end apart: 4, of which 2 were waited for; matrix products, arithmetic and copies ran while one was open for 0% of the time, Pallas kernels for 11%

profile of v2, /device:TPU:24, one launch (start us, length us, event | category | flops | bytes accessed | tf_op | source)
XLA Modules:
  0.0 65.8 jit_solution(18300401104869291719)
XLA Ops:
  0.0 1.5 %shard_map.73 = (f32[3,16,16,256]{3,2,1,0:T(8,128)S(1)}, f32[3,16,128]{2,1,0:T(8,128)S(1)}, f32[3,16,128]{2,1,0:T(8,128)S(1)}) custom-call(f32[16,16,256]{2,1,0:T(8,128)} %bitcast.7, f32[16,16,256]{2,1,0:T(8,128)} %wx_hbm.1, f32[16,16,256]{2,1,0:T(8,128)} %wy_hbm.1), custom_call_target="tpu_custom_call" | custom-call | flops 1048576 | bytes 1048576 | tf_op jit(solution)/shard_map/pallas_call | solution.py:342
  1.5 3.8 %collective-permute-start = (f32[3,16,128]{2,1,0:T(8,128)S(1)}, f32[3,16,128]{2,1,0:T(8,128)S(1)}, u32[]{:S(2)}, u32[]{:S(2)}) collective-permute-start(f32[3,16,128]{2,1,0:T(8,128)S(1)} %get-tuple-element.28), channel_id=1, source_target_pairs={{0,8},{8,16},{16,24},{1,9},{9,17},{17,25},{2,10},{10,18},{18,26},{... | collective-permute-start | bytes 73736 | tf_op jit(solution)/shard_map/ppermute | solution.py:328
  5.4 1.3 %collective-permute-start.1 = (f32[3,16,128]{2,1,0:T(8,128)S(1)}, f32[3,16,128]{2,1,0:T(8,128)S(1)}, u32[]{:S(2)}, u32[]{:S(2)}) collective-permute-start(f32[3,16,128]{2,1,0:T(8,128)S(1)} %get-tuple-element.29), channel_id=1, source_target_pairs={{8,0},{16,8},{24,16},{9,1},{17,9},{25,17},{10,2},{18,10},{26,18},{... | collective-permute-start | bytes 73736 | tf_op jit(solution)/shard_map/ppermute | solution.py:328
  6.7 0.0 copy-start
  6.7 0.7 %copy-done = s32[16,256]{1,0:T(8,128)S(1)} copy-done((s32[16,256]{1,0:T(8,128)S(1)}, s32[16,256]{1,0:T(8,128)}, u32[]{:S(2)}) %copy-start) | copy-done | bytes 16408
  7.4 0.0 copy-start.1
  7.4 0.7 %copy-done.1 = s32[16,256]{1,0:T(8,128)S(1)} copy-done((s32[16,256]{1,0:T(8,128)S(1)}, s32[16,256]{1,0:T(8,128)}, u32[]{:S(2)}) %copy-start.1) | copy-done | bytes 16408
  8.1 0.0 copy-start.3
  8.1 0.7 %copy-done.3 = f32[8,128]{1,0:T(8,128)S(1)} copy-done((f32[8,128]{1,0:T(8,128)S(1)}, f32[8,128]{1,0:T(8,128)}, u32[]{:S(2)}) %copy-start.3) | copy-done | bytes 4120
  8.8 1.8 %shard_map.74.k_ref = f32[129,16,256]{2,1,0:T(8,128)S(1)} custom-call(f32[8,128]{1,0:T(8,128)S(1)} %copy-done.3, s32[16,256]{1,0:T(8,128)S(1)} %copy-done, s32[16,256]{1,0:T(8,128)S(1)} %copy-done.1), custom_call_target="tpu_custom_call" | custom-call | flops 16777216 | bytes 1048576 | tf_op jit(solution)/shard_map/pallas_call | solution.py:348
  10.6 0.0 copy-start.2
  10.6 0.0 collective-permute-done.south_ref
  10.6 0.5 collective-permute-done.1.north_ref
  11.1 0.9 %shard_map.75 = (f32[47,16,128]{2,1,0:T(8,128)}, f32[49,16,128]{2,1,0:T(8,128)}, f32[3,16,128]{2,1,0:T(8,128)S(1)}, f32[3,16,128]{2,1,0:T(8,128)S(1)}) custom-call(f32[3,16,16,256]{3,2,1,0:T(8,128)S(1)} %get-tuple-element.30.own_ref, f32[3,16,128]{2,1,0:T(8,128)S(1)} %collective-permute-done.south_ref, f32[3,16,128]{2,1,0:T(8,128)S(1)} %collective-permute-done.1.north_ref), custom_call_target="tpu_custom_call" | custom-call | flops 1048576 | bytes 1048576 | tf_op jit(solution)/shard_map/pallas_call | solution.py:352
  12.0 3.0 %collective-permute-start.2 = (f32[49,16,128]{2,1,0:T(8,128)}, f32[49,16,128]{2,1,0:T(8,128)S(1)}, u32[]{:S(2)}, u32[]{:S(2)}) collective-permute-start(f32[49,16,128]{2,1,0:T(8,128)} %get-tuple-element.33), channel_id=1, source_target_pairs={{0,32},{32,64},{64,96},{96,128},{128,160},{160,192},{192,224},{224... | collective-permute-start | bytes 1204232 | tf_op jit(solution)/shard_map/ppermute | solution.py:328
  15.0 2.8 %collective-permute-start.3 = (f32[47,16,128]{2,1,0:T(8,128)}, f32[47,16,128]{2,1,0:T(8,128)}, u32[]{:S(2)}, u32[]{:S(2)}) collective-permute-start(f32[47,16,128]{2,1,0:T(8,128)} %get-tuple-element.34), channel_id=1, source_target_pairs={{32,0},{64,32},{96,64},{128,96},{160,128},{192,160},{224,192},{256... | collective-permute-start | bytes 1155080 | tf_op jit(solution)/shard_map/ppermute | solution.py:328
  17.8 0.1 stack.15.idx_ref
  17.9 2.9 %shard_map.77 = (f32[32,16,256]{2,1,0:T(8,128)S(1)}, f32[32,16,256]{2,1,0:T(8,128)S(1)}, f32[16,16,256]{2,1,0:T(8,128)S(1)}, f32[16,16,256]{2,1,0:T(8,128)S(1)},...) custom-call(s32[5]{0:T(128)S(1)} %stack.15.idx_ref, f32[129,16,256]{2,1,0:T(8,128)S(1)} %shard_map.74.k_ref), custom_call_target="tpu_custom_call" | custom-call | flops 16777216 | bytes 1048576 | tf_op jit(solution)/shard_map/pallas_call | solution.py:362
  20.8 2.4 %shard_map.76 = (f32[5,16,16,384]{3,2,1,0:T(8,128)S(1)}, f32[8,4,16,384]{3,2,1,0:T(8,128)S(1)}, f32[16,384]{1,0:T(8,128)S(1)}) custom-call(s32[5]{0:T(128)S(1)} %stack.15.idx_ref, f32[3,16,16,256]{3,2,1,0:T(8,128)S(1)} %get-tuple-element.30.own_ref, f32[3,16,128]{2,1,0:T(8,128)S(1)} %get-tuple-element.35.side_lo_ref, ...), custom_call_target="tpu_custom_call" | custom-call | flops 16777216 | bytes 1048576 | tf_op jit(solution)/shard_map/pallas_call | solution.py:357
  23.2 5.8 %collective-permute-done.3.east_ref = f32[47,16,128]{2,1,0:T(8,128)} collective-permute-done((f32[47,16,128]{2,1,0:T(8,128)}, f32[47,16,128]{2,1,0:T(8,128)}, u32[]{:S(2)}, u32[]{:S(2)}) %collective-permute-start.3) | collective-permute-done | bytes 385056 | tf_op jit(solution)/shard_map/ppermute | solution.py:328
  29.0 0.0 collective-permute-done.2.west_ref
  29.0 0.0 copy-done.2
  29.0 3.9 %shard_map.78 = (f32[16,16,256]{2,1,0:T(8,128)S(1)}, f32[8,16,256]{2,1,0:T(8,128)S(1)}) custom-call(s32[5]{0:T(128)S(1)} %stack.15.idx_ref, f32[49,16,128]{2,1,0:T(8,128)S(1)} %collective-permute-done.2.west_ref, f32[47,16,128]{2,1,0:T(8,128)} %collective-permute-done.3.east_ref, f32[5,16,16,384]{3,2,1,0:T(8,128)S(1)} %get-tuple-element.37.inner_ref, ...), custom_call_target="tpu_custom_call" | custom-call | flops 16777216 | bytes 1048576 | tf_op jit(solution)/shard_map/pallas_call | solution.py:366
  32.9 31.5 %all_to_all.5.got_ref = f32[8,16,256]{2,1,0:T(8,128)S(1)} all-to-all(f32[8,16,256]{2,1,0:T(8,128)S(1)} %get-tuple-element.48), channel_id=1, replica_groups=mesh['gx'=16,'gy'=4,'gz'=8] {'gz'}, dimensions={0} | all-to-all | bytes 262144 | tf_op jit(solution)/shard_map/all_to_all | solution.py:370
  64.4 1.3 %shard_map.79 = f32[16,16,256]{2,1,0:T(8,128)} custom-call(s32[5]{0:T(128)S(1)} %stack.15.idx_ref, f32[16,16,256]{2,1,0:T(8,128)S(1)} %get-tuple-element.44.u_ref, f32[16,16,256]{2,1,0:T(8,128)S(1)} %get-tuple-element.45.a_ref, f32[16,16,256]{2,1,0:T(8,128)S(1)} %get-tuple-element.46.b_ref, f32[8,16,256]{2,1,0:T(8,128)S(1)} %get-tuple-element.47.w_ref, ...), custom_call_target="tpu_custom_call" | custom-call | flops 1048576 | bytes 1048576 | tf_op jit(solution)/shard_map/pallas_call | solution.py:371
Async XLA Ops:
  1.5 9.0 %collective-permute-start = (f32[3,16,128]{2,1,0:T(8,128)S(1)}, f32[3,16,128]{2,1,0:T(8,128)S(1)}, u32[]{:S(2)}, u32[]{:S(2)}) collective-permute-start(f32[3,16,128]{2,1,0:T(8,128)S(1)} %get-tuple-element.28), channel_id=1, source_target_pairs={{0,8},{8,16},{16,24},{1,9},{9,17},{17,25},{2,10},{10,18},{18,26},{... | collective-permute-start | bytes 73736 | tf_op jit(solution)/shard_map/ppermute | solution.py:328
  5.4 5.7 %collective-permute-start.1 = (f32[3,16,128]{2,1,0:T(8,128)S(1)}, f32[3,16,128]{2,1,0:T(8,128)S(1)}, u32[]{:S(2)}, u32[]{:S(2)}) collective-permute-start(f32[3,16,128]{2,1,0:T(8,128)S(1)} %get-tuple-element.29), channel_id=1, source_target_pairs={{8,0},{16,8},{24,16},{9,1},{17,9},{25,17},{10,2},{18,10},{26,18},{... | collective-permute-start | bytes 73736 | tf_op jit(solution)/shard_map/ppermute | solution.py:328
  6.7 0.7 %copy-start = (s32[16,256]{1,0:T(8,128)S(1)}, s32[16,256]{1,0:T(8,128)}, u32[]{:S(2)}) copy-start(s32[16,256]{1,0:T(8,128)} %classes_ref.1) | copy-start | bytes 49156
  7.4 0.7 %copy-start.1 = (s32[16,256]{1,0:T(8,128)S(1)}, s32[16,256]{1,0:T(8,128)}, u32[]{:S(2)}) copy-start(s32[16,256]{1,0:T(8,128)} %heights_ref.1) | copy-start | bytes 49156
  8.1 0.7 %copy-start.3 = (f32[8,128]{1,0:T(8,128)S(1)}, f32[8,128]{1,0:T(8,128)}, u32[]{:S(2)}) copy-start(f32[8,128]{1,0:T(8,128)} %profiles_ref.1) | copy-start | bytes 12292
  10.6 18.5 %copy-start.2 = (f32[1,16,256]{2,1,0:T(8,128)S(1)}, f32[1,16,256]{2,1,0:T(8,128)}, u32[]{:S(2)}) copy-start(f32[1,16,256]{2,1,0:T(8,128)} %param.13) | copy-start | bytes 49156
  12.0 17.0 %collective-permute-start.2 = (f32[49,16,128]{2,1,0:T(8,128)}, f32[49,16,128]{2,1,0:T(8,128)S(1)}, u32[]{:S(2)}, u32[]{:S(2)}) collective-permute-start(f32[49,16,128]{2,1,0:T(8,128)} %get-tuple-element.33), channel_id=1, source_target_pairs={{0,32},{32,64},{64,96},{96,128},{128,160},{160,192},{192,224},{224... | collective-permute-start | bytes 1204232 | tf_op jit(solution)/shard_map/ppermute | solution.py:328
  15.0 14.0 %collective-permute-start.3 = (f32[47,16,128]{2,1,0:T(8,128)}, f32[47,16,128]{2,1,0:T(8,128)}, u32[]{:S(2)}, u32[]{:S(2)}) collective-permute-start(f32[47,16,128]{2,1,0:T(8,128)} %get-tuple-element.34), channel_id=1, source_target_pairs={{32,0},{64,32},{96,64},{128,96},{160,128},{192,160},{224,192},{256... | collective-permute-start | bytes 1155080 | tf_op jit(solution)/shard_map/ppermute | solution.py:328

commit v3 on v2

--- a/solution.py
+++ b/solution.py
@@ -1,3 +1,5 @@
+import functools
+
 import jax
 import jax.numpy as jnp
 from jax import lax
@@ -10,7 +12,7 @@
 TILE = 128
 DIFFUSION = 0.05
 CANOPY = 0.2
-LIMIT = 10 * 1024 * 1024
+LIMIT = 8 * 1024 * 1024
 PARTS = 4
 
 VMEM = pl.BlockSpec(memory_space=pltpu.VMEM)
@@ -21,7 +23,7 @@
 def call(kernel, ins, outs, scratch, flops, out_spec=VMEM):
     return pl.pallas_call(
         kernel,
-        out_shape=[jax.ShapeDtypeStruct(s, jnp.float32) for s in outs],
+        out_shape=[jax.ShapeDtypeStruct(s, jnp.float32) if isinstance(s, tuple) else s for s in outs],
         in_specs=ins,
         out_specs=[out_spec] * len(outs),
         scratch_shapes=[pltpu.VMEM(s, jnp.float32) if isinstance(s, tuple) else s for s in scratch],
@@ -30,7 +32,8 @@
     )
 
 
-def pack_kernel(c_hbm, wx_hbm, wy_hbm, own_ref, yl_ref, yr_ref, in_ref, sems):
+def pack_kernel(c_hbm, wx_hbm, wy_hbm, *refs):
+    small, (own_ref, yl_ref, yr_ref), kept, (in_ref, sems, small_sems) = refs[:4], refs[4:7], refs[7:11], refs[11:]
     depth, rows, width = c_hbm.shape
     half, strip, part = rows // 2, HSTEPS, depth // PARTS
     copies = []
@@ -39,6 +42,9 @@
             at = pl.ds(q * part, part)
             copies.append(pltpu.make_async_copy(ref.at[at], in_ref.at[a, at], sems.at[a * PARTS + q]))
             copies[-1].start()
+    others = [pltpu.make_async_copy(s, d, small_sems.at[i]) for i, (s, d) in enumerate(zip(small, kept))]
+    for copy in others:
+        copy.start()
     lane = lax.broadcasted_iota(jnp.int32, (depth, TILE), 1) // strip
     for a in range(3):
         for q in range(PARTS):
@@ -59,6 +65,8 @@
             right = jnp.where(lane == to_right, last, right)
         yl_ref[a] = left
         yr_ref[a] = right
+    for copy in others:
+        copy.wait()
 
 
 def send_kernel(own_ref, south_ref, north_ref, lo_ref, hi_ref, side_lo_ref, side_hi_ref):
@@ -67,13 +75,12 @@
     to_lo, to_hi = 0, 0
     for a in range(3):
         for x in range(rows):
-            first, last = own_ref[a, x, :, :TILE], own_ref[a, x, :, TILE:]
             if x < half and not (a > 0 and x == half - 1):
-                lo_ref[to_lo], lo_ref[to_lo + 1] = first, last
-                to_lo += 2
+                lo_ref[to_lo] = own_ref[a, x]
+                to_lo += 1
             if x >= half and not (a == 2 and x == half):
-                hi_ref[to_hi], hi_ref[to_hi + 1] = first, last
-                to_hi += 2
+                hi_ref[to_hi] = own_ref[a, x]
+                to_hi += 1
     even = lax.broadcasted_iota(jnp.int32, (depth, TILE), 1) // HSTEPS % 2 == 0
     for a in range(3):
         south, north = south_ref[a], north_ref[a]
@@ -81,8 +88,9 @@
         high = jnp.where(even, pltpu.roll(south, TILE - HSTEPS, 1), pltpu.roll(north, HSTEPS, 1))
         side_lo_ref[a] = low
         side_hi_ref[a] = high
-        lo_ref[to_lo + a] = low
-        hi_ref[to_hi + a] = high
+        lanes = pl.ds(a % 2 * TILE, TILE)
+        lo_ref[to_lo + a // 2, :, lanes] = low
+        hi_ref[to_hi + a // 2, :, lanes] = high
 
 
 def table_kernel(profiles_ref, classes_ref, heights_ref, k_ref):
@@ -178,9 +186,9 @@
     return (k_ref[0, r] * own + k_ref[1, r] * east) + (k_ref[2, r] * west + k_ref[3, r] * north) + k_ref[4, r] * south
 
 
-def with_strips(first, last, side, row):
+def with_strips(cells, side, row):
     by = (TILE - HSTEPS - 2 * HSTEPS * row) % TILE
-    return jnp.concatenate([first, last, pltpu.roll(side, by, 1) if by else side], axis=1)
+    return jnp.concatenate([cells, pltpu.roll(side, by, 1) if by else side], axis=1)
 
 
 def inside_mask(depth, width, gy, n_gy):
@@ -197,7 +205,7 @@
 
     def plane(a, x):
         side = side_lo_ref[a] if x < half else side_hi_ref[a]
-        return with_strips(own_ref[a, x, :, :TILE], own_ref[a, x, :, TILE:], side, x % half)
+        return with_strips(own_ref[a, x], side, x % half)
 
     aw = None
     for x in range(rows):
@@ -215,97 +223,95 @@
             c_ref[1 - src, x] = substep(k_ref, x, c_ref[src, x], c_ref[src, x + 1], c_ref[src, x - 1])
 
 
-def outer_kernel(idx_ref, west_ref, east_ref, inner_ref, edge_ref, wind_ref, f_ref, h_ref, g_ref, emission_ref,
+def outer_kernel(low, idx_ref, got_ref, inner_ref, edge_ref, wind_ref, f_ref, h_ref, g_ref, emission_ref,
                  u_ref, send_ref, c_ref, k_ref, t_ref):
     gx, gy, me = idx_ref[0], idx_ref[1], idx_ref[2]
     n_gx, n_gy = idx_ref[3], idx_ref[4]
-    depth, rows, width = u_ref.shape
+    depth, half, width = u_ref.shape
     groups = send_ref.shape[0]
-    half, strip = rows // 2, HSTEPS
-    ext = rows + 2 * strip
+    strip = HSTEPS
     inside = inside_mask(depth, width, gy, n_gy)
-    west_in = inside * jnp.where(gx > 0, 1.0, 0.0)
-    east_in = inside * jnp.where(gx < n_gx - 1, 1.0, 0.0)
-
-    def west_plane(a, r):
-        at = 2 * (half * a + r - (a == 2))
-        return with_strips(west_ref[at], west_ref[at + 1], west_ref[6 * half - 2 + a], r)
-
-    def east_plane(a, r):
-        at = 2 * (half * a + r - (a == 2))
-        return with_strips(east_ref[at], east_ref[at + 1], east_ref[6 * half - 4 + a], r)
-
-    aw = west_plane(1, 0)
-    c_ref[0, 0] = west_plane(0, 0)
-    for r in range(1, strip):
-        c_ref[0, r] = west_plane(0, r)
-        ax = west_plane(1, r)
-        for i, k in enumerate(coefficients(ax, aw, west_plane(2, r), west_in)):
+    halo_in = inside * jnp.where(gx > 0 if low else gx < n_gx - 1, 1.0, 0.0)
+    n_got = 3 * half - (1 if low else 2)
+
+    def plane(a, r):
+        side = got_ref[n_got + a // 2, :, pl.ds(a % 2 * TILE, TILE)]
+        return with_strips(got_ref[half * a + r - (a == 2)], side, r)
+
+    first = 0 if low else half + 1
+    aw = plane(1, 0) if low else wind_ref[...]
+    if low:
+        c_ref[0, 0] = plane(0, 0)
+    else:
+        c_ref[0, first + strip - 1] = plane(0, strip - 1)
+    for r in range(1, strip) if low else range(strip - 1):
+        c_ref[0, first + r] = plane(0, r)
+        ax = plane(1, r)
+        for i, k in enumerate(coefficients(ax, aw, plane(2, r), halo_in)):
             k_ref[i, r] = k
         aw = ax
-    for i in range(5):
-        k = inner_ref[i, 0]
-        if i == 0:
-            k = k + jnp.minimum(aw, 0.0) * inside
-        if i == 2:
-            k = k + jnp.maximum(aw, 0.0) * inside
-        k_ref[i, strip] = k
-    aw = wind_ref[...]
-    for r in range(strip - 1):
-        c_ref[0, strip + rows + r] = east_plane(0, r)
-        ax = east_plane(1, r)
-        for i, k in enumerate(coefficients(ax, aw, east_plane(2, r), east_in)):
-            k_ref[i, strip + rows + r] = k
-        aw = ax
-    c_ref[0, ext - 1] = east_plane(0, strip - 1)
+    if low:
+        for i in range(5):
+            k = inner_ref[i, 0]
+            if i == 0:
+                k = k + jnp.minimum(aw, 0.0) * inside
+            if i == 2:
+                k = k + jnp.maximum(aw, 0.0) * inside
+            k_ref[i, strip] = k
 
     for step in range(1, strip + 1):
         src = (step - 1) % 2
+        reach = strip - 1 + step if low else half + 1 - step
+
+        def at(q):
+            if low and q >= reach:
+                return edge_ref[step - 1, q - reach]
+            if not low and q <= reach:
+                return edge_ref[step - 1, q - reach + 3]
+            return c_ref[src, q]
+
         for i in range(strip):
-            for r, side in ((step + i, 0), (ext - 1 - step - i, 1)):
-                low_side = side == 0
-                def at(q):
-                    if low_side and q >= strip - 1 + step:
-                        return edge_ref[step - 1, q - (strip - 1 + step)]
-                    if not low_side and q <= strip + rows - step:
-                        return edge_ref[step - 1, q - (strip + rows - step) + 3]
-                    return c_ref[src, q]
-                weights = k_ref if r <= strip or r >= strip + rows else inner_ref
-                row = r if weights is k_ref else r - strip
-                new = substep(weights, row, at(r), at(r + 1), at(r - 1))
-                if step < strip:
-                    c_ref[1 - src, r] = new
-                else:
-                    c_ref[1 - src, r, :, :width] = new[:, :width]
+            r = (step if low else reach) + i
+            if low:
+                weights, row = (k_ref, r) if r <= strip else (inner_ref, r - strip)
+            else:
+                weights, row = (k_ref, r - first) if r >= first else (inner_ref, r + half - 1)
+            new = substep(weights, row, at(r), at(r + 1), at(r - 1))
+            if step < strip:
+                c_ref[1 - src, r] = new
+            else:
+                c_ref[1 - src, r, :, :width] = new[:, :width]
     last = strip % 2
+    begin = strip if low else 1
 
     def level(z):
-        d = c_ref[last, strip : strip + rows, z, :width]
+        d = c_ref[last, begin : begin + half, z, :width]
         if z == 0:
-            d = d + emission_ref[...] * jnp.where(me == 0, 1.0, 0.0)
+            mine = emission_ref[:half] if low else emission_ref[half:]
+            d = d + mine * jnp.where(me == 0, 1.0, 0.0)
         return d
 
+    mine = pl.ds(0 if low else half, half)
     run = None
     for z in range(depth):
         d = level(z)
-        run = d if z == 0 else d + f_ref[z - 1] * run
+        run = d if z == 0 else d + f_ref[z - 1, mine] * run
         t_ref[z] = run - d
-    beta = f_ref[depth - 1] * run
+    beta = f_ref[depth - 1, mine] * run
     run = None
     for z in reversed(range(depth)):
         d = level(z)
-        run = d if z == depth - 1 else d + h_ref[z + 1] * run
-        u_ref[z] = g_ref[z] * (t_ref[z] + run)
-    gamma = h_ref[0] * run
+        run = d if z == depth - 1 else d + h_ref[z + 1, mine] * run
+        u_ref[z] = g_ref[z, mine] * (t_ref[z] + run)
+    gamma = h_ref[0, mine] * run
     for s in range(groups):
         send_ref[s] = jnp.where(s > me, beta, gamma)
 
 
-def finish_kernel(idx_ref, u_ref, a_ref, b_ref, w_ref, got_ref, out_hbm, out_ref, sems):
+def finish_kernel(idx_ref, west_ref, east_ref, a_ref, b_ref, w_ref, got_ref, out_hbm, out_ref, sems):
     me = idx_ref[2]
-    depth, rows, width = u_ref.shape
-    groups = w_ref.shape[0]
-    part = depth // PARTS
+    depth, rows, width = a_ref.shape
+    groups, half, part = w_ref.shape[0], rows // 2, depth // PARTS
     zero = jnp.zeros((rows, width), jnp.float32)
     below, above = zero, zero
     for s in range(groups):
@@ -315,7 +321,9 @@
     copies = []
     for q in range(PARTS):
         for z in range(q * part, (q + 1) * part):
-            out_ref[z] = u_ref[z] + (a_ref[z] * below + b_ref[z] * above)
+            more = a_ref[z] * below + b_ref[z] * above
+            out_ref[z, :half] = west_ref[z] + more[:half]
+            out_ref[z, half:] = east_ref[z] + more[half:]
         at = pl.ds(q * part, part)
         copies.append(pltpu.make_async_copy(out_ref.at[at], out_hbm.at[at], sems.at[q]))
         copies[-1].start()
@@ -331,18 +339,20 @@
 def local(conc, wind_x, wind_y, profiles, classes, heights, emission):
     species, depth, rows, width = conc.shape
     groups = lax.axis_size("gz")
-    half, ext, wide = rows // 2, rows + 2 * HSTEPS, width + TILE
+    half, wide = rows // 2, width + TILE
     idx = jnp.stack(
         [lax.axis_index("gx"), lax.axis_index("gy"), lax.axis_index("gz"),
          jnp.int32(lax.axis_size("gx")), jnp.int32(lax.axis_size("gy"))]
     ).astype(jnp.int32)
     block, pane, tile, row = (depth, rows, width), (rows, width), (depth, TILE), (depth, wide)
-    n_lo, n_hi = 6 * half - 4, 6 * half - 2
-
-    own, left, right = call(
-        pack_kernel, [HBM] * 3, [(3, rows, depth, width), (3, *tile), (3, *tile)],
-        [(3, *block), pltpu.SemaphoreType.DMA((3 * PARTS,))], 1 << 20,
-    )(*(pltpu.with_memory_space_constraint(x, pltpu.HBM) for x in (conc[0], wind_x, wind_y)))
+    n_lo, n_hi = 3 * half - 2, 3 * half - 1
+
+    small = (profiles, classes, heights, emission[0])
+    own, left, right, profiles, classes, heights, emission = call(
+        pack_kernel, [HBM] * 7,
+        [(3, rows, depth, width), (3, *tile), (3, *tile), *(jax.ShapeDtypeStruct(x.shape, x.dtype) for x in small)],
+        [(3, *block), pltpu.SemaphoreType.DMA((3 * PARTS,)), pltpu.SemaphoreType.DMA((len(small),))], 1 << 20,
+    )(*(pltpu.with_memory_space_constraint(x, pltpu.HBM) for x in (conc[0], wind_x, wind_y, *small)))
     south = shifted(right, "gy", 1)
     north = shifted(left, "gy", -1)
     (k,) = call(table_kernel, [SMEM, VMEM, VMEM], [(depth * groups + 1, *pane)], [], 1 << 24)(
@@ -350,7 +360,8 @@
     )
     own, south, north, k = lax.optimization_barrier((own, south, north, k))
     lo, hi, side_lo, side_hi = call(
-        send_kernel, [VMEM] * 3, [(n_lo + 3, *tile), (n_hi + 3, *tile), (3, *tile), (3, *tile)], [], 1 << 20
+        send_kernel, [VMEM] * 3,
+        [(n_lo + 2, depth, width), (n_hi + 2, depth, width), (3, *tile), (3, *tile)], [], 1 << 20
     )(own, south, north)
     west = shifted(hi, "gx", 1)
     east = shifted(lo, "gx", -1)
@@ -363,14 +374,20 @@
         factor_kernel, [SMEM, VMEM], [twice, twice, block, block, block, (groups, *pane)],
         [twice, twice, (groups, *pane), (groups, *pane)], 1 << 24,
     )(idx, k)
-    u, send = call(
-        outer_kernel, [SMEM] + [VMEM] * 9, [block, (groups, *pane)],
-        [(2, ext, *row), (5, ext, *row), block], 1 << 24,
-    )(idx, west, east, weights, edge, wind, f, h, g, emission[0])
+    halves = []
+    for low, got in ((True, west), (False, east)):
+        if not low:
+            wind, _ = lax.optimization_barrier((wind, halves[0][1]))
+        halves.append(call(
+            functools.partial(outer_kernel, low), [SMEM] + [VMEM] * 8,
+            [(depth, half, width), (groups, half, width)],
+            [(2, half + HSTEPS + 1, *row), (5, HSTEPS + 1, *row), (depth, half, width)], 1 << 24,
+        )(idx, got, weights, edge, wind, f, h, g, emission))
+    send = jnp.concatenate([s for _, s in halves], axis=1)
     got = lax.all_to_all(send, "gz", split_axis=0, concat_axis=0, tiled=True)
     (out,) = call(
-        finish_kernel, [SMEM] + [VMEM] * 5, [block], [block, pltpu.SemaphoreType.DMA((PARTS,))], 1 << 20, HBM
-    )(idx, u, a, b, w, got)
+        finish_kernel, [SMEM] + [VMEM] * 6, [block], [block, pltpu.SemaphoreType.DMA((PARTS,))], 1 << 20, HBM
+    )(idx, *(u for u, _ in halves), a, b, w, got)
     return out[None]
 
 

time: 66.2 us -> 62.8 us (0.949)
  the two profiles are of different devices: /device:TPU:24 before, /device:TPU:58 now
where the time goes in v3:
time: 62.8 us; the launch traced here: 62.5 us
  blocking collectives  30.1 us (48%)
  Pallas kernels  15.1 us (24%)
  starting transfers between devices  11.7 us (19%)
  waiting for transfers between devices  5.48 us (9%)
    all_to_all x1, blocking collectives, local(): got = lax.all_to_all(send, 'gz', split_axis=0, concat_axis=0, tiled=True)  30.1 us
    ppermute x4, starting transfers between devices, shifted(): lax.ppermute(x, axis, [(i, i + by) for i in range(length) if 0 <= i + by...  11.7 us
    ppermute x4, waiting for transfers between devices, shifted(): lax.ppermute(x, axis, [(i, i + by) for i in range(length) if 0 <= i + by...  5.48 us
    pallas_call x2, Pallas kernels, local(): call(functools.partial(outer_kernel, low), [SMEM] + [VMEM] * 8, [(depth,...  4.22 us
    pallas_call x1, Pallas kernels, local(): call(factor_kernel, [SMEM, VMEM], [twice, twice, block, block, block, (gr...  2.85 us
    pallas_call x1, Pallas kernels, local(): call(inner_kernel, [SMEM] + [VMEM] * 3, [(5, rows, *row), (HSTEPS, 4, *ro...  2.45 us
    pallas_call x1, Pallas kernels, local(): call(table_kernel, [SMEM, VMEM, VMEM], [(depth * groups + 1, *pane)], [],...  1.77 us
    pallas_call x1, Pallas kernels, local(): call(pack_kernel, [HBM] * 7, [(3, rows, depth, width), (3, *tile), (3, *t...  1.56 us
  transfers between devices with their start and end apart: 4, of which 3 were waited for; matrix products, arithmetic and copies ran while one was open for 0% of the time, Pallas kernels for 14%

profile of v3, /device:TPU:58, one launch (start us, length us, event | category | flops | bytes accessed | tf_op | source)
XLA Modules:
  0.0 62.5 jit_solution(14653639602543531386)
XLA Ops:
  0.0 1.6 %shard_map.73 = (f32[3,16,16,256]{3,2,1,0:T(8,128)S(1)}, f32[3,16,128]{2,1,0:T(8,128)S(1)}, f32[3,16,128]{2,1,0:T(8,128)S(1)}, f32[8,128]{1,0:T(8,128)S(1)}, s32...) custom-call(f32[16,16,256]{2,1,0:T(8,128)} %bitcast.6, f32[16,16,256]{2,1,0:T(8,128)} %wx_hbm.1, ...), custom_call_target="tpu_custom_call" | custom-call | flops 1048576 | bytes 1048576 | tf_op jit(solution)/shard_map/pallas_call | solution.py:351
  1.6 3.8 %collective-permute-start = (f32[3,16,128]{2,1,0:T(8,128)S(1)}, f32[3,16,128]{2,1,0:T(8,128)S(1)}, u32[]{:S(2)}, u32[]{:S(2)}) collective-permute-start(f32[3,16,128]{2,1,0:T(8,128)S(1)} %get-tuple-element.35), channel_id=1, source_target_pairs={{0,8},{8,16},{16,24},{1,9},{9,17},{17,25},{2,10},{10,18},{18,26},{... | collective-permute-start | bytes 73736 | tf_op jit(solution)/shard_map/ppermute | solution.py:336
  5.4 2.0 %collective-permute-start.1 = (f32[3,16,128]{2,1,0:T(8,128)S(1)}, f32[3,16,128]{2,1,0:T(8,128)S(1)}, u32[]{:S(2)}, u32[]{:S(2)}) collective-permute-start(f32[3,16,128]{2,1,0:T(8,128)S(1)} %get-tuple-element.36), channel_id=1, source_target_pairs={{8,0},{16,8},{24,16},{9,1},{17,9},{25,17},{10,2},{18,10},{26,18},{... | collective-permute-start | bytes 73736 | tf_op jit(solution)/shard_map/ppermute | solution.py:336
  7.4 1.8 %shard_map.74.k_ref = f32[129,16,256]{2,1,0:T(8,128)S(1)} custom-call(f32[8,128]{1,0:T(8,128)S(1)} %get-tuple-element.37.profiles_ref, s32[16,256]{1,0:T(8,128)S(1)} %get-tuple-element.38.classes_ref, s32[16,256]{1,0:T(8,128)S(1)} %get-tuple-element.39.heights_ref), custom_call_target="tpu_custom_call" | custom-call | flops 16777216 | bytes 1048576 | tf_op jit(solution)/shard_map/pallas_call | solution.py:358
  9.2 0.0 collective-permute-done.south_ref
  9.2 1.9 %collective-permute-done.1.north_ref = f32[3,16,128]{2,1,0:T(8,128)S(1)} collective-permute-done((f32[3,16,128]{2,1,0:T(8,128)S(1)}, f32[3,16,128]{2,1,0:T(8,128)S(1)}, u32[]{:S(2)}, u32[]{:S(2)}) %collective-permute-start.1) | collective-permute-done | bytes 24608 | tf_op jit(solution)/shard_map/ppermute | solution.py:336
  11.1 0.9 %shard_map.75 = (f32[24,16,256]{2,1,0:T(8,128)}, f32[25,16,256]{2,1,0:T(8,128)}, f32[3,16,128]{2,1,0:T(8,128)S(1)}, f32[3,16,128]{2,1,0:T(8,128)S(1)}) custom-call(f32[3,16,16,256]{3,2,1,0:T(8,128)S(1)} %get-tuple-element.40.own_ref, f32[3,16,128]{2,1,0:T(8,128)S(1)} %collective-permute-done.south_ref, f32[3,16,128]{2,1,0:T(8,128)S(1)} %collective-permute-done.1.north_ref), custom_call_target="tpu_custom_call" | custom-call | flops 1048576 | bytes 1048576 | tf_op jit(solution)/shard_map/pallas_call | solution.py:362
  12.0 3.0 %collective-permute-start.2 = (f32[25,16,256]{2,1,0:T(8,128)}, f32[25,16,256]{2,1,0:T(8,128)S(1)}, u32[]{:S(2)}, u32[]{:S(2)}) collective-permute-start(f32[25,16,256]{2,1,0:T(8,128)} %get-tuple-element.43), channel_id=1, source_target_pairs={{0,32},{32,64},{64,96},{96,128},{128,160},{160,192},{192,224},{224... | collective-permute-start | bytes 1228808 | tf_op jit(solution)/shard_map/ppermute | solution.py:336
  15.1 2.8 %collective-permute-start.3 = (f32[24,16,256]{2,1,0:T(8,128)}, f32[24,16,256]{2,1,0:T(8,128)}, u32[]{:S(2)}, u32[]{:S(2)}) collective-permute-start(f32[24,16,256]{2,1,0:T(8,128)} %get-tuple-element.55), channel_id=1, source_target_pairs={{32,0},{64,32},{96,64},{128,96},{160,128},{192,160},{224,192},{256... | collective-permute-start | bytes 1179656 | tf_op jit(solution)/shard_map/ppermute | solution.py:336
  17.9 0.1 stack.15.idx_ref
  18.0 2.8 %shard_map.77 = (f32[32,16,256]{2,1,0:T(8,128)S(1)}, f32[32,16,256]{2,1,0:T(8,128)S(1)}, f32[16,16,256]{2,1,0:T(8,128)S(1)}, f32[16,16,256]{2,1,0:T(8,128)S(1)},...) custom-call(s32[5]{0:T(128)S(1)} %stack.15.idx_ref, f32[129,16,256]{2,1,0:T(8,128)S(1)} %shard_map.74.k_ref), custom_call_target="tpu_custom_call" | custom-call | flops 16777216 | bytes 1048576 | tf_op jit(solution)/shard_map/pallas_call | solution.py:373
  20.8 2.4 %shard_map.76 = (f32[5,16,16,384]{3,2,1,0:T(8,128)S(1)}, f32[8,4,16,384]{3,2,1,0:T(8,128)S(1)}, f32[16,384]{1,0:T(8,128)S(1)}) custom-call(s32[5]{0:T(128)S(1)} %stack.15.idx_ref, f32[3,16,16,256]{3,2,1,0:T(8,128)S(1)} %get-tuple-element.40.own_ref, f32[3,16,128]{2,1,0:T(8,128)S(1)} %get-tuple-element.44.side_lo_ref, ...), custom_call_target="tpu_custom_call" | custom-call | flops 16777216 | bytes 1048576 | tf_op jit(solution)/shard_map/pallas_call | solution.py:368
  23.3 0.8 %collective-permute-done.2.got_ref = f32[25,16,256]{2,1,0:T(8,128)S(1)} collective-permute-done((f32[25,16,256]{2,1,0:T(8,128)}, f32[25,16,256]{2,1,0:T(8,128)S(1)}, u32[]{:S(2)}, u32[]{:S(2)}) %collective-permute-start.2) | collective-permute-done | bytes 409632 | tf_op jit(solution)/shard_map/ppermute | solution.py:336
  24.1 1.9 %shard_map.78 = (f32[16,8,256]{2,1,0:T(8,128)S(1)}, f32[8,8,256]{2,1,0:T(8,128)S(1)}) custom-call(s32[5]{0:T(128)S(1)} %stack.15.idx_ref, f32[25,16,256]{2,1,0:T(8,128)S(1)} %collective-permute-done.2.got_ref, f32[5,16,16,384]{3,2,1,0:T(8,128)S(1)} %get-tuple-element.46.inner_ref, f32[8,4,16,384]{3,2,1,0:T(8,128)S(1)} %get-tuple-element.47.edge_ref, ...), custom_call_target="tpu_custom_call" | custom-call | flops 16777216 | bytes 1048576 | tf_op jit(solution)/shard_map/pallas_call | solution.py:381
  26.0 2.8 %collective-permute-done.3.got_ref = f32[24,16,256]{2,1,0:T(8,128)} collective-permute-done((f32[24,16,256]{2,1,0:T(8,128)}, f32[24,16,256]{2,1,0:T(8,128)}, u32[]{:S(2)}, u32[]{:S(2)}) %collective-permute-start.3) | collective-permute-done | bytes 393248 | tf_op jit(solution)/shard_map/ppermute | solution.py:336
  28.7 2.3 %shard_map.79 = (f32[16,8,256]{2,1,0:T(8,128)S(1)}, f32[8,8,256]{2,1,0:T(8,128)S(1)}) custom-call(s32[5]{0:T(128)S(1)} %stack.15.idx_ref, f32[24,16,256]{2,1,0:T(8,128)} %collective-permute-done.3.got_ref, f32[5,16,16,384]{3,2,1,0:T(8,128)S(1)} %get-tuple-element.46.inner_ref, f32[8,4,16,384]{3,2,1,0:T(8,128)S(1)} %get-tuple-element.47.edge_ref, ...), custom_call_target="tpu_custom_call" | custom-call | flops 16777216 | bytes 1048576 | tf_op jit(solution)/shard_map/pallas_call | solution.py:381
  31.1 30.1 %all_to_all.5.got_ref = f32[8,16,256]{2,1,0:T(8,128)S(1)} all-to-all(f32[8,16,256]{2,1,0:T(8,128)S(1)} %pad_maximum_fusion), channel_id=1, replica_groups=mesh['gx'=16,'gy'=4,'gz'=8] {'gz'}, dimensions={0} | all-to-all | bytes 262144 | tf_op jit(solution)/shard_map/all_to_all | solution.py:387
  61.2 1.3 %shard_map.80 = f32[16,16,256]{2,1,0:T(8,128)} custom-call(s32[5]{0:T(128)S(1)} %stack.15.idx_ref, f32[16,8,256]{2,1,0:T(8,128)S(1)} %get-tuple-element.54.west_ref, f32[16,8,256]{2,1,0:T(8,128)S(1)} %get-tuple-element.58.east_ref, f32[16,16,256]{2,1,0:T(8,128)S(1)} %get-tuple-element.59.a_ref, f32[16,16,256]{2,1,0:T(8,128)S(1)} %get-tuple-element.60.b_ref, ...), custom_call_target="tpu_custom_call" | custom-call | flops 1048576 | bytes 1048576 | tf_op jit(solution)/shard_map/pallas_call | solution.py:388
  (1 shorter events, 0.0 us)
Async XLA Ops:
  1.6 7.6 %collective-permute-start = (f32[3,16,128]{2,1,0:T(8,128)S(1)}, f32[3,16,128]{2,1,0:T(8,128)S(1)}, u32[]{:S(2)}, u32[]{:S(2)}) collective-permute-start(f32[3,16,128]{2,1,0:T(8,128)S(1)} %get-tuple-element.35), channel_id=1, source_target_pairs={{0,8},{8,16},{16,24},{1,9},{9,17},{17,25},{2,10},{10,18},{18,26},{... | collective-permute-start | bytes 73736 | tf_op jit(solution)/shard_map/ppermute | solution.py:336
  5.4 5.7 %collective-permute-start.1 = (f32[3,16,128]{2,1,0:T(8,128)S(1)}, f32[3,16,128]{2,1,0:T(8,128)S(1)}, u32[]{:S(2)}, u32[]{:S(2)}) collective-permute-start(f32[3,16,128]{2,1,0:T(8,128)S(1)} %get-tuple-element.36), channel_id=1, source_target_pairs={{8,0},{16,8},{24,16},{9,1},{17,9},{25,17},{10,2},{18,10},{26,18},{... | collective-permute-start | bytes 73736 | tf_op jit(solution)/shard_map/ppermute | solution.py:336
  12.0 12.1 %collective-permute-start.2 = (f32[25,16,256]{2,1,0:T(8,128)}, f32[25,16,256]{2,1,0:T(8,128)S(1)}, u32[]{:S(2)}, u32[]{:S(2)}) collective-permute-start(f32[25,16,256]{2,1,0:T(8,128)} %get-tuple-element.43), channel_id=1, source_target_pairs={{0,32},{32,64},{64,96},{96,128},{128,160},{160,192},{192,224},{224... | collective-permute-start | bytes 1228808 | tf_op jit(solution)/shard_map/ppermute | solution.py:336
  15.1 13.6 %collective-permute-start.3 = (f32[24,16,256]{2,1,0:T(8,128)}, f32[24,16,256]{2,1,0:T(8,128)}, u32[]{:S(2)}, u32[]{:S(2)}) collective-permute-start(f32[24,16,256]{2,1,0:T(8,128)} %get-tuple-element.55), channel_id=1, source_target_pairs={{32,0},{64,32},{96,64},{128,96},{160,128},{192,160},{224,192},{256... | collective-permute-start | bytes 1179656 | tf_op jit(solution)/shard_map/ppermute | solution.py:336

commit v4 on v3

--- a/solution.py
+++ b/solution.py
@@ -13,7 +13,8 @@
 DIFFUSION = 0.05
 CANOPY = 0.2
 LIMIT = 8 * 1024 * 1024
-PARTS = 4
+PARTS = 1
+LEVELS = 8
 
 VMEM = pl.BlockSpec(memory_space=pltpu.VMEM)
 SMEM = pl.BlockSpec(memory_space=pltpu.SMEM)
@@ -32,7 +33,7 @@
     )
 
 
-def pack_kernel(c_hbm, wx_hbm, wy_hbm, *refs):
+def pack_kernel(idx_ref, c_hbm, wx_hbm, wy_hbm, *refs):
     small, (own_ref, yl_ref, yr_ref), kept, (in_ref, sems, small_sems) = refs[:4], refs[4:7], refs[7:11], refs[11:]
     depth, rows, width = c_hbm.shape
     half, strip, part = rows // 2, HSTEPS, depth // PARTS
@@ -111,7 +112,7 @@
 
 
 def factor_kernel(idx_ref, k_ref, f_ref, h_ref, g_ref, a_ref, b_ref, w_ref,
-                  e_ref, d_ref, up_ref, down_ref):
+                  n_ref, m_ref, p_ref, q_ref, up_ref, down_ref):
     me = idx_ref[2]
     depth = g_ref.shape[0]
     groups = w_ref.shape[0]
@@ -119,37 +120,39 @@
     total = depth * groups
     one = jnp.ones(shape, jnp.float32)
 
-    def chunk(n, carry):
-        e, d = carry
-        m = groups - 1 - n
-        aside_e = jnp.where(n == me, 0, depth)
-        aside_d = jnp.where(m == me, 0, depth)
-
-        def level(i, carry):
-            e, d, up, down = carry
-            k = k_ref[n * depth + i + 1]
-            f = k / (e + k)
-            f_ref[aside_e + i] = f
-            e_ref[aside_e + i] = e
-            j = depth - 1 - i
-            kb = k_ref[m * depth + j]
-            h = kb / (d + kb)
-            h_ref[aside_d + j] = h
-            d_ref[aside_d + j] = d
-            return 1.0 + f * e, 1.0 + h * d, up * f, down * h
-
-        e, d, up, down = lax.fori_loop(0, depth, level, (e, d, one, one))
-        up_ref[n] = up
-        down_ref[m] = down
-        return e, d
-
-    lax.fori_loop(0, groups, chunk, (one, 1.0 + k_ref[total]))
-
+    def some(t, carry):
+        n, p, up, down = carry
+        low = t * LEVELS
+        high = total - 1 - low
+        chunk_n, chunk_p = low // depth, high // depth
+        at_n = low % depth + jnp.where(chunk_n == me, 0, depth)
+        at_p = high % depth + jnp.where(chunk_p == me, 0, depth)
+        m, q = one, one
+        for i in range(LEVELS):
+            k, kb = k_ref[low + i + 1], k_ref[high - i]
+            n_ref[at_n + i], m_ref[at_n + i] = n, m
+            p_ref[at_p - i], q_ref[at_p - i] = p, q
+            m, q = n + k * m, p + kb * q
+            n, p = m + k * n, q + kb * p
+            up, down = up * k, down * kb
+        m, q = 1.0 / m, 1.0 / q
+        up, down = up * m, down * q
+        up_ref[chunk_n], down_ref[chunk_p] = up, down
+        fresh = low % depth + LEVELS == depth
+        return n * m, p * q, jnp.where(fresh, one, up), jnp.where(fresh, one, down)
+
+    lax.fori_loop(0, total // LEVELS, some, (one, 1.0 + k_ref[total], one, one))
+
+    begin = me * depth
+    for i in range(depth):
+        m, q = m_ref[i], q_ref[i]
+        k, kb = k_ref[begin + i + 1], k_ref[begin + i]
+        f_ref[i] = k * m / (n_ref[i] + k * m)
+        h_ref[i] = kb * q / (p_ref[i] + kb * q)
+        g_ref[i] = m * q / (n_ref[i] * q + p_ref[i] * m - m * q)
     run = one
     for i in range(depth):
-        g = 1.0 / (e_ref[i] + d_ref[i] - 1.0)
-        g_ref[i] = g
-        a_ref[i] = g * run
+        a_ref[i] = g_ref[i] * run
         run = run * f_ref[i]
     run = one
     for i in reversed(range(depth)):
@@ -349,10 +352,10 @@
 
     small = (profiles, classes, heights, emission[0])
     own, left, right, profiles, classes, heights, emission = call(
-        pack_kernel, [HBM] * 7,
+        pack_kernel, [SMEM] + [HBM] * 7,
         [(3, rows, depth, width), (3, *tile), (3, *tile), *(jax.ShapeDtypeStruct(x.shape, x.dtype) for x in small)],
         [(3, *block), pltpu.SemaphoreType.DMA((3 * PARTS,)), pltpu.SemaphoreType.DMA((len(small),))], 1 << 20,
-    )(*(pltpu.with_memory_space_constraint(x, pltpu.HBM) for x in (conc[0], wind_x, wind_y, *small)))
+    )(idx, *(pltpu.with_memory_space_constraint(x, pltpu.HBM) for x in (conc[0], wind_x, wind_y, *small)))
     south = shifted(right, "gy", 1)
     north = shifted(left, "gy", -1)
     (k,) = call(table_kernel, [SMEM, VMEM, VMEM], [(depth * groups + 1, *pane)], [], 1 << 24)(
@@ -371,8 +374,8 @@
     )(idx, own, side_lo, side_hi)
     twice = (2 * depth, rows, width)
     f, h, g, a, b, w = call(
-        factor_kernel, [SMEM, VMEM], [twice, twice, block, block, block, (groups, *pane)],
-        [twice, twice, (groups, *pane), (groups, *pane)], 1 << 24,
+        factor_kernel, [SMEM, VMEM], [block] * 5 + [(groups, *pane)],
+        [twice] * 4 + [(groups, *pane)] * 2, 1 << 24,
     )(idx, k)
     halves = []
     for low, got in ((True, west), (False, east)):

time: 62.8 us -> 61.7 us (0.982)
  Pallas kernels: 15.1 us -> 13.4 us
  waiting for transfers between devices: 5.48 us -> 6.15 us
    pallas_call x1, Pallas kernels: 0.9 us -> 0.1 us  [local(): call(send_kernel, [VMEM] * 3, [(n_lo + 2, depth, width), (n_hi + 2, depth...]
    ppermute x4, waiting for transfers between devices: 5.48 us -> 6.15 us  [shifted(): lax.ppermute(x, axis, [(i, i + by) for i in range(length) if 0 <= i + by...]
  transfers between devices with their start and end apart: 4 -> 4, of which waited for: 3 -> 3; matrix products, arithmetic and copies ran while one was open for 0% -> 0% of each run, Pallas kernels for 14% -> 13%
where the time goes in v4:
time: 61.7 us; the launch traced here: 61.5 us
  blocking collectives  30.1 us (49%)
  Pallas kernels  13.4 us (22%)
  starting transfers between devices  11.7 us (19%)
  waiting for transfers between devices  6.15 us (10%)
    all_to_all x1, blocking collectives, local(): got = lax.all_to_all(send, 'gz', split_axis=0, concat_axis=0, tiled=True)  30.1 us
    ppermute x4, starting transfers between devices, shifted(): lax.ppermute(x, axis, [(i, i + by) for i in range(length) if 0 <= i + by...  11.7 us
    ppermute x4, waiting for transfers between devices, shifted(): lax.ppermute(x, axis, [(i, i + by) for i in range(length) if 0 <= i + by...  6.15 us
    pallas_call x2, Pallas kernels, local(): call(functools.partial(outer_kernel, low), [SMEM] + [VMEM] * 8, [(depth,...  3.76 us
    pallas_call x1, Pallas kernels, local(): call(inner_kernel, [SMEM] + [VMEM] * 3, [(5, rows, *row), (HSTEPS, 4, *ro...  2.45 us
    pallas_call x1, Pallas kernels, local(): call(pack_kernel, [SMEM] + [HBM] * 7, [(3, rows, depth, width), (3, *tile...  2.04 us
    pallas_call x1, Pallas kernels, local(): call(factor_kernel, [SMEM, VMEM], [block] * 5 + [(groups, *pane)], [twice...  1.95 us
    pallas_call x1, Pallas kernels, local(): call(table_kernel, [SMEM, VMEM, VMEM], [(depth * groups + 1, *pane)], [],...  1.77 us
  transfers between devices with their start and end apart: 4, of which 3 were waited for; matrix products, arithmetic and copies ran while one was open for 0% of the time, Pallas kernels for 13%

profile of v4, /device:TPU:58, one launch (start us, length us, event | category | flops | bytes accessed | tf_op | source)
XLA Modules:
  0.0 61.5 jit_solution(13037824879233219436)
XLA Ops:
  0.0 0.1 stack.15.idx_ref
  0.1 2.0 %shard_map.73 = (f32[3,16,16,256]{3,2,1,0:T(8,128)S(1)}, f32[3,16,128]{2,1,0:T(8,128)S(1)}, f32[3,16,128]{2,1,0:T(8,128)S(1)}, f32[8,128]{1,0:T(8,128)S(1)}, s32...) custom-call(s32[5]{0:T(128)S(1)} %stack.15.idx_ref, f32[16,16,256]{2,1,0:T(8,128)} %bitcast.6, ...), custom_call_target="tpu_custom_call" | custom-call | flops 1048576 | bytes 1048576 | tf_op jit(solution)/shard_map/pallas_call | solution.py:354
  2.1 3.8 %collective-permute-start = (f32[3,16,128]{2,1,0:T(8,128)S(1)}, f32[3,16,128]{2,1,0:T(8,128)S(1)}, u32[]{:S(2)}, u32[]{:S(2)}) collective-permute-start(f32[3,16,128]{2,1,0:T(8,128)S(1)} %get-tuple-element.35), channel_id=1, source_target_pairs={{0,8},{8,16},{16,24},{1,9},{9,17},{17,25},{2,10},{10,18},{18,26},{... | collective-permute-start | bytes 73736 | tf_op jit(solution)/shard_map/ppermute | solution.py:339
  6.0 2.0 %collective-permute-start.1 = (f32[3,16,128]{2,1,0:T(8,128)S(1)}, f32[3,16,128]{2,1,0:T(8,128)S(1)}, u32[]{:S(2)}, u32[]{:S(2)}) collective-permute-start(f32[3,16,128]{2,1,0:T(8,128)S(1)} %get-tuple-element.36), channel_id=1, source_target_pairs={{8,0},{16,8},{24,16},{9,1},{17,9},{25,17},{10,2},{18,10},{26,18},{... | collective-permute-start | bytes 73736 | tf_op jit(solution)/shard_map/ppermute | solution.py:339
  8.0 1.8 %shard_map.74.k_ref = f32[129,16,256]{2,1,0:T(8,128)S(1)} custom-call(f32[8,128]{1,0:T(8,128)S(1)} %get-tuple-element.37.profiles_ref, s32[16,256]{1,0:T(8,128)S(1)} %get-tuple-element.38.classes_ref, s32[16,256]{1,0:T(8,128)S(1)} %get-tuple-element.39.heights_ref), custom_call_target="tpu_custom_call" | custom-call | flops 16777216 | bytes 1048576 | tf_op jit(solution)/shard_map/pallas_call | solution.py:361
  9.8 0.0 collective-permute-done.south_ref
  9.8 1.9 %collective-permute-done.1.north_ref = f32[3,16,128]{2,1,0:T(8,128)S(1)} collective-permute-done((f32[3,16,128]{2,1,0:T(8,128)S(1)}, f32[3,16,128]{2,1,0:T(8,128)S(1)}, u32[]{:S(2)}, u32[]{:S(2)}) %collective-permute-start.1) | collective-permute-done | bytes 24608 | tf_op jit(solution)/shard_map/ppermute | solution.py:339
  11.7 0.1 shard_map.75
  11.8 3.1 %collective-permute-start.2 = (f32[25,16,256]{2,1,0:T(8,128)S(1)}, f32[25,16,256]{2,1,0:T(8,128)S(1)}, u32[]{:S(2)}, u32[]{:S(2)}) collective-permute-start(f32[25,16,256]{2,1,0:T(8,128)S(1)} %get-tuple-element.43), channel_id=1, source_target_pairs={{0,32},{32,64},{64,96},{96,128},{128,160},{160,192},{192,224},{224... | collective-permute-start | bytes 1228808 | tf_op jit(solution)/shard_map/ppermute | solution.py:339
  14.8 2.8 %collective-permute-start.3 = (f32[24,16,256]{2,1,0:T(8,128)S(1)}, f32[24,16,256]{2,1,0:T(8,128)S(1)}, u32[]{:S(2)}, u32[]{:S(2)}) collective-permute-start(f32[24,16,256]{2,1,0:T(8,128)S(1)} %get-tuple-element.55), channel_id=1, source_target_pairs={{32,0},{64,32},{96,64},{128,96},{160,128},{192,160},{224,192},{256... | collective-permute-start | bytes 1179656 | tf_op jit(solution)/shard_map/ppermute | solution.py:339
  17.6 1.9 %shard_map.77 = (f32[16,16,256]{2,1,0:T(8,128)S(1)}, f32[16,16,256]{2,1,0:T(8,128)S(1)}, f32[16,16,256]{2,1,0:T(8,128)S(1)}, f32[16,16,256]{2,1,0:T(8,128)S(1)},...) custom-call(s32[5]{0:T(128)S(1)} %stack.15.idx_ref, f32[129,16,256]{2,1,0:T(8,128)S(1)} %shard_map.74.k_ref), custom_call_target="tpu_custom_call" | custom-call | flops 16777216 | bytes 1048576 | tf_op jit(solution)/shard_map/pallas_call | solution.py:376
  19.6 2.4 %shard_map.76 = (f32[5,16,16,384]{3,2,1,0:T(8,128)S(1)}, f32[8,4,16,384]{3,2,1,0:T(8,128)S(1)}, f32[16,384]{1,0:T(8,128)S(1)}) custom-call(s32[5]{0:T(128)S(1)} %stack.15.idx_ref, f32[3,16,16,256]{3,2,1,0:T(8,128)S(1)} %get-tuple-element.40.own_ref, f32[3,16,128]{2,1,0:T(8,128)S(1)} %get-tuple-element.44.side_lo_ref, ...), custom_call_target="tpu_custom_call" | custom-call | flops 16777216 | bytes 1048576 | tf_op jit(solution)/shard_map/pallas_call | solution.py:371
  22.1 1.6 %collective-permute-done.2.got_ref = f32[25,16,256]{2,1,0:T(8,128)S(1)} collective-permute-done((f32[25,16,256]{2,1,0:T(8,128)S(1)}, f32[25,16,256]{2,1,0:T(8,128)S(1)}, u32[]{:S(2)}, u32[]{:S(2)}) %collective-permute-start.2) | collective-permute-done | bytes 409632 | tf_op jit(solution)/shard_map/ppermute | solution.py:339
  23.6 1.9 %shard_map.78 = (f32[16,8,256]{2,1,0:T(8,128)S(1)}, f32[8,8,256]{2,1,0:T(8,128)S(1)}) custom-call(s32[5]{0:T(128)S(1)} %stack.15.idx_ref, f32[25,16,256]{2,1,0:T(8,128)S(1)} %collective-permute-done.2.got_ref, f32[5,16,16,384]{3,2,1,0:T(8,128)S(1)} %get-tuple-element.46.inner_ref, f32[8,4,16,384]{3,2,1,0:T(8,128)S(1)} %get-tuple-element.47.edge_ref, ...), custom_call_target="tpu_custom_call" | custom-call | flops 16777216 | bytes 1048576 | tf_op jit(solution)/shard_map/pallas_call | solution.py:384
  25.5 2.6 %collective-permute-done.3.got_ref = f32[24,16,256]{2,1,0:T(8,128)S(1)} collective-permute-done((f32[24,16,256]{2,1,0:T(8,128)S(1)}, f32[24,16,256]{2,1,0:T(8,128)S(1)}, u32[]{:S(2)}, u32[]{:S(2)}) %collective-permute-start.3) | collective-permute-done | bytes 393248 | tf_op jit(solution)/shard_map/ppermute | solution.py:339
  28.2 1.9 %shard_map.79 = (f32[16,8,256]{2,1,0:T(8,128)S(1)}, f32[8,8,256]{2,1,0:T(8,128)S(1)}) custom-call(s32[5]{0:T(128)S(1)} %stack.15.idx_ref, f32[24,16,256]{2,1,0:T(8,128)S(1)} %collective-permute-done.3.got_ref, f32[5,16,16,384]{3,2,1,0:T(8,128)S(1)} %get-tuple-element.46.inner_ref, f32[8,4,16,384]{3,2,1,0:T(8,128)S(1)} %get-tuple-element.47.edge_ref, ...), custom_call_target="tpu_custom_call" | custom-call | flops 16777216 | bytes 1048576 | tf_op jit(solution)/shard_map/pallas_call | solution.py:384
  30.1 30.1 %all_to_all.5.got_ref = f32[8,16,256]{2,1,0:T(8,128)S(1)} all-to-all(f32[8,16,256]{2,1,0:T(8,128)S(1)} %pad_maximum_fusion), channel_id=1, replica_groups=mesh['gx'=16,'gy'=4,'gz'=8] {'gz'}, dimensions={0} | all-to-all | bytes 262144 | tf_op jit(solution)/shard_map/all_to_all | solution.py:390
  60.2 1.3 %shard_map.80 = f32[16,16,256]{2,1,0:T(8,128)} custom-call(s32[5]{0:T(128)S(1)} %stack.15.idx_ref, f32[16,8,256]{2,1,0:T(8,128)S(1)} %get-tuple-element.54.west_ref, f32[16,8,256]{2,1,0:T(8,128)S(1)} %get-tuple-element.58.east_ref, f32[16,16,256]{2,1,0:T(8,128)S(1)} %get-tuple-element.59.a_ref, f32[16,16,256]{2,1,0:T(8,128)S(1)} %get-tuple-element.60.b_ref, ...), custom_call_target="tpu_custom_call" | custom-call | flops 1048576 | bytes 1048576 | tf_op jit(solution)/shard_map/pallas_call | solution.py:391
  (1 shorter events, 0.0 us)
Async XLA Ops:
  2.1 7.6 %collective-permute-start = (f32[3,16,128]{2,1,0:T(8,128)S(1)}, f32[3,16,128]{2,1,0:T(8,128)S(1)}, u32[]{:S(2)}, u32[]{:S(2)}) collective-permute-start(f32[3,16,128]{2,1,0:T(8,128)S(1)} %get-tuple-element.35), channel_id=1, source_target_pairs={{0,8},{8,16},{16,24},{1,9},{9,17},{17,25},{2,10},{10,18},{18,26},{... | collective-permute-start | bytes 73736 | tf_op jit(solution)/shard_map/ppermute | solution.py:339
  6.0 5.7 %collective-permute-start.1 = (f32[3,16,128]{2,1,0:T(8,128)S(1)}, f32[3,16,128]{2,1,0:T(8,128)S(1)}, u32[]{:S(2)}, u32[]{:S(2)}) collective-permute-start(f32[3,16,128]{2,1,0:T(8,128)S(1)} %get-tuple-element.36), channel_id=1, source_target_pairs={{8,0},{16,8},{24,16},{9,1},{17,9},{25,17},{10,2},{18,10},{26,18},{... | collective-permute-start | bytes 73736 | tf_op jit(solution)/shard_map/ppermute | solution.py:339
  11.8 11.8 %collective-permute-start.2 = (f32[25,16,256]{2,1,0:T(8,128)S(1)}, f32[25,16,256]{2,1,0:T(8,128)S(1)}, u32[]{:S(2)}, u32[]{:S(2)}) collective-permute-start(f32[25,16,256]{2,1,0:T(8,128)S(1)} %get-tuple-element.43), channel_id=1, source_target_pairs={{0,32},{32,64},{64,96},{96,128},{128,160},{160,192},{192,224},{224... | collective-permute-start | bytes 1228808 | tf_op jit(solution)/shard_map/ppermute | solution.py:339
  14.8 13.3 %collective-permute-start.3 = (f32[24,16,256]{2,1,0:T(8,128)S(1)}, f32[24,16,256]{2,1,0:T(8,128)S(1)}, u32[]{:S(2)}, u32[]{:S(2)}) collective-permute-start(f32[24,16,256]{2,1,0:T(8,128)S(1)} %get-tuple-element.55), channel_id=1, source_target_pairs={{32,0},{64,32},{96,64},{128,96},{160,128},{192,160},{224,192},{256... | collective-permute-start | bytes 1179656 | tf_op jit(solution)/shard_map/ppermute | solution.py:339

commit v5 on v4

--- a/solution.py
+++ b/solution.py
@@ -13,7 +13,7 @@
 DIFFUSION = 0.05
 CANOPY = 0.2
 LIMIT = 8 * 1024 * 1024
-PARTS = 1
+PARTS = 4
 LEVELS = 8
 
 VMEM = pl.BlockSpec(memory_space=pltpu.VMEM)
@@ -21,12 +21,12 @@
 HBM = pl.BlockSpec(memory_space=pltpu.HBM)
 
 
-def call(kernel, ins, outs, scratch, flops, out_spec=VMEM):
+def call(kernel, ins, outs, scratch, flops):
     return pl.pallas_call(
         kernel,
         out_shape=[jax.ShapeDtypeStruct(s, jnp.float32) if isinstance(s, tuple) else s for s in outs],
         in_specs=ins,
-        out_specs=[out_spec] * len(outs),
+        out_specs=[VMEM] * len(outs),
         scratch_shapes=[pltpu.VMEM(s, jnp.float32) if isinstance(s, tuple) else s for s in scratch],
         compiler_params=pltpu.CompilerParams(vmem_limit_bytes=LIMIT),
         cost_estimate=pl.CostEstimate(flops=flops, bytes_accessed=1 << 20, transcendentals=0),
@@ -76,12 +76,13 @@
     to_lo, to_hi = 0, 0
     for a in range(3):
         for x in range(rows):
+            first, last = own_ref[a, x, :, :TILE], own_ref[a, x, :, TILE:]
             if x < half and not (a > 0 and x == half - 1):
-                lo_ref[to_lo] = own_ref[a, x]
-                to_lo += 1
+                lo_ref[to_lo], lo_ref[to_lo + 1] = first, last
+                to_lo += 2
             if x >= half and not (a == 2 and x == half):
-                hi_ref[to_hi] = own_ref[a, x]
-                to_hi += 1
+                hi_ref[to_hi], hi_ref[to_hi + 1] = first, last
+                to_hi += 2
     even = lax.broadcasted_iota(jnp.int32, (depth, TILE), 1) // HSTEPS % 2 == 0
     for a in range(3):
         south, north = south_ref[a], north_ref[a]
@@ -89,12 +90,11 @@
         high = jnp.where(even, pltpu.roll(south, TILE - HSTEPS, 1), pltpu.roll(north, HSTEPS, 1))
         side_lo_ref[a] = low
         side_hi_ref[a] = high
-        lanes = pl.ds(a % 2 * TILE, TILE)
-        lo_ref[to_lo + a // 2, :, lanes] = low
-        hi_ref[to_hi + a // 2, :, lanes] = high
-
-
-def table_kernel(profiles_ref, classes_ref, heights_ref, k_ref):
+        lo_ref[to_lo + a] = low
+        hi_ref[to_hi + a] = high
+
+
+def mixing_numbers(profiles_ref, classes_ref, heights_ref, k_ref):
     total = k_ref.shape[0] - 1
     classes, heights = classes_ref[...], heights_ref[...]
     bits = [(classes & (1 << b)) != 0 for b in range(3)]
@@ -108,17 +108,18 @@
         k_ref[z + 1] = jnp.where(z < heights, CANOPY * k, k)
         return 0
 
-    lax.fori_loop(0, total, mixing, 0, unroll=4)
-
-
-def factor_kernel(idx_ref, k_ref, f_ref, h_ref, g_ref, a_ref, b_ref, w_ref,
-                  n_ref, m_ref, p_ref, q_ref, up_ref, down_ref):
+    lax.fori_loop(0, total, mixing, 0, unroll=8)
+
+
+def factor_kernel(idx_ref, profiles_ref, classes_ref, heights_ref, f_ref, h_ref, g_ref, a_ref, b_ref, w_ref,
+                  k_ref, n_ref, m_ref, p_ref, q_ref, up_ref, down_ref):
     me = idx_ref[2]
     depth = g_ref.shape[0]
     groups = w_ref.shape[0]
     shape = w_ref.shape[1:]
     total = depth * groups
     one = jnp.ones(shape, jnp.float32)
+    mixing_numbers(profiles_ref, classes_ref, heights_ref, k_ref)
 
     def some(t, carry):
         n, p, up, down = carry
@@ -189,9 +190,9 @@
     return (k_ref[0, r] * own + k_ref[1, r] * east) + (k_ref[2, r] * west + k_ref[3, r] * north) + k_ref[4, r] * south
 
 
-def with_strips(cells, side, row):
+def with_strips(first, last, side, row):
     by = (TILE - HSTEPS - 2 * HSTEPS * row) % TILE
-    return jnp.concatenate([cells, pltpu.roll(side, by, 1) if by else side], axis=1)
+    return jnp.concatenate([first, last, pltpu.roll(side, by, 1) if by else side], axis=1)
 
 
 def inside_mask(depth, width, gy, n_gy):
@@ -208,7 +209,7 @@
 
     def plane(a, x):
         side = side_lo_ref[a] if x < half else side_hi_ref[a]
-        return with_strips(own_ref[a, x], side, x % half)
+        return with_strips(own_ref[a, x, :, :TILE], own_ref[a, x, :, TILE:], side, x % half)
 
     aw = None
     for x in range(rows):
@@ -235,11 +236,11 @@
     strip = HSTEPS
     inside = inside_mask(depth, width, gy, n_gy)
     halo_in = inside * jnp.where(gx > 0 if low else gx < n_gx - 1, 1.0, 0.0)
-    n_got = 3 * half - (1 if low else 2)
+    n_got = 6 * half - (2 if low else 4)
 
     def plane(a, r):
-        side = got_ref[n_got + a // 2, :, pl.ds(a % 2 * TILE, TILE)]
-        return with_strips(got_ref[half * a + r - (a == 2)], side, r)
+        at = 2 * (half * a + r - (a == 2))
+        return with_strips(got_ref[at], got_ref[at + 1], got_ref[n_got + a], r)
 
     first = 0 if low else half + 1
     aw = plane(1, 0) if low else wind_ref[...]
@@ -311,27 +312,20 @@
         send_ref[s] = jnp.where(s > me, beta, gamma)
 
 
-def finish_kernel(idx_ref, west_ref, east_ref, a_ref, b_ref, w_ref, got_ref, out_hbm, out_ref, sems):
+def finish_kernel(idx_ref, west_ref, east_ref, a_ref, b_ref, w_ref, got_ref, out_ref):
     me = idx_ref[2]
     depth, rows, width = a_ref.shape
-    groups, half, part = w_ref.shape[0], rows // 2, depth // PARTS
+    groups, half = w_ref.shape[0], rows // 2
     zero = jnp.zeros((rows, width), jnp.float32)
     below, above = zero, zero
     for s in range(groups):
         term = w_ref[s] * got_ref[s]
         below = below + jnp.where(s < me, term, zero)
         above = above + jnp.where(s > me, term, zero)
-    copies = []
-    for q in range(PARTS):
-        for z in range(q * part, (q + 1) * part):
-            more = a_ref[z] * below + b_ref[z] * above
-            out_ref[z, :half] = west_ref[z] + more[:half]
-            out_ref[z, half:] = east_ref[z] + more[half:]
-        at = pl.ds(q * part, part)
-        copies.append(pltpu.make_async_copy(out_ref.at[at], out_hbm.at[at], sems.at[q]))
-        copies[-1].start()
-    for copy in copies:
-        copy.wait()
+    for z in range(depth):
+        more = a_ref[z] * below + b_ref[z] * above
+        out_ref[z, :half] = west_ref[z] + more[:half]
+        out_ref[z, half:] = east_ref[z] + more[half:]
 
 
 def shifted(x, axis, by):
@@ -348,7 +342,7 @@
          jnp.int32(lax.axis_size("gx")), jnp.int32(lax.axis_size("gy"))]
     ).astype(jnp.int32)
     block, pane, tile, row = (depth, rows, width), (rows, width), (depth, TILE), (depth, wide)
-    n_lo, n_hi = 3 * half - 2, 3 * half - 1
+    n_lo, n_hi = 6 * half - 4, 6 * half - 2
 
     small = (profiles, classes, heights, emission[0])
     own, left, right, profiles, classes, heights, emission = call(
@@ -358,13 +352,9 @@
     )(idx, *(pltpu.with_memory_space_constraint(x, pltpu.HBM) for x in (conc[0], wind_x, wind_y, *small)))
     south = shifted(right, "gy", 1)
     north = shifted(left, "gy", -1)
-    (k,) = call(table_kernel, [SMEM, VMEM, VMEM], [(depth * groups + 1, *pane)], [], 1 << 24)(
-        profiles, classes, heights
-    )
-    own, south, north, k = lax.optimization_barrier((own, south, north, k))
     lo, hi, side_lo, side_hi = call(
         send_kernel, [VMEM] * 3,
-        [(n_lo + 2, depth, width), (n_hi + 2, depth, width), (3, *tile), (3, *tile)], [], 1 << 20
+        [(n_lo + 3, *tile), (n_hi + 3, *tile), (3, *tile), (3, *tile)], [], 1 << 20
     )(own, south, north)
     west = shifted(hi, "gx", 1)
     east = shifted(lo, "gx", -1)
@@ -373,10 +363,11 @@
         [(5, rows, *row), (HSTEPS, 4, *row), row], [(2, rows, *row)], 1 << 24,
     )(idx, own, side_lo, side_hi)
     twice = (2 * depth, rows, width)
+    profiles, _ = lax.optimization_barrier((profiles, side_lo))
     f, h, g, a, b, w = call(
-        factor_kernel, [SMEM, VMEM], [block] * 5 + [(groups, *pane)],
-        [twice] * 4 + [(groups, *pane)] * 2, 1 << 24,
-    )(idx, k)
+        factor_kernel, [SMEM, SMEM, VMEM, VMEM], [block] * 5 + [(groups, *pane)],
+        [(depth * groups + 1, *pane)] + [twice] * 4 + [(groups, *pane)] * 2, 1 << 24,
+    )(idx, profiles, classes, heights)
     halves = []
     for low, got in ((True, west), (False, east)):
         if not low:
@@ -389,7 +380,7 @@
     send = jnp.concatenate([s for _, s in halves], axis=1)
     got = lax.all_to_all(send, "gz", split_axis=0, concat_axis=0, tiled=True)
     (out,) = call(
-        finish_kernel, [SMEM] + [VMEM] * 6, [block], [block, pltpu.SemaphoreType.DMA((PARTS,))], 1 << 20, HBM
+        finish_kernel, [SMEM] + [VMEM] * 6, [block], [], 1 << 20
     )(idx, *(u for u, _ in halves), a, b, w, got)
     return out[None]
 

time: 61.7 us -> 61.7 us (level)
  Pallas kernels: 13.4 us -> 12.7 us
    pallas_call x4 -> x3, Pallas kernels: 5.14 us -> 4.49 us  [the longest x1 3.05 us: local(): call(factor_kernel, [SMEM, SMEM, VMEM, VMEM], [block] * 5 + [(groups, *pa...]
  transfers between devices with their start and end apart: 4 -> 4, of which waited for: 3 -> 3; matrix products, arithmetic and copies ran while one was open for 0% -> 0% of each run, Pallas kernels for 13% -> 12%
where the time goes in v5:
time: 61.7 us; the launch traced here: 61.4 us
  blocking collectives  30.1 us (49%)
  Pallas kernels  12.7 us (21%)
  starting transfers between devices  11.7 us (19%)
  waiting for transfers between devices  6.67 us (11%)
    all_to_all x1, blocking collectives, local(): got = lax.all_to_all(send, 'gz', split_axis=0, concat_axis=0, tiled=True)  30.1 us
    ppermute x4, starting transfers between devices, shifted(): lax.ppermute(x, axis, [(i, i + by) for i in range(length) if 0 <= i + by...  11.7 us
    ppermute x4, waiting for transfers between devices, shifted(): lax.ppermute(x, axis, [(i, i + by) for i in range(length) if 0 <= i + by...  6.67 us
    pallas_call x2, Pallas kernels, local(): call(functools.partial(outer_kernel, low), [SMEM] + [VMEM] * 8, [(depth,...  3.73 us
    pallas_call x1, Pallas kernels, local(): call(factor_kernel, [SMEM, SMEM, VMEM, VMEM], [block] * 5 + [(groups, *pa...  3.05 us
    pallas_call x1, Pallas kernels, local(): call(inner_kernel, [SMEM] + [VMEM] * 3, [(5, rows, *row), (HSTEPS, 4, *ro...  2.43 us
    pallas_call x1, Pallas kernels, local(): call(pack_kernel, [SMEM] + [HBM] * 7, [(3, rows, depth, width), (3, *tile...  2.1 us
    pallas_call x1, Pallas kernels, local(): call(finish_kernel, [SMEM] + [VMEM] * 6, [block], [], 1 << 20)  1.33 us
  transfers between devices with their start and end apart: 4, of which 3 were waited for; matrix products, arithmetic and copies ran while one was open for 0% of the time, Pallas kernels for 12%

profile of v5, /device:TPU:58, one launch (start us, length us, event | category | flops | bytes accessed | tf_op | source)
XLA Modules:
  0.0 61.4 jit_solution(1017669464851209660)
XLA Ops:
  0.0 0.1 stack.15.idx_ref
  0.1 2.1 %shard_map.73 = (f32[3,16,16,256]{3,2,1,0:T(8,128)S(1)}, f32[3,16,128]{2,1,0:T(8,128)S(1)}, f32[3,16,128]{2,1,0:T(8,128)S(1)}, f32[8,128]{1,0:T(8,128)S(1)}, s32...) custom-call(s32[5]{0:T(128)S(1)} %stack.15.idx_ref, f32[16,16,256]{2,1,0:T(8,128)} %bitcast.6, ...), custom_call_target="tpu_custom_call" | custom-call | flops 1048576 | bytes 1048576 | tf_op jit(solution)/shard_map/pallas_call | solution.py:348
  2.2 3.8 %collective-permute-start = (f32[3,16,128]{2,1,0:T(8,128)S(1)}, f32[3,16,128]{2,1,0:T(8,128)S(1)}, u32[]{:S(2)}, u32[]{:S(2)}) collective-permute-start(f32[3,16,128]{2,1,0:T(8,128)S(1)} %get-tuple-element.32), channel_id=1, source_target_pairs={{0,8},{8,16},{16,24},{1,9},{9,17},{17,25},{2,10},{10,18},{18,26},{... | collective-permute-start | bytes 73736 | tf_op jit(solution)/shard_map/ppermute | solution.py:333
  6.0 2.0 %collective-permute-start.1 = (f32[3,16,128]{2,1,0:T(8,128)S(1)}, f32[3,16,128]{2,1,0:T(8,128)S(1)}, u32[]{:S(2)}, u32[]{:S(2)}) collective-permute-start(f32[3,16,128]{2,1,0:T(8,128)S(1)} %get-tuple-element.33), channel_id=1, source_target_pairs={{8,0},{16,8},{24,16},{9,1},{17,9},{25,17},{10,2},{18,10},{26,18},{... | collective-permute-start | bytes 73736 | tf_op jit(solution)/shard_map/ppermute | solution.py:333
  8.0 0.0 collective-permute-done.south_ref
  8.1 3.7 %collective-permute-done.1.north_ref = f32[3,16,128]{2,1,0:T(8,128)S(1)} collective-permute-done((f32[3,16,128]{2,1,0:T(8,128)S(1)}, f32[3,16,128]{2,1,0:T(8,128)S(1)}, u32[]{:S(2)}, u32[]{:S(2)}) %collective-permute-start.1) | collective-permute-done | bytes 24608 | tf_op jit(solution)/shard_map/ppermute | solution.py:333
  11.7 0.1 shard_map.74
  11.8 3.1 %collective-permute-start.2 = (f32[49,16,128]{2,1,0:T(8,128)S(1)}, f32[49,16,128]{2,1,0:T(8,128)S(1)}, u32[]{:S(2)}, u32[]{:S(2)}) collective-permute-start(f32[49,16,128]{2,1,0:T(8,128)S(1)} %get-tuple-element.34), channel_id=1, source_target_pairs={{0,32},{32,64},{64,96},{96,128},{128,160},{160,192},{192,224},{224... | collective-permute-start | bytes 1204232 | tf_op jit(solution)/shard_map/ppermute | solution.py:333
  14.9 2.8 %collective-permute-start.3 = (f32[47,16,128]{2,1,0:T(8,128)S(1)}, f32[47,16,128]{2,1,0:T(8,128)S(1)}, u32[]{:S(2)}, u32[]{:S(2)}) collective-permute-start(f32[47,16,128]{2,1,0:T(8,128)S(1)} %get-tuple-element.49), channel_id=1, source_target_pairs={{32,0},{64,32},{96,64},{128,96},{160,128},{192,160},{224,192},{256... | collective-permute-start | bytes 1155080 | tf_op jit(solution)/shard_map/ppermute | solution.py:333
  17.7 2.4 %shard_map.75 = (f32[5,16,16,384]{3,2,1,0:T(8,128)S(1)}, f32[8,4,16,384]{3,2,1,0:T(8,128)S(1)}, f32[16,384]{1,0:T(8,128)S(1)}) custom-call(s32[5]{0:T(128)S(1)} %stack.15.idx_ref, f32[3,16,16,256]{3,2,1,0:T(8,128)S(1)} %get-tuple-element.31.own_ref, f32[3,16,128]{2,1,0:T(8,128)S(1)} %get-tuple-element.35.side_lo_ref, ...), custom_call_target="tpu_custom_call" | custom-call | flops 16777216 | bytes 1048576 | tf_op jit(solution)/shard_map/pallas_call | solution.py:361
  20.1 3.1 %shard_map.76 = (f32[16,16,256]{2,1,0:T(8,128)S(1)}, f32[16,16,256]{2,1,0:T(8,128)S(1)}, f32[16,16,256]{2,1,0:T(8,128)S(1)}, f32[16,16,256]{2,1,0:T(8,128)S(1)},...) custom-call(s32[5]{0:T(128)S(1)} %stack.15.idx_ref, f32[8,128]{1,0:T(8,128)S(1)} %get-tuple-element.41.profiles_ref, ...), custom_call_target="tpu_custom_call" | custom-call | flops 16777216 | bytes 1048576 | tf_op jit(solution)/shard_map/pallas_call | solution.py:367
  23.2 0.3 collective-permute-done.2.got_ref
  23.5 1.9 %shard_map.77 = (f32[16,8,256]{2,1,0:T(8,128)S(1)}, f32[8,8,256]{2,1,0:T(8,128)S(1)}) custom-call(s32[5]{0:T(128)S(1)} %stack.15.idx_ref, f32[49,16,128]{2,1,0:T(8,128)S(1)} %collective-permute-done.2.got_ref, f32[5,16,16,384]{3,2,1,0:T(8,128)S(1)} %get-tuple-element.37.inner_ref, f32[8,4,16,384]{3,2,1,0:T(8,128)S(1)} %get-tuple-element.38.edge_ref, ...), custom_call_target="tpu_custom_call" | custom-call | flops 16777216 | bytes 1048576 | tf_op jit(solution)/shard_map/pallas_call | solution.py:375
  25.4 2.7 %collective-permute-done.3.got_ref = f32[47,16,128]{2,1,0:T(8,128)S(1)} collective-permute-done((f32[47,16,128]{2,1,0:T(8,128)S(1)}, f32[47,16,128]{2,1,0:T(8,128)S(1)}, u32[]{:S(2)}, u32[]{:S(2)}) %collective-permute-start.3) | collective-permute-done | bytes 385056 | tf_op jit(solution)/shard_map/ppermute | solution.py:333
  28.1 1.9 %shard_map.78 = (f32[16,8,256]{2,1,0:T(8,128)S(1)}, f32[8,8,256]{2,1,0:T(8,128)S(1)}) custom-call(s32[5]{0:T(128)S(1)} %stack.15.idx_ref, f32[47,16,128]{2,1,0:T(8,128)S(1)} %collective-permute-done.3.got_ref, f32[5,16,16,384]{3,2,1,0:T(8,128)S(1)} %get-tuple-element.37.inner_ref, f32[8,4,16,384]{3,2,1,0:T(8,128)S(1)} %get-tuple-element.38.edge_ref, ...), custom_call_target="tpu_custom_call" | custom-call | flops 16777216 | bytes 1048576 | tf_op jit(solution)/shard_map/pallas_call | solution.py:375
  29.9 30.1 %all_to_all.5.got_ref = f32[8,16,256]{2,1,0:T(8,128)S(1)} all-to-all(f32[8,16,256]{2,1,0:T(8,128)S(1)} %pad_maximum_fusion), channel_id=1, replica_groups=mesh['gx'=16,'gy'=4,'gz'=8] {'gz'}, dimensions={0} | all-to-all | bytes 262144 | tf_op jit(solution)/shard_map/all_to_all | solution.py:381
  60.1 1.3 %shard_map.79 = f32[16,16,256]{2,1,0:T(8,128)} custom-call(s32[5]{0:T(128)S(1)} %stack.15.idx_ref, f32[16,8,256]{2,1,0:T(8,128)S(1)} %get-tuple-element.48.west_ref, f32[16,8,256]{2,1,0:T(8,128)S(1)} %get-tuple-element.52.east_ref, f32[16,16,256]{2,1,0:T(8,128)S(1)} %get-tuple-element.53.a_ref, f32[16,16,256]{2,1,0:T(8,128)S(1)} %get-tuple-element.54.b_ref, ...), custom_call_target="tpu_custom_call" | custom-call | flops 1048576 | bytes 1048576 | tf_op jit(solution)/shard_map/pallas_call | solution.py:382
  (1 shorter events, 0.0 us)
Async XLA Ops:
  2.2 5.9 %collective-permute-start = (f32[3,16,128]{2,1,0:T(8,128)S(1)}, f32[3,16,128]{2,1,0:T(8,128)S(1)}, u32[]{:S(2)}, u32[]{:S(2)}) collective-permute-start(f32[3,16,128]{2,1,0:T(8,128)S(1)} %get-tuple-element.32), channel_id=1, source_target_pairs={{0,8},{8,16},{16,24},{1,9},{9,17},{17,25},{2,10},{10,18},{18,26},{... | collective-permute-start | bytes 73736 | tf_op jit(solution)/shard_map/ppermute | solution.py:333
  6.0 5.7 %collective-permute-start.1 = (f32[3,16,128]{2,1,0:T(8,128)S(1)}, f32[3,16,128]{2,1,0:T(8,128)S(1)}, u32[]{:S(2)}, u32[]{:S(2)}) collective-permute-start(f32[3,16,128]{2,1,0:T(8,128)S(1)} %get-tuple-element.33), channel_id=1, source_target_pairs={{8,0},{16,8},{24,16},{9,1},{17,9},{25,17},{10,2},{18,10},{26,18},{... | collective-permute-start | bytes 73736 | tf_op jit(solution)/shard_map/ppermute | solution.py:333
  11.8 11.7 %collective-permute-start.2 = (f32[49,16,128]{2,1,0:T(8,128)S(1)}, f32[49,16,128]{2,1,0:T(8,128)S(1)}, u32[]{:S(2)}, u32[]{:S(2)}) collective-permute-start(f32[49,16,128]{2,1,0:T(8,128)S(1)} %get-tuple-element.34), channel_id=1, source_target_pairs={{0,32},{32,64},{64,96},{96,128},{128,160},{160,192},{192,224},{224... | collective-permute-start | bytes 1204232 | tf_op jit(solution)/shard_map/ppermute | solution.py:333
  14.9 13.2 %collective-permute-start.3 = (f32[47,16,128]{2,1,0:T(8,128)S(1)}, f32[47,16,128]{2,1,0:T(8,128)S(1)}, u32[]{:S(2)}, u32[]{:S(2)}) collective-permute-start(f32[47,16,128]{2,1,0:T(8,128)S(1)} %get-tuple-element.49), channel_id=1, source_target_pairs={{32,0},{64,32},{96,64},{128,96},{160,128},{192,160},{224,192},{256... | collective-permute-start | bytes 1155080 | tf_op jit(solution)/shard_map/ppermute | solution.py:333

commit v6 on v5

--- a/solution.py
+++ b/solution.py
@@ -33,7 +33,7 @@
     )
 
 
-def pack_kernel(idx_ref, c_hbm, wx_hbm, wy_hbm, *refs):
+def pack_kernel(c_hbm, wx_hbm, wy_hbm, *refs):
     small, (own_ref, yl_ref, yr_ref), kept, (in_ref, sems, small_sems) = refs[:4], refs[4:7], refs[7:11], refs[11:]
     depth, rows, width = c_hbm.shape
     half, strip, part = rows // 2, HSTEPS, depth // PARTS
@@ -111,9 +111,9 @@
     lax.fori_loop(0, total, mixing, 0, unroll=8)
 
 
-def factor_kernel(idx_ref, profiles_ref, classes_ref, heights_ref, f_ref, h_ref, g_ref, a_ref, b_ref, w_ref,
+def factor_kernel(profiles_ref, classes_ref, heights_ref, f_ref, h_ref, g_ref, a_ref, b_ref, w_ref,
                   k_ref, n_ref, m_ref, p_ref, q_ref, up_ref, down_ref):
-    me = idx_ref[2]
+    me = lax.axis_index("gz")
     depth = g_ref.shape[0]
     groups = w_ref.shape[0]
     shape = w_ref.shape[1:]
@@ -195,17 +195,17 @@
     return jnp.concatenate([first, last, pltpu.roll(side, by, 1) if by else side], axis=1)
 
 
-def inside_mask(depth, width, gy, n_gy):
+def inside_mask(depth, width):
+    gy, n_gy = lax.axis_index("gy"), lax.axis_size("gy")
     lane = lax.broadcasted_iota(jnp.int32, (depth, TILE), 1)
     sides = jnp.where((lane < HSTEPS) & (gy < n_gy - 1) | (lane >= TILE - HSTEPS) & (gy > 0), 1.0, 0.0)
     return jnp.concatenate([jnp.ones((depth, width), jnp.float32), sides], axis=1)
 
 
-def inner_kernel(idx_ref, own_ref, side_lo_ref, side_hi_ref, k_ref, edge_ref, wind_ref, c_ref):
-    gy, n_gy = idx_ref[1], idx_ref[4]
+def inner_kernel(own_ref, side_lo_ref, side_hi_ref, k_ref, edge_ref, wind_ref, c_ref):
     _, rows, depth, width = own_ref.shape
     half = rows // 2
-    mask = inside_mask(depth, width, gy, n_gy)
+    mask = inside_mask(depth, width)
 
     def plane(a, x):
         side = side_lo_ref[a] if x < half else side_hi_ref[a]
@@ -227,14 +227,13 @@
             c_ref[1 - src, x] = substep(k_ref, x, c_ref[src, x], c_ref[src, x + 1], c_ref[src, x - 1])
 
 
-def outer_kernel(low, idx_ref, got_ref, inner_ref, edge_ref, wind_ref, f_ref, h_ref, g_ref, emission_ref,
+def outer_kernel(low, got_ref, inner_ref, edge_ref, wind_ref, f_ref, h_ref, g_ref, emission_ref,
                  u_ref, send_ref, c_ref, k_ref, t_ref):
-    gx, gy, me = idx_ref[0], idx_ref[1], idx_ref[2]
-    n_gx, n_gy = idx_ref[3], idx_ref[4]
+    gx, me, n_gx = lax.axis_index("gx"), lax.axis_index("gz"), lax.axis_size("gx")
     depth, half, width = u_ref.shape
     groups = send_ref.shape[0]
     strip = HSTEPS
-    inside = inside_mask(depth, width, gy, n_gy)
+    inside = inside_mask(depth, width)
     halo_in = inside * jnp.where(gx > 0 if low else gx < n_gx - 1, 1.0, 0.0)
     n_got = 6 * half - (2 if low else 4)
 
@@ -312,8 +311,8 @@
         send_ref[s] = jnp.where(s > me, beta, gamma)
 
 
-def finish_kernel(idx_ref, west_ref, east_ref, a_ref, b_ref, w_ref, got_ref, out_ref):
-    me = idx_ref[2]
+def finish_kernel(west_ref, east_ref, a_ref, b_ref, w_ref, got_ref, out_ref):
+    me = lax.axis_index("gz")
     depth, rows, width = a_ref.shape
     groups, half = w_ref.shape[0], rows // 2
     zero = jnp.zeros((rows, width), jnp.float32)
@@ -337,19 +336,15 @@
     species, depth, rows, width = conc.shape
     groups = lax.axis_size("gz")
     half, wide = rows // 2, width + TILE
-    idx = jnp.stack(
-        [lax.axis_index("gx"), lax.axis_index("gy"), lax.axis_index("gz"),
-         jnp.int32(lax.axis_size("gx")), jnp.int32(lax.axis_size("gy"))]
-    ).astype(jnp.int32)
     block, pane, tile, row = (depth, rows, width), (rows, width), (depth, TILE), (depth, wide)
     n_lo, n_hi = 6 * half - 4, 6 * half - 2
 
     small = (profiles, classes, heights, emission[0])
     own, left, right, profiles, classes, heights, emission = call(
-        pack_kernel, [SMEM] + [HBM] * 7,
+        pack_kernel, [HBM] * 7,
         [(3, rows, depth, width), (3, *tile), (3, *tile), *(jax.ShapeDtypeStruct(x.shape, x.dtype) for x in small)],
         [(3, *block), pltpu.SemaphoreType.DMA((3 * PARTS,)), pltpu.SemaphoreType.DMA((len(small),))], 1 << 20,
-    )(idx, *(pltpu.with_memory_space_constraint(x, pltpu.HBM) for x in (conc[0], wind_x, wind_y, *small)))
+    )(*(pltpu.with_memory_space_constraint(x, pltpu.HBM) for x in (conc[0], wind_x, wind_y, *small)))
     south = shifted(right, "gy", 1)
     north = shifted(left, "gy", -1)
     lo, hi, side_lo, side_hi = call(
@@ -359,29 +354,29 @@
     west = shifted(hi, "gx", 1)
     east = shifted(lo, "gx", -1)
     weights, edge, wind = call(
-        inner_kernel, [SMEM] + [VMEM] * 3,
+        inner_kernel, [VMEM] * 3,
         [(5, rows, *row), (HSTEPS, 4, *row), row], [(2, rows, *row)], 1 << 24,
-    )(idx, own, side_lo, side_hi)
+    )(own, side_lo, side_hi)
     twice = (2 * depth, rows, width)
     profiles, _ = lax.optimization_barrier((profiles, side_lo))
     f, h, g, a, b, w = call(
-        factor_kernel, [SMEM, SMEM, VMEM, VMEM], [block] * 5 + [(groups, *pane)],
+        factor_kernel, [SMEM, VMEM, VMEM], [block] * 5 + [(groups, *pane)],
         [(depth * groups + 1, *pane)] + [twice] * 4 + [(groups, *pane)] * 2, 1 << 24,
-    )(idx, profiles, classes, heights)
+    )(profiles, classes, heights)
     halves = []
     for low, got in ((True, west), (False, east)):
         if not low:
             wind, _ = lax.optimization_barrier((wind, halves[0][1]))
         halves.append(call(
-            functools.partial(outer_kernel, low), [SMEM] + [VMEM] * 8,
+            functools.partial(outer_kernel, low), [VMEM] * 8,
             [(depth, half, width), (groups, half, width)],
             [(2, half + HSTEPS + 1, *row), (5, HSTEPS + 1, *row), (depth, half, width)], 1 << 24,
-        )(idx, got, weights, edge, wind, f, h, g, emission))
+        )(got, weights, edge, wind, f, h, g, emission))
     send = jnp.concatenate([s for _, s in halves], axis=1)
     got = lax.all_to_all(send, "gz", split_axis=0, concat_axis=0, tiled=True)
     (out,) = call(
-        finish_kernel, [SMEM] + [VMEM] * 6, [block], [], 1 << 20
-    )(idx, *(u for u, _ in halves), a, b, w, got)
+        finish_kernel, [VMEM] * 6, [block], [], 1 << 20
+    )(*(u for u, _ in halves), a, b, w, got)
     return out[None]
 
 

time: 61.7 us -> 59.9 us (0.971)
  Pallas kernels: 12.7 us -> 9.77 us
  waiting for transfers between devices: 6.67 us -> 7.95 us
    pallas_call x6, Pallas kernels: 12.6 us -> 9.67 us  [the longest x1 3.05 us: local(): call(factor_kernel, [SMEM, VMEM, VMEM], [block] * 5 + [(groups, *pane)],...]
    ppermute x4, waiting for transfers between devices: 6.67 us -> 7.95 us  [shifted(): lax.ppermute(x, axis, [(i, i + by) for i in range(length) if 0 <= i + by...]
  transfers between devices with their start and end apart: 4 -> 4, of which waited for: 3 -> 3; matrix products, arithmetic and copies ran while one was open for 0% -> 0% of each run, Pallas kernels for 12% -> 10%
where the time goes in v6:
time: 59.9 us; the launch traced here: 59.6 us
  blocking collectives  30.1 us (50%)
  starting transfers between devices  11.7 us (20%)
  Pallas kernels  9.77 us (16%)
  waiting for transfers between devices  7.95 us (13%)
    all_to_all x1, blocking collectives, local(): got = lax.all_to_all(send, 'gz', split_axis=0, concat_axis=0, tiled=True)  30.1 us
    ppermute x4, starting transfers between devices, shifted(): lax.ppermute(x, axis, [(i, i + by) for i in range(length) if 0 <= i + by...  11.7 us
    ppermute x4, waiting for transfers between devices, shifted(): lax.ppermute(x, axis, [(i, i + by) for i in range(length) if 0 <= i + by...  7.95 us
    pallas_call x1, Pallas kernels, local(): call(factor_kernel, [SMEM, VMEM, VMEM], [block] * 5 + [(groups, *pane)],...  3.05 us
    pallas_call x2, Pallas kernels, local(): call(functools.partial(outer_kernel, low), [VMEM] * 8, [(depth, half, wid...  2.52 us
    pallas_call x1, Pallas kernels, local(): call(inner_kernel, [VMEM] * 3, [(5, rows, *row), (HSTEPS, 4, *row), row],...  1.76 us
    pallas_call x1, Pallas kernels, local(): call(pack_kernel, [HBM] * 7, [(3, rows, depth, width), (3, *tile), (3, *t...  1.56 us
  transfers between devices with their start and end apart: 4, of which 3 were waited for; matrix products, arithmetic and copies ran while one was open for 0% of the time, Pallas kernels for 10%

profile of v6, /device:TPU:58, one launch (start us, length us, event | category | flops | bytes accessed | tf_op | source)
XLA Modules:
  0.0 59.6 jit_solution(18269671886129597041)
XLA Ops:
  0.0 1.6 %shard_map.73 = (f32[3,16,16,256]{3,2,1,0:T(8,128)S(1)}, f32[3,16,128]{2,1,0:T(8,128)S(1)}, f32[3,16,128]{2,1,0:T(8,128)S(1)}, f32[8,128]{1,0:T(8,128)S(1)}, s32...) custom-call(f32[16,16,256]{2,1,0:T(8,128)} %bitcast.3, f32[16,16,256]{2,1,0:T(8,128)} %wx_hbm.1, ...), custom_call_target="tpu_custom_call" | custom-call | flops 1048576 | bytes 1048576 | tf_op jit(solution)/shard_map/pallas_call | solution.py:343
  1.6 3.8 %collective-permute-start = (f32[3,16,128]{2,1,0:T(8,128)S(1)}, f32[3,16,128]{2,1,0:T(8,128)S(1)}, u32[]{:S(2)}, u32[]{:S(2)}) collective-permute-start(f32[3,16,128]{2,1,0:T(8,128)S(1)} %get-tuple-element.32), channel_id=1, source_target_pairs={{0,8},{8,16},{16,24},{1,9},{9,17},{17,25},{2,10},{10,18},{18,26},{... | collective-permute-start | bytes 73736 | tf_op jit(solution)/shard_map/ppermute | solution.py:332
  5.4 2.0 %collective-permute-start.1 = (f32[3,16,128]{2,1,0:T(8,128)S(1)}, f32[3,16,128]{2,1,0:T(8,128)S(1)}, u32[]{:S(2)}, u32[]{:S(2)}) collective-permute-start(f32[3,16,128]{2,1,0:T(8,128)S(1)} %get-tuple-element.33), channel_id=1, source_target_pairs={{8,0},{16,8},{24,16},{9,1},{17,9},{25,17},{10,2},{18,10},{26,18},{... | collective-permute-start | bytes 73736 | tf_op jit(solution)/shard_map/ppermute | solution.py:332
  7.4 0.0 collective-permute-done.south_ref
  7.4 3.7 %collective-permute-done.1.north_ref = f32[3,16,128]{2,1,0:T(8,128)S(1)} collective-permute-done((f32[3,16,128]{2,1,0:T(8,128)S(1)}, f32[3,16,128]{2,1,0:T(8,128)S(1)}, u32[]{:S(2)}, u32[]{:S(2)}) %collective-permute-start.1) | collective-permute-done | bytes 24608 | tf_op jit(solution)/shard_map/ppermute | solution.py:332
  11.1 0.1 shard_map.74
  11.2 3.1 %collective-permute-start.2 = (f32[49,16,128]{2,1,0:T(8,128)S(1)}, f32[49,16,128]{2,1,0:T(8,128)S(1)}, u32[]{:S(2)}, u32[]{:S(2)}) collective-permute-start(f32[49,16,128]{2,1,0:T(8,128)S(1)} %get-tuple-element.34), channel_id=1, source_target_pairs={{0,32},{32,64},{64,96},{96,128},{128,160},{160,192},{192,224},{224... | collective-permute-start | bytes 1204232 | tf_op jit(solution)/shard_map/ppermute | solution.py:332
  14.3 2.8 %collective-permute-start.3 = (f32[47,16,128]{2,1,0:T(8,128)S(1)}, f32[47,16,128]{2,1,0:T(8,128)S(1)}, u32[]{:S(2)}, u32[]{:S(2)}) collective-permute-start(f32[47,16,128]{2,1,0:T(8,128)S(1)} %get-tuple-element.49), channel_id=1, source_target_pairs={{32,0},{64,32},{96,64},{128,96},{160,128},{192,160},{224,192},{256... | collective-permute-start | bytes 1155080 | tf_op jit(solution)/shard_map/ppermute | solution.py:332
  17.1 1.8 %shard_map.75 = (f32[5,16,16,384]{3,2,1,0:T(8,128)S(1)}, f32[8,4,16,384]{3,2,1,0:T(8,128)S(1)}, f32[16,384]{1,0:T(8,128)S(1)}) custom-call(f32[3,16,16,256]{3,2,1,0:T(8,128)S(1)} %get-tuple-element.31.own_ref, f32[3,16,128]{2,1,0:T(8,128)S(1)} %get-tuple-element.35.side_lo_ref, f32[3,16,128]{2,1,0:T(8,128)S(1)} %get-tuple-element.36.side_hi_ref), custom_call_target="tpu_custom_call" | custom-call | flops 16777216 | bytes 1048576 | tf_op jit(solution)/shard_map/pallas_call | solution.py:356
  18.8 3.1 %shard_map.76 = (f32[16,16,256]{2,1,0:T(8,128)S(1)}, f32[16,16,256]{2,1,0:T(8,128)S(1)}, f32[16,16,256]{2,1,0:T(8,128)S(1)}, f32[16,16,256]{2,1,0:T(8,128)S(1)},...) custom-call(f32[8,128]{1,0:T(8,128)S(1)} %get-tuple-element.41.profiles_ref, ...), custom_call_target="tpu_custom_call" | custom-call | flops 16777216 | bytes 1048576 | tf_op jit(solution)/shard_map/pallas_call | solution.py:362
  21.9 1.0 %collective-permute-done.2.got_ref = f32[49,16,128]{2,1,0:T(8,128)S(1)} collective-permute-done((f32[49,16,128]{2,1,0:T(8,128)S(1)}, f32[49,16,128]{2,1,0:T(8,128)S(1)}, u32[]{:S(2)}, u32[]{:S(2)}) %collective-permute-start.2) | collective-permute-done | bytes 401440 | tf_op jit(solution)/shard_map/ppermute | solution.py:332
  22.9 1.3 %shard_map.77 = (f32[16,8,256]{2,1,0:T(8,128)S(1)}, f32[8,8,256]{2,1,0:T(8,128)S(1)}) custom-call(f32[49,16,128]{2,1,0:T(8,128)S(1)} %collective-permute-done.2.got_ref, f32[5,16,16,384]{3,2,1,0:T(8,128)S(1)} %get-tuple-element.37.inner_ref, f32[8,4,16,384]{3,2,1,0:T(8,128)S(1)} %get-tuple-element.38.edge_ref, f32[16,384]{1,0:T(8,128)S(1)} %get-tuple-element.51.wind_ref, ...), custom_call_target="tpu_custom_call" | custom-call | flops 16777216 | bytes 1048576 | tf_op jit(solution)/shard_map/pallas_call | solution.py:370
  24.2 3.3 %collective-permute-done.3.got_ref = f32[47,16,128]{2,1,0:T(8,128)S(1)} collective-permute-done((f32[47,16,128]{2,1,0:T(8,128)S(1)}, f32[47,16,128]{2,1,0:T(8,128)S(1)}, u32[]{:S(2)}, u32[]{:S(2)}) %collective-permute-start.3) | collective-permute-done | bytes 385056 | tf_op jit(solution)/shard_map/ppermute | solution.py:332
  27.4 1.2 %shard_map.78 = (f32[16,8,256]{2,1,0:T(8,128)S(1)}, f32[8,8,256]{2,1,0:T(8,128)S(1)}) custom-call(f32[47,16,128]{2,1,0:T(8,128)S(1)} %collective-permute-done.3.got_ref, f32[5,16,16,384]{3,2,1,0:T(8,128)S(1)} %get-tuple-element.37.inner_ref, f32[8,4,16,384]{3,2,1,0:T(8,128)S(1)} %get-tuple-element.38.edge_ref, f32[16,384]{1,0:T(8,128)S(1)} %get-tuple-element.51.wind_ref, ...), custom_call_target="tpu_custom_call" | custom-call | flops 16777216 | bytes 1048576 | tf_op jit(solution)/shard_map/pallas_call | solution.py:370
  28.7 30.1 %all_to_all.5.got_ref = f32[8,16,256]{2,1,0:T(8,128)S(1)} all-to-all(f32[8,16,256]{2,1,0:T(8,128)S(1)} %pad_maximum_fusion), channel_id=1, replica_groups=mesh['gx'=16,'gy'=4,'gz'=8] {'gz'}, dimensions={0} | all-to-all | bytes 262144 | tf_op jit(solution)/shard_map/all_to_all | solution.py:376
  58.8 0.8 %shard_map.79 = f32[16,16,256]{2,1,0:T(8,128)} custom-call(f32[16,8,256]{2,1,0:T(8,128)S(1)} %get-tuple-element.48.west_ref, f32[16,8,256]{2,1,0:T(8,128)S(1)} %get-tuple-element.52.east_ref, f32[16,16,256]{2,1,0:T(8,128)S(1)} %get-tuple-element.53.a_ref, f32[16,16,256]{2,1,0:T(8,128)S(1)} %get-tuple-element.54.b_ref, ...), custom_call_target="tpu_custom_call" | custom-call | flops 1048576 | bytes 1048576 | tf_op jit(solution)/shard_map/pallas_call | solution.py:377
  (1 shorter events, 0.0 us)
Async XLA Ops:
  1.6 5.9 %collective-permute-start = (f32[3,16,128]{2,1,0:T(8,128)S(1)}, f32[3,16,128]{2,1,0:T(8,128)S(1)}, u32[]{:S(2)}, u32[]{:S(2)}) collective-permute-start(f32[3,16,128]{2,1,0:T(8,128)S(1)} %get-tuple-element.32), channel_id=1, source_target_pairs={{0,8},{8,16},{16,24},{1,9},{9,17},{17,25},{2,10},{10,18},{18,26},{... | collective-permute-start | bytes 73736 | tf_op jit(solution)/shard_map/ppermute | solution.py:332
  5.4 5.7 %collective-permute-start.1 = (f32[3,16,128]{2,1,0:T(8,128)S(1)}, f32[3,16,128]{2,1,0:T(8,128)S(1)}, u32[]{:S(2)}, u32[]{:S(2)}) collective-permute-start(f32[3,16,128]{2,1,0:T(8,128)S(1)} %get-tuple-element.33), channel_id=1, source_target_pairs={{8,0},{16,8},{24,16},{9,1},{17,9},{25,17},{10,2},{18,10},{26,18},{... | collective-permute-start | bytes 73736 | tf_op jit(solution)/shard_map/ppermute | solution.py:332
  11.2 11.7 %collective-permute-start.2 = (f32[49,16,128]{2,1,0:T(8,128)S(1)}, f32[49,16,128]{2,1,0:T(8,128)S(1)}, u32[]{:S(2)}, u32[]{:S(2)}) collective-permute-start(f32[49,16,128]{2,1,0:T(8,128)S(1)} %get-tuple-element.34), channel_id=1, source_target_pairs={{0,32},{32,64},{64,96},{96,128},{128,160},{160,192},{192,224},{224... | collective-permute-start | bytes 1204232 | tf_op jit(solution)/shard_map/ppermute | solution.py:332
  14.3 13.2 %collective-permute-start.3 = (f32[47,16,128]{2,1,0:T(8,128)S(1)}, f32[47,16,128]{2,1,0:T(8,128)S(1)}, u32[]{:S(2)}, u32[]{:S(2)}) collective-permute-start(f32[47,16,128]{2,1,0:T(8,128)S(1)} %get-tuple-element.49), channel_id=1, source_target_pairs={{32,0},{64,32},{96,64},{128,96},{160,128},{192,160},{224,192},{256... | collective-permute-start | bytes 1155080 | tf_op jit(solution)/shard_map/ppermute | solution.py:332

commit v7 on v6

--- a/solution.py
+++ b/solution.py
@@ -231,7 +231,6 @@
                  u_ref, send_ref, c_ref, k_ref, t_ref):
     gx, me, n_gx = lax.axis_index("gx"), lax.axis_index("gz"), lax.axis_size("gx")
     depth, half, width = u_ref.shape
-    groups = send_ref.shape[0]
     strip = HSTEPS
     inside = inside_mask(depth, width)
     halo_in = inside * jnp.where(gx > 0 if low else gx < n_gx - 1, 1.0, 0.0)
@@ -307,8 +306,7 @@
         run = d if z == depth - 1 else d + h_ref[z + 1, mine] * run
         u_ref[z] = g_ref[z, mine] * (t_ref[z] + run)
     gamma = h_ref[0, mine] * run
-    for s in range(groups):
-        send_ref[s] = jnp.where(s > me, beta, gamma)
+    send_ref[0], send_ref[1] = beta, gamma
 
 
 def finish_kernel(west_ref, east_ref, a_ref, b_ref, w_ref, got_ref, out_ref):
@@ -318,9 +316,8 @@
     zero = jnp.zeros((rows, width), jnp.float32)
     below, above = zero, zero
     for s in range(groups):
-        term = w_ref[s] * got_ref[s]
-        below = below + jnp.where(s < me, term, zero)
-        above = above + jnp.where(s > me, term, zero)
+        below = below + jnp.where(s < me, w_ref[s] * got_ref[2 * s], zero)
+        above = above + jnp.where(s > me, w_ref[s] * got_ref[2 * s + 1], zero)
     for z in range(depth):
         more = a_ref[z] * below + b_ref[z] * above
         out_ref[z, :half] = west_ref[z] + more[:half]
@@ -369,11 +366,11 @@
             wind, _ = lax.optimization_barrier((wind, halves[0][1]))
         halves.append(call(
             functools.partial(outer_kernel, low), [VMEM] * 8,
-            [(depth, half, width), (groups, half, width)],
+            [(depth, half, width), (2, half, width)],
             [(2, half + HSTEPS + 1, *row), (5, HSTEPS + 1, *row), (depth, half, width)], 1 << 24,
         )(got, weights, edge, wind, f, h, g, emission))
     send = jnp.concatenate([s for _, s in halves], axis=1)
-    got = lax.all_to_all(send, "gz", split_axis=0, concat_axis=0, tiled=True)
+    got = lax.all_gather(send, "gz", axis=0, tiled=True)
     (out,) = call(
         finish_kernel, [VMEM] * 6, [block], [], 1 << 20
     )(*(u for u, _ in halves), a, b, w, got)

time: 59.9 us -> 56 us (0.935)
  the two profiles are of different devices: /device:TPU:58 before, /device:TPU:25 now
where the time goes in v7:
time: 56 us; the launch traced here: 55.8 us
  blocking collectives  28.7 us (51%)
  starting transfers between devices  10.1 us (18%)
  Pallas kernels  9.77 us (17%)
  waiting for transfers between devices  7.07 us (13%)
    all_gather x1, blocking collectives, local(): got = lax.all_gather(send, 'gz', axis=0, tiled=True)  28.7 us
    ppermute x4, starting transfers between devices, shifted(): lax.ppermute(x, axis, [(i, i + by) for i in range(length) if 0 <= i + by...  10.1 us
    ppermute x4, waiting for transfers between devices, shifted(): lax.ppermute(x, axis, [(i, i + by) for i in range(length) if 0 <= i + by...  7.07 us
    pallas_call x1, Pallas kernels, local(): call(factor_kernel, [SMEM, VMEM, VMEM], [block] * 5 + [(groups, *pane)],...  3.05 us
    pallas_call x2, Pallas kernels, local(): call(functools.partial(outer_kernel, low), [VMEM] * 8, [(depth, half, wid...  2.51 us
    pallas_call x1, Pallas kernels, local(): call(inner_kernel, [VMEM] * 3, [(5, rows, *row), (HSTEPS, 4, *row), row],...  1.76 us
    pallas_call x1, Pallas kernels, local(): call(pack_kernel, [HBM] * 7, [(3, rows, depth, width), (3, *tile), (3, *t...  1.56 us
  transfers between devices with their start and end apart: 4, of which 3 were waited for; matrix products, arithmetic and copies ran while one was open for 0% of the time, Pallas kernels for 11%

profile of v7, /device:TPU:25, one launch (start us, length us, event | category | flops | bytes accessed | tf_op | source)
XLA Modules:
  0.0 55.8 jit_solution(12198042913029213360)
XLA Ops:
  0.0 1.6 %shard_map.73 = (f32[3,16,16,256]{3,2,1,0:T(8,128)S(1)}, f32[3,16,128]{2,1,0:T(8,128)S(1)}, f32[3,16,128]{2,1,0:T(8,128)S(1)}, f32[8,128]{1,0:T(8,128)S(1)}, s32...) custom-call(f32[16,16,256]{2,1,0:T(8,128)} %bitcast.3, f32[16,16,256]{2,1,0:T(8,128)} %wx_hbm.1, ...), custom_call_target="tpu_custom_call" | custom-call | flops 1048576 | bytes 1048576 | tf_op jit(solution)/shard_map/pallas_call | solution.py:340
  1.6 3.5 %collective-permute-start = (f32[3,16,128]{2,1,0:T(8,128)S(1)}, f32[3,16,128]{2,1,0:T(8,128)S(1)}, u32[]{:S(2)}, u32[]{:S(2)}) collective-permute-start(f32[3,16,128]{2,1,0:T(8,128)S(1)} %get-tuple-element.32), channel_id=1, source_target_pairs={{0,8},{8,16},{16,24},{1,9},{9,17},{17,25},{2,10},{10,18},{18,26},{... | collective-permute-start | bytes 73736 | tf_op jit(solution)/shard_map/ppermute | solution.py:329
  5.1 1.3 %collective-permute-start.1 = (f32[3,16,128]{2,1,0:T(8,128)S(1)}, f32[3,16,128]{2,1,0:T(8,128)S(1)}, u32[]{:S(2)}, u32[]{:S(2)}) collective-permute-start(f32[3,16,128]{2,1,0:T(8,128)S(1)} %get-tuple-element.33), channel_id=1, source_target_pairs={{8,0},{16,8},{24,16},{9,1},{17,9},{25,17},{10,2},{18,10},{26,18},{... | collective-permute-start | bytes 73736 | tf_op jit(solution)/shard_map/ppermute | solution.py:329
  6.4 0.0 collective-permute-done.south_ref
  6.4 3.4 %collective-permute-done.1.north_ref = f32[3,16,128]{2,1,0:T(8,128)S(1)} collective-permute-done((f32[3,16,128]{2,1,0:T(8,128)S(1)}, f32[3,16,128]{2,1,0:T(8,128)S(1)}, u32[]{:S(2)}, u32[]{:S(2)}) %collective-permute-start.1) | collective-permute-done | bytes 24608 | tf_op jit(solution)/shard_map/ppermute | solution.py:329
  9.9 0.1 shard_map.74
  10.0 2.8 %collective-permute-start.2 = (f32[49,16,128]{2,1,0:T(8,128)S(1)}, f32[49,16,128]{2,1,0:T(8,128)S(1)}, u32[]{:S(2)}, u32[]{:S(2)}) collective-permute-start(f32[49,16,128]{2,1,0:T(8,128)S(1)} %get-tuple-element.34), channel_id=1, source_target_pairs={{0,32},{32,64},{64,96},{96,128},{128,160},{160,192},{192,224},{224... | collective-permute-start | bytes 1204232 | tf_op jit(solution)/shard_map/ppermute | solution.py:329
  12.8 2.5 %collective-permute-start.3 = (f32[47,16,128]{2,1,0:T(8,128)S(1)}, f32[47,16,128]{2,1,0:T(8,128)S(1)}, u32[]{:S(2)}, u32[]{:S(2)}) collective-permute-start(f32[47,16,128]{2,1,0:T(8,128)S(1)} %get-tuple-element.49), channel_id=1, source_target_pairs={{32,0},{64,32},{96,64},{128,96},{160,128},{192,160},{224,192},{256... | collective-permute-start | bytes 1155080 | tf_op jit(solution)/shard_map/ppermute | solution.py:329
  15.3 1.8 %shard_map.75 = (f32[5,16,16,384]{3,2,1,0:T(8,128)S(1)}, f32[8,4,16,384]{3,2,1,0:T(8,128)S(1)}, f32[16,384]{1,0:T(8,128)S(1)}) custom-call(f32[3,16,16,256]{3,2,1,0:T(8,128)S(1)} %get-tuple-element.31.own_ref, f32[3,16,128]{2,1,0:T(8,128)S(1)} %get-tuple-element.35.side_lo_ref, f32[3,16,128]{2,1,0:T(8,128)S(1)} %get-tuple-element.36.side_hi_ref), custom_call_target="tpu_custom_call" | custom-call | flops 16777216 | bytes 1048576 | tf_op jit(solution)/shard_map/pallas_call | solution.py:353
  17.0 3.1 %shard_map.76 = (f32[16,16,256]{2,1,0:T(8,128)S(1)}, f32[16,16,256]{2,1,0:T(8,128)S(1)}, f32[16,16,256]{2,1,0:T(8,128)S(1)}, f32[16,16,256]{2,1,0:T(8,128)S(1)},...) custom-call(f32[8,128]{1,0:T(8,128)S(1)} %get-tuple-element.41.profiles_ref, ...), custom_call_target="tpu_custom_call" | custom-call | flops 16777216 | bytes 1048576 | tf_op jit(solution)/shard_map/pallas_call | solution.py:359
  20.1 0.6 %collective-permute-done.2.got_ref = f32[49,16,128]{2,1,0:T(8,128)S(1)} collective-permute-done((f32[49,16,128]{2,1,0:T(8,128)S(1)}, f32[49,16,128]{2,1,0:T(8,128)S(1)}, u32[]{:S(2)}, u32[]{:S(2)}) %collective-permute-start.2) | collective-permute-done | bytes 401440 | tf_op jit(solution)/shard_map/ppermute | solution.py:329
  20.7 1.3 %shard_map.77 = (f32[16,8,256]{2,1,0:T(8,128)S(1)}, f32[2,8,256]{2,1,0:T(8,128)S(1)}) custom-call(f32[49,16,128]{2,1,0:T(8,128)S(1)} %collective-permute-done.2.got_ref, f32[5,16,16,384]{3,2,1,0:T(8,128)S(1)} %get-tuple-element.37.inner_ref, f32[8,4,16,384]{3,2,1,0:T(8,128)S(1)} %get-tuple-element.38.edge_ref, f32[16,384]{1,0:T(8,128)S(1)} %get-tuple-element.51.wind_ref, ...), custom_call_target="tpu_custom_call" | custom-call | flops 16777216 | bytes 1048576 | tf_op jit(solution)/shard_map/pallas_call | solution.py:367
  22.0 3.0 %collective-permute-done.3.got_ref = f32[47,16,128]{2,1,0:T(8,128)S(1)} collective-permute-done((f32[47,16,128]{2,1,0:T(8,128)S(1)}, f32[47,16,128]{2,1,0:T(8,128)S(1)}, u32[]{:S(2)}, u32[]{:S(2)}) %collective-permute-start.3) | collective-permute-done | bytes 385056 | tf_op jit(solution)/shard_map/ppermute | solution.py:329
  25.0 1.2 %shard_map.78 = (f32[16,8,256]{2,1,0:T(8,128)S(1)}, f32[2,8,256]{2,1,0:T(8,128)S(1)}) custom-call(f32[47,16,128]{2,1,0:T(8,128)S(1)} %collective-permute-done.3.got_ref, f32[5,16,16,384]{3,2,1,0:T(8,128)S(1)} %get-tuple-element.37.inner_ref, f32[8,4,16,384]{3,2,1,0:T(8,128)S(1)} %get-tuple-element.38.edge_ref, f32[16,384]{1,0:T(8,128)S(1)} %get-tuple-element.51.wind_ref, ...), custom_call_target="tpu_custom_call" | custom-call | flops 16777216 | bytes 1048576 | tf_op jit(solution)/shard_map/pallas_call | solution.py:367
  26.3 28.7 %all_gather.3.got_ref = f32[16,16,256]{2,1,0:T(8,128)S(1)} all-gather(f32[2,16,256]{2,1,0:T(8,128)S(1)} %pad_maximum_fusion), channel_id=1, replica_groups=mesh['gx'=16,'gy'=4,'gz'=8] {'gz'}, dimensions={0}, use_global_device_ids=true | all-gather | bytes 294912 | tf_op jit(solution)/shard_map/all_gather | solution.py:373
  55.0 0.8 %shard_map.79 = f32[16,16,256]{2,1,0:T(8,128)} custom-call(f32[16,8,256]{2,1,0:T(8,128)S(1)} %get-tuple-element.48.west_ref, f32[16,8,256]{2,1,0:T(8,128)S(1)} %get-tuple-element.52.east_ref, f32[16,16,256]{2,1,0:T(8,128)S(1)} %get-tuple-element.53.a_ref, f32[16,16,256]{2,1,0:T(8,128)S(1)} %get-tuple-element.54.b_ref, ...), custom_call_target="tpu_custom_call" | custom-call | flops 1048576 | bytes 1048576 | tf_op jit(solution)/shard_map/pallas_call | solution.py:374
  (1 shorter events, 0.0 us)
Async XLA Ops:
  1.6 4.9 %collective-permute-start = (f32[3,16,128]{2,1,0:T(8,128)S(1)}, f32[3,16,128]{2,1,0:T(8,128)S(1)}, u32[]{:S(2)}, u32[]{:S(2)}) collective-permute-start(f32[3,16,128]{2,1,0:T(8,128)S(1)} %get-tuple-element.32), channel_id=1, source_target_pairs={{0,8},{8,16},{16,24},{1,9},{9,17},{17,25},{2,10},{10,18},{18,26},{... | collective-permute-start | bytes 73736 | tf_op jit(solution)/shard_map/ppermute | solution.py:329
  5.1 4.8 %collective-permute-start.1 = (f32[3,16,128]{2,1,0:T(8,128)S(1)}, f32[3,16,128]{2,1,0:T(8,128)S(1)}, u32[]{:S(2)}, u32[]{:S(2)}) collective-permute-start(f32[3,16,128]{2,1,0:T(8,128)S(1)} %get-tuple-element.33), channel_id=1, source_target_pairs={{8,0},{16,8},{24,16},{9,1},{17,9},{25,17},{10,2},{18,10},{26,18},{... | collective-permute-start | bytes 73736 | tf_op jit(solution)/shard_map/ppermute | solution.py:329
  10.0 10.8 %collective-permute-start.2 = (f32[49,16,128]{2,1,0:T(8,128)S(1)}, f32[49,16,128]{2,1,0:T(8,128)S(1)}, u32[]{:S(2)}, u32[]{:S(2)}) collective-permute-start(f32[49,16,128]{2,1,0:T(8,128)S(1)} %get-tuple-element.34), channel_id=1, source_target_pairs={{0,32},{32,64},{64,96},{96,128},{128,160},{160,192},{192,224},{224... | collective-permute-start | bytes 1204232 | tf_op jit(solution)/shard_map/ppermute | solution.py:329
  12.8 12.2 %collective-permute-start.3 = (f32[47,16,128]{2,1,0:T(8,128)S(1)}, f32[47,16,128]{2,1,0:T(8,128)S(1)}, u32[]{:S(2)}, u32[]{:S(2)}) collective-permute-start(f32[47,16,128]{2,1,0:T(8,128)S(1)} %get-tuple-element.49), channel_id=1, source_target_pairs={{32,0},{64,32},{96,64},{128,96},{160,128},{192,160},{224,192},{256... | collective-permute-start | bytes 1155080 | tf_op jit(solution)/shard_map/ppermute | solution.py:329

commit v8 on v7

--- a/solution.py
+++ b/solution.py
@@ -94,7 +94,7 @@
         hi_ref[to_hi + a] = high
 
 
-def mixing_numbers(profiles_ref, classes_ref, heights_ref, k_ref):
+def mixing_kernel(profiles_ref, classes_ref, heights_ref, k_ref):
     total = k_ref.shape[0] - 1
     classes, heights = classes_ref[...], heights_ref[...]
     bits = [(classes & (1 << b)) != 0 for b in range(3)]
@@ -111,15 +111,14 @@
     lax.fori_loop(0, total, mixing, 0, unroll=8)
 
 
-def factor_kernel(profiles_ref, classes_ref, heights_ref, f_ref, h_ref, g_ref, a_ref, b_ref, w_ref,
-                  k_ref, n_ref, m_ref, p_ref, q_ref, up_ref, down_ref):
+def factor_kernel(k_ref, f_ref, h_ref, g_ref, a_ref, b_ref, w_ref,
+                  n_ref, m_ref, p_ref, q_ref, up_ref, down_ref):
     me = lax.axis_index("gz")
     depth = g_ref.shape[0]
     groups = w_ref.shape[0]
     shape = w_ref.shape[1:]
     total = depth * groups
     one = jnp.ones(shape, jnp.float32)
-    mixing_numbers(profiles_ref, classes_ref, heights_ref, k_ref)
 
     def some(t, carry):
         n, p, up, down = carry
@@ -344,6 +343,10 @@
     )(*(pltpu.with_memory_space_constraint(x, pltpu.HBM) for x in (conc[0], wind_x, wind_y, *small)))
     south = shifted(right, "gy", 1)
     north = shifted(left, "gy", -1)
+    (k,) = call(mixing_kernel, [SMEM, VMEM, VMEM], [(depth * groups + 1, *pane)], [], 1 << 24)(
+        profiles, classes, heights
+    )
+    own, south, north, k = lax.optimization_barrier((own, south, north, k))
     lo, hi, side_lo, side_hi = call(
         send_kernel, [VMEM] * 3,
         [(n_lo + 3, *tile), (n_hi + 3, *tile), (3, *tile), (3, *tile)], [], 1 << 20
@@ -355,11 +358,10 @@
         [(5, rows, *row), (HSTEPS, 4, *row), row], [(2, rows, *row)], 1 << 24,
     )(own, side_lo, side_hi)
     twice = (2 * depth, rows, width)
-    profiles, _ = lax.optimization_barrier((profiles, side_lo))
     f, h, g, a, b, w = call(
-        factor_kernel, [SMEM, VMEM, VMEM], [block] * 5 + [(groups, *pane)],
-        [(depth * groups + 1, *pane)] + [twice] * 4 + [(groups, *pane)] * 2, 1 << 24,
-    )(profiles, classes, heights)
+        factor_kernel, [VMEM], [block] * 5 + [(groups, *pane)],
+        [twice] * 4 + [(groups, *pane)] * 2, 1 << 24,
+    )(k)
     halves = []
     for low, got in ((True, west), (False, east)):
         if not low:

time: 56 us -> 55.8 us (level)
    pallas_call x1 -> x2, Pallas kernels: 3.05 us -> 3.03 us  [the longest x1 1.66 us: local(): call(mixing_kernel, [SMEM, VMEM, VMEM], [(depth * groups + 1, *pane)], []...]
where the time goes in v8:
time: 55.8 us; the launch traced here: 55.6 us
  blocking collectives  28.6 us (51%)
  starting transfers between devices  10.1 us (18%)
  Pallas kernels  9.72 us (17%)
  waiting for transfers between devices  7.1 us (13%)
    all_gather x1, blocking collectives, local(): got = lax.all_gather(send, 'gz', axis=0, tiled=True)  28.6 us
    ppermute x4, starting transfers between devices, shifted(): lax.ppermute(x, axis, [(i, i + by) for i in range(length) if 0 <= i + by...  10.1 us
    ppermute x4, waiting for transfers between devices, shifted(): lax.ppermute(x, axis, [(i, i + by) for i in range(length) if 0 <= i + by...  7.1 us
    pallas_call x2, Pallas kernels, local(): call(functools.partial(outer_kernel, low), [VMEM] * 8, [(depth, half, wid...  2.5 us
    pallas_call x1, Pallas kernels, local(): call(inner_kernel, [VMEM] * 3, [(5, rows, *row), (HSTEPS, 4, *row), row],...  1.76 us
    pallas_call x1, Pallas kernels, local(): call(mixing_kernel, [SMEM, VMEM, VMEM], [(depth * groups + 1, *pane)], []...  1.66 us
    pallas_call x1, Pallas kernels, local(): call(pack_kernel, [HBM] * 7, [(3, rows, depth, width), (3, *tile), (3, *t...  1.56 us
    pallas_call x1, Pallas kernels, local(): call(factor_kernel, [VMEM], [block] * 5 + [(groups, *pane)], [twice] * 4...  1.37 us
  transfers between devices with their start and end apart: 4, of which 3 were waited for; matrix products, arithmetic and copies ran while one was open for 0% of the time, Pallas kernels for 11%

profile of v8, /device:TPU:25, one launch (start us, length us, event | category | flops | bytes accessed | tf_op | source)
XLA Modules:
  0.0 55.6 jit_solution(17974962653312128660)
XLA Ops:
  0.0 1.6 %shard_map.73 = (f32[3,16,16,256]{3,2,1,0:T(8,128)S(1)}, f32[3,16,128]{2,1,0:T(8,128)S(1)}, f32[3,16,128]{2,1,0:T(8,128)S(1)}, f32[8,128]{1,0:T(8,128)S(1)}, s32...) custom-call(f32[16,16,256]{2,1,0:T(8,128)} %bitcast.3, f32[16,16,256]{2,1,0:T(8,128)} %wx_hbm.1, ...), custom_call_target="tpu_custom_call" | custom-call | flops 1048576 | bytes 1048576 | tf_op jit(solution)/shard_map/pallas_call | solution.py:339
  1.6 3.5 %collective-permute-start = (f32[3,16,128]{2,1,0:T(8,128)S(1)}, f32[3,16,128]{2,1,0:T(8,128)S(1)}, u32[]{:S(2)}, u32[]{:S(2)}) collective-permute-start(f32[3,16,128]{2,1,0:T(8,128)S(1)} %get-tuple-element.35), channel_id=1, source_target_pairs={{0,8},{8,16},{16,24},{1,9},{9,17},{17,25},{2,10},{10,18},{18,26},{... | collective-permute-start | bytes 73736 | tf_op jit(solution)/shard_map/ppermute | solution.py:328
  5.1 1.3 %collective-permute-start.1 = (f32[3,16,128]{2,1,0:T(8,128)S(1)}, f32[3,16,128]{2,1,0:T(8,128)S(1)}, u32[]{:S(2)}, u32[]{:S(2)}) collective-permute-start(f32[3,16,128]{2,1,0:T(8,128)S(1)} %get-tuple-element.36), channel_id=1, source_target_pairs={{8,0},{16,8},{24,16},{9,1},{17,9},{25,17},{10,2},{18,10},{26,18},{... | collective-permute-start | bytes 73736 | tf_op jit(solution)/shard_map/ppermute | solution.py:328
  6.4 1.7 %shard_map.74.k_ref = f32[129,16,256]{2,1,0:T(8,128)S(1)} custom-call(f32[8,128]{1,0:T(8,128)S(1)} %get-tuple-element.37.profiles_ref, s32[16,256]{1,0:T(8,128)S(1)} %get-tuple-element.38.classes_ref, s32[16,256]{1,0:T(8,128)S(1)} %get-tuple-element.39.heights_ref), custom_call_target="tpu_custom_call" | custom-call | flops 16777216 | bytes 1048576 | tf_op jit(solution)/shard_map/pallas_call | solution.py:346
  8.1 0.0 collective-permute-done.south_ref
  8.1 1.8 %collective-permute-done.1.north_ref = f32[3,16,128]{2,1,0:T(8,128)S(1)} collective-permute-done((f32[3,16,128]{2,1,0:T(8,128)S(1)}, f32[3,16,128]{2,1,0:T(8,128)S(1)}, u32[]{:S(2)}, u32[]{:S(2)}) %collective-permute-start.1) | collective-permute-done | bytes 24608 | tf_op jit(solution)/shard_map/ppermute | solution.py:328
  9.9 0.1 shard_map.75
  10.0 2.8 %collective-permute-start.2 = (f32[49,16,128]{2,1,0:T(8,128)S(1)}, f32[49,16,128]{2,1,0:T(8,128)S(1)}, u32[]{:S(2)}, u32[]{:S(2)}) collective-permute-start(f32[49,16,128]{2,1,0:T(8,128)S(1)} %get-tuple-element.43), channel_id=1, source_target_pairs={{0,32},{32,64},{64,96},{96,128},{128,160},{160,192},{192,224},{224... | collective-permute-start | bytes 1204232 | tf_op jit(solution)/shard_map/ppermute | solution.py:328
  12.8 2.5 %collective-permute-start.3 = (f32[47,16,128]{2,1,0:T(8,128)S(1)}, f32[47,16,128]{2,1,0:T(8,128)S(1)}, u32[]{:S(2)}, u32[]{:S(2)}) collective-permute-start(f32[47,16,128]{2,1,0:T(8,128)S(1)} %get-tuple-element.55), channel_id=1, source_target_pairs={{32,0},{64,32},{96,64},{128,96},{160,128},{192,160},{224,192},{256... | collective-permute-start | bytes 1155080 | tf_op jit(solution)/shard_map/ppermute | solution.py:328
  15.3 1.4 %shard_map.77 = (f32[16,16,256]{2,1,0:T(8,128)S(1)}, f32[16,16,256]{2,1,0:T(8,128)S(1)}, f32[16,16,256]{2,1,0:T(8,128)S(1)}, f32[16,16,256]{2,1,0:T(8,128)S(1)},...) custom-call(f32[129,16,256]{2,1,0:T(8,128)S(1)} %shard_map.74.k_ref), custom_call_target="tpu_custom_call" | custom-call | flops 16777216 | bytes 1048576 | tf_op jit(solution)/shard_map/pallas_call | solution.py:361
  16.6 1.8 %shard_map.76 = (f32[5,16,16,384]{3,2,1,0:T(8,128)S(1)}, f32[8,4,16,384]{3,2,1,0:T(8,128)S(1)}, f32[16,384]{1,0:T(8,128)S(1)}) custom-call(f32[3,16,16,256]{3,2,1,0:T(8,128)S(1)} %get-tuple-element.40.own_ref, f32[3,16,128]{2,1,0:T(8,128)S(1)} %get-tuple-element.44.side_lo_ref, f32[3,16,128]{2,1,0:T(8,128)S(1)} %get-tuple-element.45.side_hi_ref), custom_call_target="tpu_custom_call" | custom-call | flops 16777216 | bytes 1048576 | tf_op jit(solution)/shard_map/pallas_call | solution.py:356
  18.4 2.3 %collective-permute-done.2.got_ref = f32[49,16,128]{2,1,0:T(8,128)S(1)} collective-permute-done((f32[49,16,128]{2,1,0:T(8,128)S(1)}, f32[49,16,128]{2,1,0:T(8,128)S(1)}, u32[]{:S(2)}, u32[]{:S(2)}) %collective-permute-start.2) | collective-permute-done | bytes 401440 | tf_op jit(solution)/shard_map/ppermute | solution.py:328
  20.7 1.3 %shard_map.78 = (f32[16,8,256]{2,1,0:T(8,128)S(1)}, f32[2,8,256]{2,1,0:T(8,128)S(1)}) custom-call(f32[49,16,128]{2,1,0:T(8,128)S(1)} %collective-permute-done.2.got_ref, f32[5,16,16,384]{3,2,1,0:T(8,128)S(1)} %get-tuple-element.46.inner_ref, f32[8,4,16,384]{3,2,1,0:T(8,128)S(1)} %get-tuple-element.47.edge_ref, f32[16,384]{1,0:T(8,128)S(1)} %get-tuple-element.57.wind_ref, ...), custom_call_target="tpu_custom_call" | custom-call | flops 16777216 | bytes 1048576 | tf_op jit(solution)/shard_map/pallas_call | solution.py:369
  22.0 3.0 %collective-permute-done.3.got_ref = f32[47,16,128]{2,1,0:T(8,128)S(1)} collective-permute-done((f32[47,16,128]{2,1,0:T(8,128)S(1)}, f32[47,16,128]{2,1,0:T(8,128)S(1)}, u32[]{:S(2)}, u32[]{:S(2)}) %collective-permute-start.3) | collective-permute-done | bytes 385056 | tf_op jit(solution)/shard_map/ppermute | solution.py:328
  25.0 1.2 %shard_map.79 = (f32[16,8,256]{2,1,0:T(8,128)S(1)}, f32[2,8,256]{2,1,0:T(8,128)S(1)}) custom-call(f32[47,16,128]{2,1,0:T(8,128)S(1)} %collective-permute-done.3.got_ref, f32[5,16,16,384]{3,2,1,0:T(8,128)S(1)} %get-tuple-element.46.inner_ref, f32[8,4,16,384]{3,2,1,0:T(8,128)S(1)} %get-tuple-element.47.edge_ref, f32[16,384]{1,0:T(8,128)S(1)} %get-tuple-element.57.wind_ref, ...), custom_call_target="tpu_custom_call" | custom-call | flops 16777216 | bytes 1048576 | tf_op jit(solution)/shard_map/pallas_call | solution.py:369
  26.3 28.6 %all_gather.3.got_ref = f32[16,16,256]{2,1,0:T(8,128)S(1)} all-gather(f32[2,16,256]{2,1,0:T(8,128)S(1)} %pad_maximum_fusion), channel_id=1, replica_groups=mesh['gx'=16,'gy'=4,'gz'=8] {'gz'}, dimensions={0}, use_global_device_ids=true | all-gather | bytes 294912 | tf_op jit(solution)/shard_map/all_gather | solution.py:375
  54.8 0.8 %shard_map.80 = f32[16,16,256]{2,1,0:T(8,128)} custom-call(f32[16,8,256]{2,1,0:T(8,128)S(1)} %get-tuple-element.54.west_ref, f32[16,8,256]{2,1,0:T(8,128)S(1)} %get-tuple-element.58.east_ref, f32[16,16,256]{2,1,0:T(8,128)S(1)} %get-tuple-element.59.a_ref, f32[16,16,256]{2,1,0:T(8,128)S(1)} %get-tuple-element.60.b_ref, ...), custom_call_target="tpu_custom_call" | custom-call | flops 1048576 | bytes 1048576 | tf_op jit(solution)/shard_map/pallas_call | solution.py:376
  (1 shorter events, 0.0 us)
Async XLA Ops:
  1.6 6.5 %collective-permute-start = (f32[3,16,128]{2,1,0:T(8,128)S(1)}, f32[3,16,128]{2,1,0:T(8,128)S(1)}, u32[]{:S(2)}, u32[]{:S(2)}) collective-permute-start(f32[3,16,128]{2,1,0:T(8,128)S(1)} %get-tuple-element.35), channel_id=1, source_target_pairs={{0,8},{8,16},{16,24},{1,9},{9,17},{17,25},{2,10},{10,18},{18,26},{... | collective-permute-start | bytes 73736 | tf_op jit(solution)/shard_map/ppermute | solution.py:328
  5.1 4.8 %collective-permute-start.1 = (f32[3,16,128]{2,1,0:T(8,128)S(1)}, f32[3,16,128]{2,1,0:T(8,128)S(1)}, u32[]{:S(2)}, u32[]{:S(2)}) collective-permute-start(f32[3,16,128]{2,1,0:T(8,128)S(1)} %get-tuple-element.36), channel_id=1, source_target_pairs={{8,0},{16,8},{24,16},{9,1},{17,9},{25,17},{10,2},{18,10},{26,18},{... | collective-permute-start | bytes 73736 | tf_op jit(solution)/shard_map/ppermute | solution.py:328
  10.0 10.8 %collective-permute-start.2 = (f32[49,16,128]{2,1,0:T(8,128)S(1)}, f32[49,16,128]{2,1,0:T(8,128)S(1)}, u32[]{:S(2)}, u32[]{:S(2)}) collective-permute-start(f32[49,16,128]{2,1,0:T(8,128)S(1)} %get-tuple-element.43), channel_id=1, source_target_pairs={{0,32},{32,64},{64,96},{96,128},{128,160},{160,192},{192,224},{224... | collective-permute-start | bytes 1204232 | tf_op jit(solution)/shard_map/ppermute | solution.py:328
  12.8 12.2 %collective-permute-start.3 = (f32[47,16,128]{2,1,0:T(8,128)S(1)}, f32[47,16,128]{2,1,0:T(8,128)S(1)}, u32[]{:S(2)}, u32[]{:S(2)}) collective-permute-start(f32[47,16,128]{2,1,0:T(8,128)S(1)} %get-tuple-element.55), channel_id=1, source_target_pairs={{32,0},{64,32},{96,64},{128,96},{160,128},{192,160},{224,192},{256... | collective-permute-start | bytes 1155080 | tf_op jit(solution)/shard_map/ppermute | solution.py:328

commit v9 on v8

--- a/solution.py
+++ b/solution.py
@@ -108,7 +108,7 @@
         k_ref[z + 1] = jnp.where(z < heights, CANOPY * k, k)
         return 0
 
-    lax.fori_loop(0, total, mixing, 0, unroll=8)
+    lax.fori_loop(0, total, mixing, 0, unroll=32)
 
 
 def factor_kernel(k_ref, f_ref, h_ref, g_ref, a_ref, b_ref, w_ref,

time: 55.8 us -> 55.8 us (level)
  no operation moved by 1% of the time
where the time goes in v9:
time: 55.8 us; the launch traced here: 55.6 us
  blocking collectives  28.6 us (51%)
  starting transfers between devices  10.1 us (18%)
  Pallas kernels  9.64 us (17%)
  waiting for transfers between devices  7.18 us (13%)
    all_gather x1, blocking collectives, local(): got = lax.all_gather(send, 'gz', axis=0, tiled=True)  28.6 us
    ppermute x4, starting transfers between devices, shifted(): lax.ppermute(x, axis, [(i, i + by) for i in range(length) if 0 <= i + by...  10.1 us
    ppermute x4, waiting for transfers between devices, shifted(): lax.ppermute(x, axis, [(i, i + by) for i in range(length) if 0 <= i + by...  7.18 us
    pallas_call x2, Pallas kernels, local(): call(functools.partial(outer_kernel, low), [VMEM] * 8, [(depth, half, wid...  2.5 us
    pallas_call x1, Pallas kernels, local(): call(inner_kernel, [VMEM] * 3, [(5, rows, *row), (HSTEPS, 4, *row), row],...  1.76 us
    pallas_call x1, Pallas kernels, local(): call(mixing_kernel, [SMEM, VMEM, VMEM], [(depth * groups + 1, *pane)], []...  1.58 us
    pallas_call x1, Pallas kernels, local(): call(pack_kernel, [HBM] * 7, [(3, rows, depth, width), (3, *tile), (3, *t...  1.56 us
    pallas_call x1, Pallas kernels, local(): call(factor_kernel, [VMEM], [block] * 5 + [(groups, *pane)], [twice] * 4...  1.37 us
  transfers between devices with their start and end apart: 4, of which 3 were waited for; matrix products, arithmetic and copies ran while one was open for 0% of the time, Pallas kernels for 11%

profile of v9, /device:TPU:25, one launch (start us, length us, event | category | flops | bytes accessed | tf_op | source)
XLA Modules:
  0.0 55.6 jit_solution(6104576399995153079)
XLA Ops:
  0.0 1.6 %shard_map.73 = (f32[3,16,16,256]{3,2,1,0:T(8,128)S(1)}, f32[3,16,128]{2,1,0:T(8,128)S(1)}, f32[3,16,128]{2,1,0:T(8,128)S(1)}, f32[8,128]{1,0:T(8,128)S(1)}, s32...) custom-call(f32[16,16,256]{2,1,0:T(8,128)} %bitcast.3, f32[16,16,256]{2,1,0:T(8,128)} %wx_hbm.1, ...), custom_call_target="tpu_custom_call" | custom-call | flops 1048576 | bytes 1048576 | tf_op jit(solution)/shard_map/pallas_call | solution.py:339
  1.6 3.5 %collective-permute-start = (f32[3,16,128]{2,1,0:T(8,128)S(1)}, f32[3,16,128]{2,1,0:T(8,128)S(1)}, u32[]{:S(2)}, u32[]{:S(2)}) collective-permute-start(f32[3,16,128]{2,1,0:T(8,128)S(1)} %get-tuple-element.35), channel_id=1, source_target_pairs={{0,8},{8,16},{16,24},{1,9},{9,17},{17,25},{2,10},{10,18},{18,26},{... | collective-permute-start | bytes 73736 | tf_op jit(solution)/shard_map/ppermute | solution.py:328
  5.1 1.3 %collective-permute-start.1 = (f32[3,16,128]{2,1,0:T(8,128)S(1)}, f32[3,16,128]{2,1,0:T(8,128)S(1)}, u32[]{:S(2)}, u32[]{:S(2)}) collective-permute-start(f32[3,16,128]{2,1,0:T(8,128)S(1)} %get-tuple-element.36), channel_id=1, source_target_pairs={{8,0},{16,8},{24,16},{9,1},{17,9},{25,17},{10,2},{18,10},{26,18},{... | collective-permute-start | bytes 73736 | tf_op jit(solution)/shard_map/ppermute | solution.py:328
  6.4 1.6 %shard_map.74.k_ref = f32[129,16,256]{2,1,0:T(8,128)S(1)} custom-call(f32[8,128]{1,0:T(8,128)S(1)} %get-tuple-element.37.profiles_ref, s32[16,256]{1,0:T(8,128)S(1)} %get-tuple-element.38.classes_ref, s32[16,256]{1,0:T(8,128)S(1)} %get-tuple-element.39.heights_ref), custom_call_target="tpu_custom_call" | custom-call | flops 16777216 | bytes 1048576 | tf_op jit(solution)/shard_map/pallas_call | solution.py:346
  8.0 0.0 collective-permute-done.south_ref
  8.0 1.9 %collective-permute-done.1.north_ref = f32[3,16,128]{2,1,0:T(8,128)S(1)} collective-permute-done((f32[3,16,128]{2,1,0:T(8,128)S(1)}, f32[3,16,128]{2,1,0:T(8,128)S(1)}, u32[]{:S(2)}, u32[]{:S(2)}) %collective-permute-start.1) | collective-permute-done | bytes 24608 | tf_op jit(solution)/shard_map/ppermute | solution.py:328
  9.9 0.1 shard_map.75
  10.0 2.8 %collective-permute-start.2 = (f32[49,16,128]{2,1,0:T(8,128)S(1)}, f32[49,16,128]{2,1,0:T(8,128)S(1)}, u32[]{:S(2)}, u32[]{:S(2)}) collective-permute-start(f32[49,16,128]{2,1,0:T(8,128)S(1)} %get-tuple-element.43), channel_id=1, source_target_pairs={{0,32},{32,64},{64,96},{96,128},{128,160},{160,192},{192,224},{224... | collective-permute-start | bytes 1204232 | tf_op jit(solution)/shard_map/ppermute | solution.py:328
  12.8 2.5 %collective-permute-start.3 = (f32[47,16,128]{2,1,0:T(8,128)S(1)}, f32[47,16,128]{2,1,0:T(8,128)S(1)}, u32[]{:S(2)}, u32[]{:S(2)}) collective-permute-start(f32[47,16,128]{2,1,0:T(8,128)S(1)} %get-tuple-element.55), channel_id=1, source_target_pairs={{32,0},{64,32},{96,64},{128,96},{160,128},{192,160},{224,192},{256... | collective-permute-start | bytes 1155080 | tf_op jit(solution)/shard_map/ppermute | solution.py:328
  15.3 1.4 %shard_map.77 = (f32[16,16,256]{2,1,0:T(8,128)S(1)}, f32[16,16,256]{2,1,0:T(8,128)S(1)}, f32[16,16,256]{2,1,0:T(8,128)S(1)}, f32[16,16,256]{2,1,0:T(8,128)S(1)},...) custom-call(f32[129,16,256]{2,1,0:T(8,128)S(1)} %shard_map.74.k_ref), custom_call_target="tpu_custom_call" | custom-call | flops 16777216 | bytes 1048576 | tf_op jit(solution)/shard_map/pallas_call | solution.py:361
  16.6 1.8 %shard_map.76 = (f32[5,16,16,384]{3,2,1,0:T(8,128)S(1)}, f32[8,4,16,384]{3,2,1,0:T(8,128)S(1)}, f32[16,384]{1,0:T(8,128)S(1)}) custom-call(f32[3,16,16,256]{3,2,1,0:T(8,128)S(1)} %get-tuple-element.40.own_ref, f32[3,16,128]{2,1,0:T(8,128)S(1)} %get-tuple-element.44.side_lo_ref, f32[3,16,128]{2,1,0:T(8,128)S(1)} %get-tuple-element.45.side_hi_ref), custom_call_target="tpu_custom_call" | custom-call | flops 16777216 | bytes 1048576 | tf_op jit(solution)/shard_map/pallas_call | solution.py:356
  18.4 2.3 %collective-permute-done.2.got_ref = f32[49,16,128]{2,1,0:T(8,128)S(1)} collective-permute-done((f32[49,16,128]{2,1,0:T(8,128)S(1)}, f32[49,16,128]{2,1,0:T(8,128)S(1)}, u32[]{:S(2)}, u32[]{:S(2)}) %collective-permute-start.2) | collective-permute-done | bytes 401440 | tf_op jit(solution)/shard_map/ppermute | solution.py:328
  20.7 1.3 %shard_map.78 = (f32[16,8,256]{2,1,0:T(8,128)S(1)}, f32[2,8,256]{2,1,0:T(8,128)S(1)}) custom-call(f32[49,16,128]{2,1,0:T(8,128)S(1)} %collective-permute-done.2.got_ref, f32[5,16,16,384]{3,2,1,0:T(8,128)S(1)} %get-tuple-element.46.inner_ref, f32[8,4,16,384]{3,2,1,0:T(8,128)S(1)} %get-tuple-element.47.edge_ref, f32[16,384]{1,0:T(8,128)S(1)} %get-tuple-element.57.wind_ref, ...), custom_call_target="tpu_custom_call" | custom-call | flops 16777216 | bytes 1048576 | tf_op jit(solution)/shard_map/pallas_call | solution.py:369
  22.0 3.0 %collective-permute-done.3.got_ref = f32[47,16,128]{2,1,0:T(8,128)S(1)} collective-permute-done((f32[47,16,128]{2,1,0:T(8,128)S(1)}, f32[47,16,128]{2,1,0:T(8,128)S(1)}, u32[]{:S(2)}, u32[]{:S(2)}) %collective-permute-start.3) | collective-permute-done | bytes 385056 | tf_op jit(solution)/shard_map/ppermute | solution.py:328
  25.0 1.2 %shard_map.79 = (f32[16,8,256]{2,1,0:T(8,128)S(1)}, f32[2,8,256]{2,1,0:T(8,128)S(1)}) custom-call(f32[47,16,128]{2,1,0:T(8,128)S(1)} %collective-permute-done.3.got_ref, f32[5,16,16,384]{3,2,1,0:T(8,128)S(1)} %get-tuple-element.46.inner_ref, f32[8,4,16,384]{3,2,1,0:T(8,128)S(1)} %get-tuple-element.47.edge_ref, f32[16,384]{1,0:T(8,128)S(1)} %get-tuple-element.57.wind_ref, ...), custom_call_target="tpu_custom_call" | custom-call | flops 16777216 | bytes 1048576 | tf_op jit(solution)/shard_map/pallas_call | solution.py:369
  26.3 28.6 %all_gather.3.got_ref = f32[16,16,256]{2,1,0:T(8,128)S(1)} all-gather(f32[2,16,256]{2,1,0:T(8,128)S(1)} %pad_maximum_fusion), channel_id=1, replica_groups=mesh['gx'=16,'gy'=4,'gz'=8] {'gz'}, dimensions={0}, use_global_device_ids=true | all-gather | bytes 294912 | tf_op jit(solution)/shard_map/all_gather | solution.py:375
  54.8 0.8 %shard_map.80 = f32[16,16,256]{2,1,0:T(8,128)} custom-call(f32[16,8,256]{2,1,0:T(8,128)S(1)} %get-tuple-element.54.west_ref, f32[16,8,256]{2,1,0:T(8,128)S(1)} %get-tuple-element.58.east_ref, f32[16,16,256]{2,1,0:T(8,128)S(1)} %get-tuple-element.59.a_ref, f32[16,16,256]{2,1,0:T(8,128)S(1)} %get-tuple-element.60.b_ref, ...), custom_call_target="tpu_custom_call" | custom-call | flops 1048576 | bytes 1048576 | tf_op jit(solution)/shard_map/pallas_call | solution.py:376
  (1 shorter events, 0.0 us)
Async XLA Ops:
  1.6 6.4 %collective-permute-start = (f32[3,16,128]{2,1,0:T(8,128)S(1)}, f32[3,16,128]{2,1,0:T(8,128)S(1)}, u32[]{:S(2)}, u32[]{:S(2)}) collective-permute-start(f32[3,16,128]{2,1,0:T(8,128)S(1)} %get-tuple-element.35), channel_id=1, source_target_pairs={{0,8},{8,16},{16,24},{1,9},{9,17},{17,25},{2,10},{10,18},{18,26},{... | collective-permute-start | bytes 73736 | tf_op jit(solution)/shard_map/ppermute | solution.py:328
  5.1 4.8 %collective-permute-start.1 = (f32[3,16,128]{2,1,0:T(8,128)S(1)}, f32[3,16,128]{2,1,0:T(8,128)S(1)}, u32[]{:S(2)}, u32[]{:S(2)}) collective-permute-start(f32[3,16,128]{2,1,0:T(8,128)S(1)} %get-tuple-element.36), channel_id=1, source_target_pairs={{8,0},{16,8},{24,16},{9,1},{17,9},{25,17},{10,2},{18,10},{26,18},{... | collective-permute-start | bytes 73736 | tf_op jit(solution)/shard_map/ppermute | solution.py:328
  10.0 10.8 %collective-permute-start.2 = (f32[49,16,128]{2,1,0:T(8,128)S(1)}, f32[49,16,128]{2,1,0:T(8,128)S(1)}, u32[]{:S(2)}, u32[]{:S(2)}) collective-permute-start(f32[49,16,128]{2,1,0:T(8,128)S(1)} %get-tuple-element.43), channel_id=1, source_target_pairs={{0,32},{32,64},{64,96},{96,128},{128,160},{160,192},{192,224},{224... | collective-permute-start | bytes 1204232 | tf_op jit(solution)/shard_map/ppermute | solution.py:328
  12.8 12.2 %collective-permute-start.3 = (f32[47,16,128]{2,1,0:T(8,128)S(1)}, f32[47,16,128]{2,1,0:T(8,128)S(1)}, u32[]{:S(2)}, u32[]{:S(2)}) collective-permute-start(f32[47,16,128]{2,1,0:T(8,128)S(1)} %get-tuple-element.55), channel_id=1, source_target_pairs={{32,0},{64,32},{96,64},{128,96},{160,128},{192,160},{224,192},{256... | collective-permute-start | bytes 1155080 | tf_op jit(solution)/shard_map/ppermute | solution.py:328
